TPU v7x, 32 devices: a whole 2x2x4 slice. The times are simulated.
32 devices in a mesh: parts: 2 (over y), ctx: 4 (over z), grid: 4 (over x, core).
Axes of the slice: x: 2, y: 2, z: 4, core: 2. Of those that a mesh axis runs over, the one named last changes fastest.
Arguments:
- frames_in: bfloat16 [4096, 1536], P(('parts', 'ctx'), 'grid'), parts along dimension 0, may hold values from -230 to 230
- norm1_gain: bfloat16 [1536], P('grid'), may hold values from 0.25 to 1.75
- norm1_bias: bfloat16 [1536], P('grid'), may hold values from -3 to 3
- w_query: bfloat16 [1536, 1536], P(None, 'grid'), may hold values from -0.5 to 0.5
- w_key: bfloat16 [1536, 1536], P(None, 'grid'), may hold values from -2 to 2
- w_value: bfloat16 [1536, 1536], P(None, 'grid'), may hold values from -0.15625 to 0.15625
- w_out: bfloat16 [1536, 1536], P('grid'), may hold values from -0.15625 to 0.15625
- norm2_gain: bfloat16 [1536], P('grid'), may hold values from 0.099609375 to 1.8984375
- norm2_bias: bfloat16 [1536], P('grid'), may hold values from -3 to 3
- w_glu_value: bfloat16 [1536, 1536], P(None, 'grid'), may hold values from -0.15625 to 0.15625
- w_glu_gate: bfloat16 [1536, 1536], P(None, 'grid'), may hold values from -0.15625 to 0.15625
- depth_kernel: float32 [31, 1536], P(None, 'grid'), may hold values from -1 to 1
- bn_scale: float32 [1536], P('grid'), may hold values from 0.25 to 1.75
- bn_shift: float32 [1536], P('grid'), may hold values from -3 to 3
- w_proj: bfloat16 [1536, 1536], P('grid'), may hold values from -0.3125 to 0.3125
Outputs:
- layer_out: bfloat16 [4096, 1536], P(('parts', 'ctx'), 'grid'), parts along dimension 0
There are 2 independent parts, one for each index of `parts`. A program takes and returns all parts, laid end to end along the dimension named above; an argument that names none is the same for every part. Nothing has to cross between parts.
All inputs are finite; a program needn't handle non-finite values.
Results may differ from a plain program's by a relative error of at most 0.009.
Values may be sent and summed in bfloat16 or wider, within the bound.
No kernel may reach another device: no remote copies, remote signals or barrier semaphores. Data moves between devices by JAX's collectives and lax.ppermute only.
A program may use at most 256 MiB of HBM per device.

v0:
```python
import functools
import math

import jax
import jax.numpy as jnp
from jax import lax
from jax.experimental import pallas as pl
from jax.experimental.pallas import tpu as pltpu
from jax.sharding import PartitionSpec as P

HEAD_DIM = 64
PAIR = 2 * HEAD_DIM
KERNEL = 31
HALF = 15
HALO = 16
EPSILON = 1e-05
CORES = 2
VMEM_BYTES = 16 * 1024 * 1024
BF16 = jnp.bfloat16
F32 = jnp.float32
SCORE_SCALE = math.log2(math.e) / math.sqrt(HEAD_DIM)


def exchange(cells, axis, distance):
    count = lax.axis_size(axis)
    return lax.ppermute(cells, axis, [(i, i ^ distance) for i in range(count)])


def kernel_call(body, outs, operands, spaces=None, scratch=(), aliases=None):
    spaces = spaces or {}
    operands = [
        pltpu.with_memory_space_constraint(cells, pltpu.HBM) if spaces.get(i) == pltpu.HBM else cells
        for i, cells in enumerate(operands)
    ]
    in_specs = [
        pl.BlockSpec(memory_space=spaces.get(i, pltpu.VMEM)) for i in range(len(operands))
    ]
    return pl.pallas_call(
        body,
        in_specs=in_specs,
        out_specs=tuple(pl.BlockSpec(memory_space=pltpu.VMEM) for _ in outs),
        out_shape=tuple(jax.ShapeDtypeStruct(shape, dtype) for shape, dtype in outs),
        scratch_shapes=list(scratch),
        input_output_aliases=aliases or {},
        compiler_params=pltpu.CompilerParams(vmem_limit_bytes=VMEM_BYTES),
        cost_estimate=pl.CostEstimate(flops=1000, bytes_accessed=1000, transcendentals=0),
    )(*operands)


def after(cells, *done):
    def body(*refs):
        pass

    anywhere = pl.BlockSpec(memory_space=pl.ANY)
    return pl.pallas_call(
        body,
        in_specs=[anywhere] * (1 + len(done)),
        out_specs=anywhere,
        out_shape=jax.ShapeDtypeStruct(cells.shape, cells.dtype),
        input_output_aliases={0: 0},
        compiler_params=pltpu.CompilerParams(vmem_limit_bytes=64 * 1024),
        cost_estimate=pl.CostEstimate(flops=0, bytes_accessed=0, transcendentals=0),
    )(cells, *done)


def fold_kernel(order, which, count, me_ref, *refs):
    gains, refs = refs[: len(order)], refs[len(order) :]
    sources, (folded_ref, sums_ref), weights, done = refs[:count], refs[count : count + 2], refs[count + 2 : -1], refs[-1]
    copies = [pltpu.make_async_copy(sources[n], weights[n], done.at[n]) for n in range(count)]
    for copy in copies:
        copy.start()
    width = gains[0].shape[1]
    columns = weights[0].shape[1]
    factors = []
    for k in range(len(order)):
        gain = jnp.transpose(jnp.broadcast_to(gains[k][which : which + 1, :], (PAIR, width)))
        bias = jnp.broadcast_to(gains[k][which + 1 : which + 2, :], (8, width)).astype(BF16)
        factors.append((gain, bias))
    for n, ref in enumerate(weights):
        copies[n].wait()
        total = jnp.zeros((8, columns), F32)
        for k, r in enumerate(order):
            gain, bias = factors[k]
            start = pl.multiple_of((me_ref[0] ^ r) * width, width)
            block = ref[pl.ds(start, width), :]
            total = total + jnp.dot(bias, block, preferred_element_type=F32)
            for j in range(columns // PAIR):
                target = (j * count + n) * PAIR
                folded_ref[k * width : (k + 1) * width, target : target + PAIR] = (
                    block[:, j * PAIR : (j + 1) * PAIR].astype(F32) * gain
                ).astype(BF16)
        for j in range(columns // PAIR):
            target = (j * count + n) * PAIR
            sums_ref[1:2, target : target + PAIR] = total[0:1, j * PAIR : (j + 1) * PAIR]
    sums = jnp.dot(jnp.ones((8, folded_ref.shape[0]), BF16), folded_ref[...], preferred_element_type=F32)
    sums_ref[0:1, :] = sums[0:1]


def folded(me, order, which, gains, weights):
    rows, columns = weights[0].shape
    total = columns * len(weights)
    first = 1 + len(gains)
    spaces = {first + n: pltpu.HBM for n in range(len(weights))}
    return kernel_call(
        functools.partial(fold_kernel, order, which, len(weights)),
        [((rows, total), BF16), ((2, total), F32)],
        [me, *gains, *weights],
        spaces={0: pltpu.SMEM, **spaces},
        scratch=[pltpu.VMEM((rows, columns), BF16)] * len(weights) + [pltpu.SemaphoreType.DMA((len(weights),))],
    )


def stack_kernel(*refs):
    count = (len(refs) - 2) // 2
    sources, out_ref, rows, done = refs[:count], refs[count], refs[count + 1 : -1], refs[-1]
    copies = [pltpu.make_async_copy(sources[i], rows[i], done.at[i]) for i in range(count)]
    for copy in copies:
        copy.start()
    out_ref[...] = jnp.zeros_like(out_ref)
    for i, copy in enumerate(copies):
        copy.wait()
        out_ref[i : i + 1, :] = rows[i][...].astype(F32).reshape(1, out_ref.shape[1])


def reorder_kernel(order, me_ref, source_ref, out_ref, done):
    width = source_ref.shape[1] // len(order)
    copies = []
    for k, r in enumerate(order):
        cols = pl.ds(pl.multiple_of((me_ref[0] ^ r) * width, PAIR), width)
        copies.append(
            pltpu.make_async_copy(source_ref.at[:, cols], out_ref.at[:, k * width : (k + 1) * width], done.at[k])
        )
        copies[-1].start()
    for copy in copies:
        copy.wait()


def half_kernel(part_ref, source_ref, half_ref, done):
    rows = half_ref.shape[0]
    copy = pltpu.make_async_copy(
        source_ref.at[pl.ds(pl.multiple_of(part_ref[0] * rows, rows), rows), :], half_ref, done.at[0]
    )
    copy.start()
    copy.wait()


def row_statistics(refs):
    rows, width = refs[0].shape
    full = width * len(refs)
    means, scales = [], []
    step = math.gcd(rows, 64)
    for start in range(0, rows, step):
        parts = [ref[start : start + step, :].astype(F32) for ref in refs]
        mean = sum(jnp.sum(part, axis=1, keepdims=True) for part in parts) / full
        variance = sum(jnp.sum(jnp.square(part - mean), axis=1, keepdims=True) for part in parts) / full
        means.append(mean)
        scales.append(lax.rsqrt(variance + EPSILON))
    return jnp.concatenate(means, axis=0), jnp.concatenate(scales, axis=0)


def norm_product(cells, mean, scale, folded_ref, sums_ref, start, columns):
    cols = slice(start, start + columns)
    product = jnp.dot(cells, folded_ref[:, cols], preferred_element_type=F32)
    return (product - mean * sums_ref[0:1, cols]) * scale + sums_ref[1:2, cols]


def lane_masks():
    lanes = lax.broadcasted_iota(jnp.int32, (1, PAIR), 1)
    return lanes < HEAD_DIM


def keys_values(projected):
    low = lane_masks()
    values = projected[:, PAIR : 2 * PAIR]
    return (
        projected[:, :PAIR].astype(BF16),
        jnp.where(low, values, 1.0).astype(BF16),
        jnp.where(low, 1.0, values).astype(BF16),
    )


def project_kernel(count, *refs):
    blocks, (folded_ref, sums_ref), (query_ref, key_ref, value_ref) = refs[:count], refs[count : count + 2], refs[-4:-1]
    sent_ref = refs[-1]
    mean, scale = row_statistics(blocks)
    cells = jnp.concatenate([ref[...] for ref in blocks], axis=1)
    low = lane_masks()
    for j in range(key_ref.shape[1] // PAIR):
        projected = norm_product(cells, mean, scale, folded_ref, sums_ref, j * 3 * PAIR, 3 * PAIR)
        keys, low_values, high_values = keys_values(projected)
        queries = projected[:, 2 * PAIR :] * SCORE_SCALE
        base = 2 * j * PAIR
        sent_ref[:, base : base + 2 * PAIR] = projected[:, : 2 * PAIR].astype(BF16)
        key_ref[:, j * PAIR : (j + 1) * PAIR] = keys
        value_ref[:, base : base + PAIR] = low_values
        value_ref[:, base + PAIR : base + 2 * PAIR] = high_values
        query_ref[:, base : base + PAIR] = jnp.where(low, queries, 0.0).astype(BF16)
        query_ref[:, base + PAIR : base + 2 * PAIR] = jnp.where(low, 0.0, queries).astype(BF16)


def attend_pair(pair, query_rows, query_ref, keys, values, state_ref):
    total = query_ref.shape[0]
    for start in range(0, total, query_rows):
        rows = slice(start, start + query_rows)
        for head in range(2):
            index = 2 * pair + head
            queries = query_ref[rows, index * PAIR : (index + 1) * PAIR]
            scores = lax.dot_general(
                queries, keys, (((1,), (1,)), ((), ())), preferred_element_type=F32
            )
            peak = jnp.max(scores, axis=1, keepdims=True)
            soft = jnp.exp2(scores - peak).astype(BF16)
            sums = jnp.dot(soft, values[head], preferred_element_type=F32)
            state_ref[rows, 2 * index * PAIR : (2 * index + 1) * PAIR] = sums
            state_ref[rows, (2 * index + 1) * PAIR : (2 * index + 2) * PAIR] = jnp.broadcast_to(
                peak, (query_rows, PAIR)
            )


def merge_head(old_ref, part_ref, rows, index):
    sums = slice(2 * index * PAIR, (2 * index + 1) * PAIR)
    peaks = slice((2 * index + 1) * PAIR, (2 * index + 2) * PAIR)
    old_peak, part_peak = old_ref[rows, peaks], part_ref[rows, peaks]
    peak = jnp.maximum(old_peak, part_peak)
    total = old_ref[rows, sums] * jnp.exp2(old_peak - peak) + part_ref[rows, sums] * jnp.exp2(part_peak - peak)
    return total, peak


def first_kernel(query_rows, query_ref, key_ref, value_ref, _, state_ref, token_ref):
    token_ref[...] = jnp.zeros_like(token_ref)
    for j in range(key_ref.shape[1] // PAIR):
        values = [value_ref[:, n * PAIR : (n + 1) * PAIR] for n in (2 * j, 2 * j + 1)]
        attend_pair(j, query_rows, query_ref, key_ref[:, j * PAIR : (j + 1) * PAIR], values, state_ref)


def slot_kernel(count, last, query_rows, *refs):
    query_ref, old_ref, *refs = refs
    if count:
        blocks, (folded_ref, sums_ref) = refs[:count], refs[count : count + 2]
        mean, scale = row_statistics(blocks)
        cells = jnp.concatenate([ref[...] for ref in blocks], axis=1)
    else:
        sent_ref = refs[0]
    if last:
        attended, part = refs[-2:]
    else:
        state_ref, token_ref, part = refs[-3:]
        token_ref[...] = jnp.zeros_like(token_ref)
    pairs = query_ref.shape[1] // (2 * PAIR)
    for j in range(pairs):
        if count:
            projected = norm_product(cells, mean, scale, folded_ref, sums_ref, j * 3 * PAIR, 2 * PAIR)
        else:
            projected = sent_ref[:, 2 * j * PAIR : 2 * (j + 1) * PAIR].astype(F32)
        keys, *values = keys_values(projected)
        attend_pair(j, query_rows, query_ref, keys, values, part)
    total = query_ref.shape[0]
    low = lane_masks()
    for start in range(0, total, query_rows):
        rows = slice(start, start + query_rows)
        for j in range(pairs):
            heads = [merge_head(old_ref, part, rows, 2 * j + head) for head in range(2)]
            if last:
                (one, _), (two, _) = heads
                both = jnp.where(low, one, two)
                weight = pltpu.roll(jnp.where(low, two, one), HEAD_DIM, 1)
                attended[rows, j * PAIR : (j + 1) * PAIR] = (both / weight).astype(BF16)
            else:
                for head, (sums, peak) in enumerate(heads):
                    at = 2 * (2 * j + head) * PAIR
                    state_ref[rows, at : at + PAIR] = sums
                    state_ref[rows, at + PAIR : at + 2 * PAIR] = peak


def middle_kernel(count, order, me_ref, part_ref, *refs):
    attended, frames_refs, refs = refs[:count], refs[count : 2 * count], refs[2 * count :]
    *pieces, folded_ref, sums_ref, own_ref, out_ref, head_ref, tail_ref, middle = refs
    width = frames_refs[0].shape[1]
    cells = jnp.concatenate([ref[:, :width] for ref in attended], axis=1)
    swap = part_ref[0] != 0

    def weights(k):
        if width % PAIR:
            cols = slice(k * width, (k + 1) * width)
        else:
            cols = pl.ds(pl.multiple_of((me_ref[0] ^ order[k]) * width, PAIR), width)
        rows, index = [], 0
        while index < len(pieces):
            mine = pieces[index][:, cols]
            index += 1
            if mine.shape[0] < width:
                other = pieces[index][:, cols]
                index += 1
                mine = jnp.concatenate([jnp.where(swap, other, mine), jnp.where(swap, mine, other)], axis=0)
            rows.append(mine)
        return jnp.concatenate(rows, axis=0)

    for k in range(0, count, 2):
        both = jnp.concatenate([weights(k), weights(k + 1)], axis=1)
        share = jnp.dot(cells, both, preferred_element_type=F32)
        for n in range(2):
            cols = slice((k + n) * width, (k + n + 1) * width)
            middle[:, cols] = (
                frames_refs[k + n][...].astype(F32) + share[:, n * width : (n + 1) * width]
            ).astype(BF16)
    own_ref[...] = middle[:, :width]
    mean, scale = row_statistics((middle,))
    cells = middle[...]
    for j in range(out_ref.shape[1] // PAIR):
        both = norm_product(cells, mean, scale, folded_ref, sums_ref, j * 2 * PAIR, 2 * PAIR)
        out_ref[:, j * PAIR : (j + 1) * PAIR] = (
            both[:, :PAIR] / (1.0 + jnp.exp(-both[:, PAIR:]))
        ).astype(BF16)
    total = out_ref.shape[0]
    head_ref[...] = out_ref[:HALO, :]
    tail_ref[...] = out_ref[total - HALO :, :]


def conv_rows(padded, start, piece, cols, taps, scale, shift):
    window = padded[pl.ds(start, piece + 2 * HALO), cols]
    convolved = None
    for residue in range(8):
        part = None
        for offset in range(residue, KERNEL + 1, 8):
            if offset == 0:
                continue
            base = offset - residue
            term = taps[offset - 1] * window[base : base + piece + 8]
            part = term if part is None else part + term
        part = part[residue : residue + piece]
        convolved = part if convolved is None else convolved + part
    value = convolved * scale + shift
    return (value / (1.0 + jnp.exp(-value))).astype(BF16)


def conv_inner_kernel(gated_ref, taps_ref, bn_ref, activated_ref, padded):
    total, width = gated_ref.shape
    piece = 32
    padded[HALO : HALO + total, :] = gated_ref[...].astype(F32)
    for col in range(0, width, PAIR):
        cols = slice(col, col + PAIR)
        taps = [taps_ref[j : j + 1, cols] for j in range(KERNEL)]
        scale, shift = bn_ref[0:1, cols], bn_ref[1:2, cols]

        def block(index, carry):
            start = pl.multiple_of(HALO + index * piece, HALO)
            activated_ref[pl.ds(start, piece), cols] = conv_rows(padded, start, piece, cols, taps, scale, shift)
            return carry

        lax.fori_loop(0, total // piece - 1, block, 0, unroll=3)


def conv_outer_kernel(gated_ref, left_ref, right_ref, taps_ref, bn_ref, activated_ref, w_ref, keep_ref, send_ref, padded):
    total, width = gated_ref.shape
    half = keep_ref.shape[1]
    ends = []
    for first, rows in (
        (True, (left_ref[...], gated_ref[: 2 * HALO, :])),
        (False, (gated_ref[total - 2 * HALO :, :], right_ref[...])),
    ):
        padded[...] = jnp.concatenate([part.astype(F32) for part in rows], axis=0)
        parts = []
        for col in range(0, width, PAIR):
            cols = slice(col, col + PAIR)
            taps = [taps_ref[j : j + 1, cols] for j in range(KERNEL)]
            parts.append(conv_rows(padded, 0, HALO, cols, taps, bn_ref[0:1, cols], bn_ref[1:2, cols]))
        ends.append(jnp.concatenate(parts, axis=1))
    share = jnp.concatenate([ends[0], activated_ref[HALO : total - HALO, :], ends[1]], axis=0)
    keep_ref[...] = jnp.dot(share, w_ref[:, :half], preferred_element_type=F32).astype(BF16)
    send_ref[...] = jnp.dot(share, w_ref[:, half:], preferred_element_type=F32).astype(BF16)


def pad_columns(weight, width):
    if weight.shape[1] == width:
        return weight
    return jnp.pad(weight, ((0, 0), (0, width - weight.shape[1])))


def on_device(
    frames_in,
    norm1_gain,
    norm1_bias,
    w_query,
    w_key,
    w_value,
    w_out,
    norm2_gain,
    norm2_bias,
    w_glu_value,
    w_glu_gate,
    depth_kernel,
    bn_scale,
    bn_shift,
    w_proj,
):
    frames, width = frames_in.shape
    grid, ctx = lax.axis_size("grid"), lax.axis_size("ctx")
    me = lax.axis_index("grid")
    place = me.astype(jnp.int32).reshape(1)
    order = list(range(0, grid, CORES)) + list(range(1, grid, CORES))
    padded = -(-width // PAIR) * PAIR
    query_rows = math.gcd(frames, 256)

    def by_distance(cells):
        return jnp.concatenate(
            [lax.dynamic_slice_in_dim(cells, (me ^ r) * width, width, 1) for r in order], axis=1
        )

    def over_chips(block):
        return [exchange(block, "grid", CORES * a) for a in range(1, grid // CORES)]

    def other_core(blocks):
        return [exchange(block, "grid", 1) for block in blocks]

    steps = [1 << k for k in range(1, ctx.bit_length() - 1)]
    raw = {0: frames_in}
    chips = {0: over_chips(frames_in)}
    for distance in steps:
        raw[distance] = exchange(frames_in, "ctx", distance)
    vectors = [norm1_gain, norm1_bias, norm2_gain, norm2_bias]
    (gains,) = kernel_call(
        stack_kernel,
        [((8, width), F32)],
        vectors,
        spaces={i: pltpu.HBM for i in range(len(vectors))},
        scratch=[pltpu.VMEM((width,), BF16)] * len(vectors) + [pltpu.SemaphoreType.DMA((len(vectors),))],
    )
    gains = [gains] + over_chips(gains)
    gains = gains + other_core(gains)

    w_query, w_key, w_value, w_glu_value, w_glu_gate = (
        pad_columns(weight, padded) for weight in (w_query, w_key, w_value, w_glu_value, w_glu_gate)
    )
    if width % PAIR:
        row_pad = ((0, padded - width), (0, 0))
        w_p = jnp.pad(by_distance(w_proj), row_pad)
    else:
        (w_p,) = kernel_call(
            functools.partial(reorder_kernel, order),
            [(w_proj.shape, BF16)],
            [place, w_proj],
            spaces={0: pltpu.SMEM, 1: pltpu.HBM},
            scratch=[pltpu.SemaphoreType.DMA((grid,))],
        )
    taps = pad_columns(depth_kernel, padded)
    bn = pad_columns(jnp.stack([bn_scale, bn_shift]), padded)
    qkv, qkv_sums = folded(place, order, 0, gains, (w_key, w_value, w_query))
    chips[0] = [after(block, qkv_sums) for block in chips[0]]
    glu, glu_sums = folded(place, order, 2, gains, (w_glu_value, w_glu_gate))
    raw.update({s: after(block, qkv_sums) for s, block in raw.items() if s})

    parts = lax.axis_size("parts")
    part = lax.axis_index("parts").astype(jnp.int32).reshape(1)
    if parts == 2:
        (half,) = kernel_call(
            half_kernel,
            [((width // 2, w_out.shape[1]), BF16)],
            [part, w_out],
            spaces={0: pltpu.SMEM, 1: pltpu.HBM},
            scratch=[pltpu.SemaphoreType.DMA((1,))],
        )
    else:
        half = w_out
    crossed = over_chips(after(half, *chips[0]))
    state_shape = ((frames, 4 * padded), F32)
    token_shape = ((8, 128), F32)
    own = [frames_in] + chips[0]
    blocks = own + other_core(own)
    own_blocks = blocks
    n = len(blocks)
    queries, keys, values, sent = kernel_call(
        functools.partial(project_kernel, n),
        [
            ((frames, 2 * padded), BF16),
            ((frames, padded), BF16),
            ((frames, 2 * padded), BF16),
            ((frames, 2 * padded), BF16),
        ],
        [*blocks, qkv, qkv_sums],
    )
    sent = exchange(sent, "ctx", 1)
    sequence = [2, 1, *range(3, ctx)] if ctx > 2 else [1]

    def prepare(s):
        if s > 1:
            low = s & -s
            if s != low:
                raw[s] = exchange(raw[s ^ low], "ctx", low)
            chips[s] = over_chips(raw[s])

    for s in sequence[:1]:
        prepare(s)
    state, token = kernel_call(
        functools.partial(first_kernel, query_rows),
        [state_shape, token_shape],
        [queries, keys, values, raw.get(2, frames_in)],
        spaces={3: pl.ANY},
    )
    crossed = [after(block, token) for block in crossed]
    swapped = [exchange(block, "parts", 1) for block in crossed] if parts == 2 else []
    pieces = [w_out]
    for a, block in enumerate(crossed):
        pieces += [block, swapped[a]] if swapped else [block]
    pieces = pieces + other_core(pieces)
    late = [crossed, swapped]
    for index, s in enumerate(sequence):
        last = index == len(sequence) - 1
        for ahead in sequence[index + 1 : index + 3]:
            if ahead not in chips:
                prepare(ahead)
        if s == 1:
            operands = [queries, state, sent]
            count = 0
        else:
            mine = [raw[s]] + [after(block, token) for block in chips[s]]
            operands = [queries, state, *mine, *other_core(mine), qkv, qkv_sums]
            count = n
        behind = late.pop(0) if late else []
        if index == 0:
            behind = [*behind, *[raw[ahead] for ahead in sequence[1:3] if ahead > 1]]
        outs = [((frames, padded), BF16)] if last else [state_shape, token_shape]
        results = kernel_call(
            functools.partial(slot_kernel, count, last, query_rows),
            outs,
            operands + behind,
            spaces={len(operands) + i: pl.ANY for i in range(len(behind))},
            aliases={} if last else {1: 0},
            scratch=[pltpu.VMEM(*state_shape)],
        )
        if last:
            (attended,) = results
        else:
            state, token = results
    attended = [attended] + over_chips(attended)
    attended = attended + other_core(attended)
    if width % PAIR:
        pieces = [by_distance(piece) for piece in pieces]
    middle, gated, head, tail = kernel_call(
        functools.partial(middle_kernel, n, order),
        [
            ((frames, width), BF16),
            ((frames, padded), BF16),
            ((HALO, padded), BF16),
            ((HALO, padded), BF16),
        ],
        [place, part, *attended, *own_blocks, *pieces, glu, glu_sums],
        spaces={0: pltpu.SMEM, 1: pltpu.SMEM},
        scratch=[pltpu.VMEM((frames, grid * width), BF16)],
    )
    left = lax.ppermute(tail, "ctx", [(i, i + 1) for i in range(ctx - 1)])
    right = lax.ppermute(head, "ctx", [(i + 1, i) for i in range(ctx - 1)])
    (activated,) = kernel_call(
        conv_inner_kernel,
        [((frames, padded), BF16)],
        [gated, taps, bn],
        scratch=[pltpu.VMEM((frames + 2 * HALO, padded), F32)],
    )
    keep, send = kernel_call(
        conv_outer_kernel,
        [((frames, grid // CORES * width), BF16)] * 2,
        [gated, left, right, taps, bn, activated, w_p],
        scratch=[pltpu.VMEM((3 * HALO, padded), F32)],
    )
    pair_sum = keep.astype(F32) + exchange(send, "grid", 1).astype(F32)
    result = middle.astype(F32) + pair_sum[:, :width]
    for a in range(1, grid // CORES):
        share = pair_sum[:, a * width : (a + 1) * width].astype(BF16)
        result = result + exchange(share, "grid", CORES * a).astype(F32)
    return result.astype(BF16)


def solution(mesh):
    return jax.shard_map(
        on_device,
        mesh=mesh,
        in_specs=(
            P(("parts", "ctx"), "grid"),
            P("grid"),
            P("grid"),
            P(None, "grid"),
            P(None, "grid"),
            P(None, "grid"),
            P("grid", None),
            P("grid"),
            P("grid"),
            P(None, "grid"),
            P(None, "grid"),
            P(None, "grid"),
            P("grid"),
            P("grid"),
            P("grid", None),
        ),
        out_specs=P(("parts", "ctx"), "grid"),
        check_vma=False,
    )
```

profile of v0, /device:TPU:0, one launch (start us, length us, event | category | flops | bytes accessed | tf_op | source)
XLA Modules:
  0.0 132.7 jit_solution(1169195824604196374)
XLA Ops:
  0.0 2.9 %collective-permute-start = (bf16[512,384]{1,0:T(8,128)(2,1)}, bf16[512,384]{1,0:T(8,128)(2,1)S(1)}, u32[]{:S(2)}, u32[]{:S(2)}) collective-permute-start(bf16[512,384]{1,0:T(8,128)(2,1)} %refs_4_.5), channel_id=1, source_target_pairs={{0,2},{1,3},{2,0},{3,1},{4,6},{5,7},{6,4},{7,5},{8,10},{9,11},{10,... | collective-permute-start | bytes 1179656 | tf_op jit(solution)/shard_map/ppermute | solution.py:26
  2.9 0.8 shard_map.145.refs_0_
  3.7 0.1 collective-permute-start.1
  3.8 0.1 collective-permute-start.2
  3.9 8.6 %collective-permute-done.1.refs_1_ = f32[8,384]{1,0:T(8,128)S(1)} collective-permute-done((f32[8,384]{1,0:T(8,128)S(1)}, f32[8,384]{1,0:T(8,128)S(1)}, u32[]{:S(2)}, u32[]{:S(2)}) %collective-permute-start.1) | collective-permute-done | bytes 12320 | tf_op jit(solution)/shard_map/ppermute | solution.py:26
  12.5 0.0 collective-permute-start.3
  12.5 0.5 collective-permute-start.4
  13.0 2.8 %collective-permute-start.6 = (bf16[512,384]{1,0:T(8,128)(2,1)}, bf16[512,384]{1,0:T(8,128)(2,1)S(1)}, u32[]{:S(2)}, u32[]{:S(2)}) collective-permute-start(bf16[512,384]{1,0:T(8,128)(2,1)} %refs_4_.5), channel_id=1, source_target_pairs={{0,8},{4,12},{8,0},{12,4},{1,9},{5,13},{9,1},{13,5},{2,10},{6,14},... | collective-permute-start | bytes 1179656 | tf_op jit(solution)/shard_map/ppermute | solution.py:26
  15.9 3.1 %shard_map.146 = (bf16[1536,1152]{1,0:T(8,128)(2,1)S(1)}, f32[2,1152]{1,0:T(2,128)S(1)}) custom-call(s32[1]{0:T(128)} %bitcast.me_ref, f32[8,384]{1,0:T(8,128)S(1)} %shard_map.145.refs_0_, f32[8,384]{1,0:T(8,128)S(1)} %collective-permute-done.1.refs_1_, f32[8,384]{1,0:T(8,128)S(1)} %collective-permute-done.2.refs_2_, ...), custom_call_target="tpu_custom_call" | custom-call | flops 1000 | bytes 1000 | tf_op jit(solution)/shard_map/pallas_call | solution.py:38
  19.0 0.1 collective-permute-start.5
  19.1 1.1 shard_map.152.refs_0_
  20.2 0.0 copy-start.1
  20.2 1.6 %collective-permute-start.10 = (bf16[192,1536]{1,0:T(8,128)(2,1)S(1)}, bf16[192,1536]{1,0:T(8,128)(2,1)S(1)}, u32[]{:S(2)}, u32[]{:S(2)}) collective-permute-start(bf16[192,1536]{1,0:T(8,128)(2,1)S(1)} %shard_map.153), channel_id=1, source_target_pairs={{0,2},{1,3},{2,0},{3,1},{4,6},{5,7},{6,4},{7,5},{8,10},{9,11},{10,... | collective-permute-start | bytes 1769480 | tf_op jit(solution)/shard_map/ppermute | solution.py:26
  21.8 12.0 %collective-permute-done.6.refs_0_ = bf16[512,384]{1,0:T(8,128)(2,1)S(1)} collective-permute-done((bf16[512,384]{1,0:T(8,128)(2,1)}, bf16[512,384]{1,0:T(8,128)(2,1)S(1)}, u32[]{:S(2)}, u32[]{:S(2)}) %collective-permute-start.6) | collective-permute-done | bytes 393248 | tf_op jit(solution)/shard_map/ppermute | solution.py:26
  33.8 1.5 %collective-permute-start.7 = (bf16[512,384]{1,0:T(8,128)(2,1)S(1)}, bf16[512,384]{1,0:T(8,128)(2,1)S(1)}, u32[]{:S(2)}, u32[]{:S(2)}) collective-permute-start(bf16[512,384]{1,0:T(8,128)(2,1)S(1)} %shard_map.149._.refs_2_), channel_id=1, source_target_pairs={{0,2},{1,3},{2,0},{3,1},{4,6},{5,7},{6,4},{7,5},{8,10},{9,11},{10,... | collective-permute-start | bytes 1179656 | tf_op jit(solution)/shard_map/ppermute | solution.py:26
  35.4 3.0 %shard_map.148 = (bf16[512,768]{1,0:T(8,128)(2,1)S(1)}, bf16[512,384]{1,0:T(8,128)(2,1)S(1)}, bf16[512,768]{1,0:T(8,128)(2,1)S(1)}, bf16[512,768]{1,0:T(8,128)(2,1)S(1)}) custom-call(bf16[512,384]{1,0:T(8,128)(2,1)S(1)} %copy-done.1, bf16[512,384]{1,0:T(8,128)(2,1)S(1)} %shard_map.147.refs_1_.refs_5_, ...), custom_call_target="tpu_custom_call" | custom-call | flops 1000 | bytes 1000 | tf_op jit(solution)/shard_map/pallas_call | solution.py:38
  38.3 0.8 collective-permute-start.12
  39.2 1.3 collective-permute-start.11
  40.4 3.7 %shard_map.150 = (f32[512,1536]{1,0:T(8,128)S(1)}, f32[8,128]{1,0:T(8,128)S(1)}) custom-call(bf16[512,768]{1,0:T(8,128)(2,1)S(1)} %get-tuple-element.26.query_ref.refs_0_, bf16[512,384]{1,0:T(8,128)(2,1)S(1)} %get-tuple-element.27.key_ref, bf16[512,768]{1,0:T(8,128)(2,1)S(1)} %get-tuple-element.28.value_ref, bf16[512,384]{1,0:T(8,128)(2,1)S(1)} %shard_map.149._.refs_2_), custom_call_target="tpu_custom_call" | custom-call | flops 1000 | bytes 1000 | tf_op jit(solution)/shard_map/pallas_call | solution.py:38
  44.2 0.0 copy-start
  44.2 1.6 %collective-permute-start.13 = (bf16[192,1536]{1,0:T(8,128)(2,1)S(1)}, bf16[192,1536]{1,0:T(8,128)(2,1)S(1)}, u32[]{:S(2)}, u32[]{:S(2)}) collective-permute-start(bf16[192,1536]{1,0:T(8,128)(2,1)S(1)} %shard_map.154.refs_8_.refs_9_), channel_id=1, source_target_pairs={{0,16},{16,0},{1,17},{17,1},{2,18},{18,2},{3,19},{19,3},{4,20},{20... | collective-permute-start | bytes 1769480 | tf_op jit(solution)/shard_map/ppermute | solution.py:26
  45.8 0.5 collective-permute-start.9
  46.3 18.8 %collective-permute-done.11.refs_9_.refs_2_ = bf16[512,384]{1,0:T(8,128)(2,1)S(1)} collective-permute-done((bf16[512,384]{1,0:T(8,128)(2,1)S(1)}, bf16[512,384]{1,0:T(8,128)(2,1)S(1)}, u32[]{:S(2)}, u32[]{:S(2)}) %collective-permute-start.11) | collective-permute-done | bytes 393248 | tf_op jit(solution)/shard_map/ppermute | solution.py:26
  65.1 0.7 collective-permute-start.14
  65.9 0.5 collective-permute-start.15
  66.4 8.9 %shard_map.155 = (f32[512,1536]{1,0:T(8,128)S(1)}, f32[8,128]{1,0:T(8,128)}) custom-call(bf16[512,768]{1,0:T(8,128)(2,1)S(1)} %get-tuple-element.26.query_ref.refs_0_, f32[512,1536]{1,0:T(8,128)S(1)} %get-tuple-element.29.refs_1_, bf16[512,384]{1,0:T(8,128)(2,1)S(1)} %shard_map.149._.refs_2_, ...), custom_call_target="tpu_custom_call", output_to_operand_aliasing={{0}: (1, {})} | custom-call | flops 1000 | bytes 1000 | tf_op jit(solution)/shard_map/pallas_call | solution.py:38
  75.3 4.2 %shard_map.156 = (f32[512,1536]{1,0:T(8,128)S(1)}, f32[8,128]{1,0:T(8,128)S(1)}) custom-call(bf16[512,768]{1,0:T(8,128)(2,1)S(1)} %get-tuple-element.26.query_ref.refs_0_, f32[512,1536]{1,0:T(8,128)S(1)} %get-tuple-element.31.refs_1_, bf16[512,768]{1,0:T(8,128)(2,1)S(1)} %collective-permute-done.12.refs_2_, ...), custom_call_target="tpu_custom_call", output_to_operand_aliasing={{0}: (1, {})} | custom-call | flops 1000 | bytes 1000 | tf_op jit(solution)/shard_map/pallas_call | solution.py:38
  79.5 0.1 collective-permute-start.16
  79.6 1.6 %collective-permute-done.16.refs_5_ = bf16[512,384]{1,0:T(8,128)(2,1)S(1)} collective-permute-done((bf16[512,384]{1,0:T(8,128)(2,1)S(1)}, bf16[512,384]{1,0:T(8,128)(2,1)S(1)}, u32[]{:S(2)}, u32[]{:S(2)}) %collective-permute-start.16) | collective-permute-done | bytes 393248 | tf_op jit(solution)/shard_map/ppermute | solution.py:26
  81.3 7.9 %shard_map.158.refs_0_ = bf16[512,384]{1,0:T(8,128)(2,1)S(1)} custom-call(bf16[512,768]{1,0:T(8,128)(2,1)S(1)} %get-tuple-element.26.query_ref.refs_0_, f32[512,1536]{1,0:T(8,128)S(1)} %get-tuple-element.33.refs_1_, bf16[512,384]{1,0:T(8,128)(2,1)S(1)} %collective-permute-done.11.refs_9_.refs_2_, bf16[512,384]{1,0:T(8,128)(2,1)S(1)} %shard_map.157.refs_3_, ...), custom_call_target="tpu_custom_call" | custom-call | flops 1000 | bytes 1000 | tf_op jit(solution)/shard_map/pallas_call | solution.py:38
  89.2 1.4 %collective-permute-start.17 = (bf16[512,384]{1,0:T(8,128)(2,1)S(1)}, bf16[512,384]{1,0:T(8,128)(2,1)S(1)}, u32[]{:S(2)}, u32[]{:S(2)}) collective-permute-start(bf16[512,384]{1,0:T(8,128)(2,1)S(1)} %shard_map.158.refs_0_), channel_id=1, source_target_pairs={{0,2},{1,3},{2,0},{3,1},{4,6},{5,7},{6,4},{7,5},{8,10},{9,11},{10,... | collective-permute-start | bytes 1179656 | tf_op jit(solution)/shard_map/ppermute | solution.py:26
  90.6 0.5 collective-permute-start.22
  91.1 9.3 %collective-permute-done.17.refs_1_ = bf16[512,384]{1,0:T(8,128)(2,1)S(1)} collective-permute-done((bf16[512,384]{1,0:T(8,128)(2,1)S(1)}, bf16[512,384]{1,0:T(8,128)(2,1)S(1)}, u32[]{:S(2)}, u32[]{:S(2)}) %collective-permute-start.17) | collective-permute-done | bytes 393248 | tf_op jit(solution)/shard_map/ppermute | solution.py:26
  100.5 2.6 %shard_map.159 = (bf16[1536,768]{1,0:T(8,128)(2,1)S(1)}, f32[2,768]{1,0:T(2,128)S(1)}) custom-call(s32[1]{0:T(128)} %bitcast.me_ref, f32[8,384]{1,0:T(8,128)S(1)} %shard_map.145.refs_0_, f32[8,384]{1,0:T(8,128)S(1)} %collective-permute-done.1.refs_1_, f32[8,384]{1,0:T(8,128)S(1)} %collective-permute-done.2.refs_2_, ...), custom_call_target="tpu_custom_call" | custom-call | flops 1000 | bytes 1000 | tf_op jit(solution)/shard_map/pallas_call | solution.py:38
  103.2 4.6 %shard_map.160 = (bf16[512,384]{1,0:T(8,128)(2,1)S(1)}, bf16[512,384]{1,0:T(8,128)(2,1)S(1)}, bf16[16,384]{1,0:T(8,128)(2,1)S(1)}, bf16[16,384]{1,0:T(8,128)(2,1)S(1)}) custom-call(s32[1]{0:T(128)} %bitcast.me_ref, s32[1]{0:T(128)} %bitcast.1.part_ref, bf16[512,384]{1,0:T(8,128)(2,1)S(1)} %shard_map.158.refs_0_, ...), custom_call_target="tpu_custom_call" | custom-call | flops 1000 | bytes 1000 | tf_op jit(solution)/shard_map/pallas_call | solution.py:38
  107.8 0.0 copy-start.2
  107.8 3.5 %collective-permute-start.23 = (bf16[16,384]{1,0:T(8,128)(2,1)S(1)}, bf16[16,384]{1,0:T(8,128)(2,1)S(1)}, u32[]{:S(2)}, u32[]{:S(2)}) collective-permute-start(bf16[16,384]{1,0:T(8,128)(2,1)S(1)} %get-tuple-element.39), channel_id=1, source_target_pairs={{0,4},{4,8},{8,12},{1,5},{5,9},{9,13},{2,6},{6,10},{10,14},{3,7},{... | collective-permute-start | bytes 36872 | tf_op jit(solution)/shard_map/ppermute | solution.py:550
  111.3 1.3 collective-permute-start.24
  112.6 1.3 shard_map.162.w_ref
  113.9 2.8 %shard_map.161.activated_ref = bf16[512,384]{1,0:T(8,128)(2,1)S(1)} custom-call(bf16[512,384]{1,0:T(8,128)(2,1)S(1)} %get-tuple-element.38.gated_ref, f32[31,384]{1,0:T(8,128)S(1)} %copy-done.2, f32[2,384]{1,0:T(2,128)S(1)} %pad_maximum_fusion.bn_ref), custom_call_target="tpu_custom_call" | custom-call | flops 1000 | bytes 1000 | tf_op jit(solution)/shard_map/pallas_call | solution.py:38
  116.7 0.3 collective-permute-done.24.right_ref
  117.0 1.1 shard_map.163
  118.0 0.1 collective-permute-start.25
  118.1 2.3 %collective-permute-done.25 = bf16[512,768]{1,0:T(8,128)(2,1)S(1)} collective-permute-done((bf16[512,768]{1,0:T(8,128)(2,1)S(1)}, bf16[512,768]{1,0:T(8,128)(2,1)S(1)}, u32[]{:S(2)}, u32[]{:S(2)}) %collective-permute-start.25) | collective-permute-done | bytes 786464 | tf_op jit(solution)/shard_map/ppermute | solution.py:26
  120.4 0.2 convert_add_fusion
  120.6 1.6 %collective-permute-start.26 = (bf16[512,384]{1,0:T(8,128)(2,1)S(1)}, bf16[512,384]{1,0:T(8,128)(2,1)S(1)}, u32[]{:S(2)}, u32[]{:S(2)}) collective-permute-start(bf16[512,384]{1,0:T(8,128)(2,1)S(1)} %slice.17), channel_id=1, source_target_pairs={{0,2},{1,3},{2,0},{3,1},{4,6},{5,7},{6,4},{7,5},{8,10},{9,11},{10,... | collective-permute-start | bytes 1179656 | tf_op jit(solution)/shard_map/ppermute | solution.py:26
  122.2 9.7 %collective-permute-done.26 = bf16[512,384]{1,0:T(8,128)(2,1)S(1)} collective-permute-done((bf16[512,384]{1,0:T(8,128)(2,1)S(1)}, bf16[512,384]{1,0:T(8,128)(2,1)S(1)}, u32[]{:S(2)}, u32[]{:S(2)}) %collective-permute-start.26) | collective-permute-done | bytes 393248 | tf_op jit(solution)/shard_map/ppermute | solution.py:26
  131.9 0.9 fusion.1
  (41 shorter events, 0.1 us)
Async XLA Ops:
  0.0 19.0 %collective-permute-start = (bf16[512,384]{1,0:T(8,128)(2,1)}, bf16[512,384]{1,0:T(8,128)(2,1)S(1)}, u32[]{:S(2)}, u32[]{:S(2)}) collective-permute-start(bf16[512,384]{1,0:T(8,128)(2,1)} %refs_4_.5), channel_id=1, source_target_pairs={{0,2},{1,3},{2,0},{3,1},{4,6},{5,7},{6,4},{7,5},{8,10},{9,11},{10,... | collective-permute-start | bytes 1179656 | tf_op jit(solution)/shard_map/ppermute | solution.py:26
  3.7 8.8 %collective-permute-start.1 = (f32[8,384]{1,0:T(8,128)S(1)}, f32[8,384]{1,0:T(8,128)S(1)}, u32[]{:S(2)}, u32[]{:S(2)}) collective-permute-start(f32[8,384]{1,0:T(8,128)S(1)} %shard_map.145.refs_0_), channel_id=1, source_target_pairs={{0,2},{1,3},{2,0},{3,1},{4,6},{5,7},{6,4},{7,5},{8,10},{9,11},{10,... | collective-permute-start | bytes 36872 | tf_op jit(solution)/shard_map/ppermute | solution.py:26
  3.8 12.1 %collective-permute-start.2 = (f32[8,384]{1,0:T(8,128)S(1)}, f32[8,384]{1,0:T(8,128)S(1)}, u32[]{:S(2)}, u32[]{:S(2)}) collective-permute-start(f32[8,384]{1,0:T(8,128)S(1)} %shard_map.145.refs_0_), channel_id=1, source_target_pairs={{0,1},{1,0},{2,3},{3,2},{4,5},{5,4},{6,7},{7,6},{8,9},{9,8},{10,11... | collective-permute-start | bytes 36872 | tf_op jit(solution)/shard_map/ppermute | solution.py:26
  12.5 3.4 %collective-permute-start.3 = (f32[8,384]{1,0:T(8,128)S(1)}, f32[8,384]{1,0:T(8,128)S(1)}, u32[]{:S(2)}, u32[]{:S(2)}) collective-permute-start(f32[8,384]{1,0:T(8,128)S(1)} %collective-permute-done.1.refs_1_), channel_id=1, source_target_pairs={{0,1},{1,0},{2,3},{3,2},{4,5},{5,4},{6,7},{7,6},{8,9},{9,8},{10,11... | collective-permute-start | bytes 36872 | tf_op jit(solution)/shard_map/ppermute | solution.py:26
  12.5 22.8 %collective-permute-start.4 = (bf16[512,384]{1,0:T(8,128)(2,1)}, bf16[512,384]{1,0:T(8,128)(2,1)S(1)}, u32[]{:S(2)}, u32[]{:S(2)}) collective-permute-start(bf16[512,384]{1,0:T(8,128)(2,1)} %refs_4_.5), channel_id=1, source_target_pairs={{0,1},{1,0},{2,3},{3,2},{4,5},{5,4},{6,7},{7,6},{8,9},{9,8},{10,11... | collective-permute-start | bytes 1179656 | tf_op jit(solution)/shard_map/ppermute | solution.py:26
  13.0 20.8 %collective-permute-start.6 = (bf16[512,384]{1,0:T(8,128)(2,1)}, bf16[512,384]{1,0:T(8,128)(2,1)S(1)}, u32[]{:S(2)}, u32[]{:S(2)}) collective-permute-start(bf16[512,384]{1,0:T(8,128)(2,1)} %refs_4_.5), channel_id=1, source_target_pairs={{0,8},{4,12},{8,0},{12,4},{1,9},{5,13},{9,1},{13,5},{2,10},{6,14},... | collective-permute-start | bytes 1179656 | tf_op jit(solution)/shard_map/ppermute | solution.py:26
  19.0 16.3 %collective-permute-start.5 = (bf16[512,384]{1,0:T(8,128)(2,1)S(1)}, bf16[512,384]{1,0:T(8,128)(2,1)S(1)}, u32[]{:S(2)}, u32[]{:S(2)}) collective-permute-start(bf16[512,384]{1,0:T(8,128)(2,1)S(1)} %shard_map.147.refs_1_.refs_5_), channel_id=1, source_target_pairs={{0,1},{1,0},{2,3},{3,2},{4,5},{5,4},{6,7},{7,6},{8,9},{9,8},{10,11... | collective-permute-start | bytes 1179656 | tf_op jit(solution)/shard_map/ppermute | solution.py:26
  20.2 15.2 %copy-start.1 = (bf16[512,384]{1,0:T(8,128)(2,1)S(1)}, bf16[512,384]{1,0:T(8,128)(2,1)}, u32[]{:S(2)}) copy-start(bf16[512,384]{1,0:T(8,128)(2,1)} %refs_4_.5) | copy-start | bytes 1179652
  20.2 24.0 %collective-permute-start.10 = (bf16[192,1536]{1,0:T(8,128)(2,1)S(1)}, bf16[192,1536]{1,0:T(8,128)(2,1)S(1)}, u32[]{:S(2)}, u32[]{:S(2)}) collective-permute-start(bf16[192,1536]{1,0:T(8,128)(2,1)S(1)} %shard_map.153), channel_id=1, source_target_pairs={{0,2},{1,3},{2,0},{3,1},{4,6},{5,7},{6,4},{7,5},{8,10},{9,11},{10,... | collective-permute-start | bytes 1769480 | tf_op jit(solution)/shard_map/ppermute | solution.py:26
  33.8 12.0 %collective-permute-start.7 = (bf16[512,384]{1,0:T(8,128)(2,1)S(1)}, bf16[512,384]{1,0:T(8,128)(2,1)S(1)}, u32[]{:S(2)}, u32[]{:S(2)}) collective-permute-start(bf16[512,384]{1,0:T(8,128)(2,1)S(1)} %shard_map.149._.refs_2_), channel_id=1, source_target_pairs={{0,2},{1,3},{2,0},{3,1},{4,6},{5,7},{6,4},{7,5},{8,10},{9,11},{10,... | collective-permute-start | bytes 1179656 | tf_op jit(solution)/shard_map/ppermute | solution.py:26
  38.3 37.0 %collective-permute-start.12 = (bf16[512,768]{1,0:T(8,128)(2,1)S(1)}, bf16[512,768]{1,0:T(8,128)(2,1)S(1)}, u32[]{:S(2)}, u32[]{:S(2)}) collective-permute-start(bf16[512,768]{1,0:T(8,128)(2,1)S(1)} %get-tuple-element.32), channel_id=1, source_target_pairs={{0,4},{4,0},{8,12},{12,8},{1,5},{5,1},{9,13},{13,9},{2,6},{6,2},{1... | collective-permute-start | bytes 2359304 | tf_op jit(solution)/shard_map/ppermute | solution.py:26
  39.2 26.0 %collective-permute-start.11 = (bf16[512,384]{1,0:T(8,128)(2,1)S(1)}, bf16[512,384]{1,0:T(8,128)(2,1)S(1)}, u32[]{:S(2)}, u32[]{:S(2)}) collective-permute-start(bf16[512,384]{1,0:T(8,128)(2,1)S(1)} %shard_map.149._.refs_2_), channel_id=1, source_target_pairs={{0,4},{4,0},{8,12},{12,8},{1,5},{5,1},{9,13},{13,9},{2,6},{6,2},{1... | collective-permute-start | bytes 1179656 | tf_op jit(solution)/shard_map/ppermute | solution.py:26
  44.2 21.7 %copy-start = (bf16[384,1536]{1,0:T(8,128)(2,1)S(1)}, bf16[384,1536]{1,0:T(8,128)(2,1)}, u32[]{:S(2)}) copy-start(bf16[384,1536]{1,0:T(8,128)(2,1)} %refs_8_.1) | copy-start | bytes 3538948
  44.2 31.1 %collective-permute-start.13 = (bf16[192,1536]{1,0:T(8,128)(2,1)S(1)}, bf16[192,1536]{1,0:T(8,128)(2,1)S(1)}, u32[]{:S(2)}, u32[]{:S(2)}) collective-permute-start(bf16[192,1536]{1,0:T(8,128)(2,1)S(1)} %shard_map.154.refs_8_.refs_9_), channel_id=1, source_target_pairs={{0,16},{16,0},{1,17},{17,1},{2,18},{18,2},{3,19},{19,3},{4,20},{20... | collective-permute-start | bytes 1769480 | tf_op jit(solution)/shard_map/ppermute | solution.py:26
  45.8 20.1 %collective-permute-start.8 = (bf16[512,384]{1,0:T(8,128)(2,1)S(1)}, bf16[512,384]{1,0:T(8,128)(2,1)S(1)}, u32[]{:S(2)}, u32[]{:S(2)}) collective-permute-start(bf16[512,384]{1,0:T(8,128)(2,1)S(1)} %shard_map.149._.refs_2_), channel_id=1, source_target_pairs={{0,1},{1,0},{2,3},{3,2},{4,5},{5,4},{6,7},{7,6},{8,9},{9,8},{10,11... | collective-permute-start | bytes 1179656 | tf_op jit(solution)/shard_map/ppermute | solution.py:26
  45.8 20.1 %collective-permute-start.9 = (bf16[512,384]{1,0:T(8,128)(2,1)S(1)}, bf16[512,384]{1,0:T(8,128)(2,1)S(1)}, u32[]{:S(2)}, u32[]{:S(2)}) collective-permute-start(bf16[512,384]{1,0:T(8,128)(2,1)S(1)} %shard_map.151.refs_3_), channel_id=1, source_target_pairs={{0,1},{1,0},{2,3},{3,2},{4,5},{5,4},{6,7},{7,6},{8,9},{9,8},{10,11... | collective-permute-start | bytes 1179656 | tf_op jit(solution)/shard_map/ppermute | solution.py:26
  65.1 14.3 %collective-permute-start.14 = (bf16[512,384]{1,0:T(8,128)(2,1)S(1)}, bf16[512,384]{1,0:T(8,128)(2,1)S(1)}, u32[]{:S(2)}, u32[]{:S(2)}) collective-permute-start(bf16[512,384]{1,0:T(8,128)(2,1)S(1)} %collective-permute-done.11.refs_9_.refs_2_), channel_id=1, source_target_pairs={{0,2},{1,3},{2,0},{3,1},{4,6},{5,7},{6,4},{7,5},{8,10},{9,11},{10,... | collective-permute-start | bytes 1179656 | tf_op jit(solution)/shard_map/ppermute | solution.py:26
  65.9 37.2 %collective-permute-start.20 = (bf16[384,1536]{1,0:T(8,128)(2,1)S(1)}, bf16[384,1536]{1,0:T(8,128)(2,1)S(1)}, u32[]{:S(2)}, u32[]{:S(2)}) collective-permute-start(bf16[384,1536]{1,0:T(8,128)(2,1)S(1)} %copy-done), channel_id=1, source_target_pairs={{0,1},{1,0},{2,3},{3,2},{4,5},{5,4},{6,7},{7,6},{8,9},{9,8},{10,11... | collective-permute-start | bytes 3538952 | tf_op jit(solution)/shard_map/ppermute | solution.py:26
  65.9 13.8 %collective-permute-start.15 = (bf16[512,384]{1,0:T(8,128)(2,1)S(1)}, bf16[512,384]{1,0:T(8,128)(2,1)S(1)}, u32[]{:S(2)}, u32[]{:S(2)}) collective-permute-start(bf16[512,384]{1,0:T(8,128)(2,1)S(1)} %collective-permute-done.11.refs_9_.refs_2_), channel_id=1, source_target_pairs={{0,1},{1,0},{2,3},{3,2},{4,5},{5,4},{6,7},{7,6},{8,9},{9,8},{10,11... | collective-permute-start | bytes 1179656 | tf_op jit(solution)/shard_map/ppermute | solution.py:26
  79.5 1.8 %collective-permute-start.16 = (bf16[512,384]{1,0:T(8,128)(2,1)S(1)}, bf16[512,384]{1,0:T(8,128)(2,1)S(1)}, u32[]{:S(2)}, u32[]{:S(2)}) collective-permute-start(bf16[512,384]{1,0:T(8,128)(2,1)S(1)} %shard_map.157.refs_3_), channel_id=1, source_target_pairs={{0,1},{1,0},{2,3},{3,2},{4,5},{5,4},{6,7},{7,6},{8,9},{9,8},{10,11... | collective-permute-start | bytes 1179656 | tf_op jit(solution)/shard_map/ppermute | solution.py:26
  81.3 19.2 %copy-start.3 = (f32[384]{0:T(512)S(1)}, f32[384]{0:T(512)}, u32[]{:S(2)}) copy-start(f32[384]{0:T(512)} %param.28) | copy-start | bytes 4612
  81.3 19.2 %copy-start.4 = (f32[384]{0:T(512)S(1)}, f32[384]{0:T(512)}, u32[]{:S(2)}) copy-start(f32[384]{0:T(512)} %param.27) | copy-start | bytes 4612
  89.2 11.2 %collective-permute-start.17 = (bf16[512,384]{1,0:T(8,128)(2,1)S(1)}, bf16[512,384]{1,0:T(8,128)(2,1)S(1)}, u32[]{:S(2)}, u32[]{:S(2)}) collective-permute-start(bf16[512,384]{1,0:T(8,128)(2,1)S(1)} %shard_map.158.refs_0_), channel_id=1, source_target_pairs={{0,2},{1,3},{2,0},{3,1},{4,6},{5,7},{6,4},{7,5},{8,10},{9,11},{10,... | collective-permute-start | bytes 1179656 | tf_op jit(solution)/shard_map/ppermute | solution.py:26
  90.6 12.5 %collective-permute-start.21 = (bf16[192,1536]{1,0:T(8,128)(2,1)S(1)}, bf16[192,1536]{1,0:T(8,128)(2,1)S(1)}, u32[]{:S(2)}, u32[]{:S(2)}) collective-permute-start(bf16[192,1536]{1,0:T(8,128)(2,1)S(1)} %shard_map.154.refs_8_.refs_9_), channel_id=1, source_target_pairs={{0,1},{1,0},{2,3},{3,2},{4,5},{5,4},{6,7},{7,6},{8,9},{9,8},{10,11... | collective-permute-start | bytes 1769480 | tf_op jit(solution)/shard_map/ppermute | solution.py:26
  90.6 12.5 %collective-permute-start.22 = (bf16[192,1536]{1,0:T(8,128)(2,1)S(1)}, bf16[192,1536]{1,0:T(8,128)(2,1)S(1)}, u32[]{:S(2)}, u32[]{:S(2)}) collective-permute-start(bf16[192,1536]{1,0:T(8,128)(2,1)S(1)} %collective-permute-done.13.refs_3_.refs_10_), channel_id=1, source_target_pairs={{0,1},{1,0},{2,3},{3,2},{4,5},{5,4},{6,7},{7,6},{8,9},{9,8},{10,11... | collective-permute-start | bytes 1769480 | tf_op jit(solution)/shard_map/ppermute | solution.py:26
  91.1 12.0 %collective-permute-start.18 = (bf16[512,384]{1,0:T(8,128)(2,1)S(1)}, bf16[512,384]{1,0:T(8,128)(2,1)S(1)}, u32[]{:S(2)}, u32[]{:S(2)}) collective-permute-start(bf16[512,384]{1,0:T(8,128)(2,1)S(1)} %shard_map.158.refs_0_), channel_id=1, source_target_pairs={{0,1},{1,0},{2,3},{3,2},{4,5},{5,4},{6,7},{7,6},{8,9},{9,8},{10,11... | collective-permute-start | bytes 1179656 | tf_op jit(solution)/shard_map/ppermute | solution.py:26
  100.5 2.7 %collective-permute-start.19 = (bf16[512,384]{1,0:T(8,128)(2,1)S(1)}, bf16[512,384]{1,0:T(8,128)(2,1)S(1)}, u32[]{:S(2)}, u32[]{:S(2)}) collective-permute-start(bf16[512,384]{1,0:T(8,128)(2,1)S(1)} %collective-permute-done.17.refs_1_), channel_id=1, source_target_pairs={{0,1},{1,0},{2,3},{3,2},{4,5},{5,4},{6,7},{7,6},{8,9},{9,8},{10,11... | collective-permute-start | bytes 1179656 | tf_op jit(solution)/shard_map/ppermute | solution.py:26
  107.8 6.1 %copy-start.2 = (f32[31,384]{1,0:T(8,128)S(1)}, f32[31,384]{1,0:T(8,128)}, u32[]{:S(2)}) copy-start(f32[31,384]{1,0:T(8,128)} %taps_ref.3) | copy-start | bytes 142852
  107.8 8.9 %collective-permute-start.23 = (bf16[16,384]{1,0:T(8,128)(2,1)S(1)}, bf16[16,384]{1,0:T(8,128)(2,1)S(1)}, u32[]{:S(2)}, u32[]{:S(2)}) collective-permute-start(bf16[16,384]{1,0:T(8,128)(2,1)S(1)} %get-tuple-element.39), channel_id=1, source_target_pairs={{0,4},{4,8},{8,12},{1,5},{5,9},{9,13},{2,6},{6,10},{10,14},{3,7},{... | collective-permute-start | bytes 36872 | tf_op jit(solution)/shard_map/ppermute | solution.py:550
  111.3 5.7 %collective-permute-start.24 = (bf16[16,384]{1,0:T(8,128)(2,1)S(1)}, bf16[16,384]{1,0:T(8,128)(2,1)S(1)}, u32[]{:S(2)}, u32[]{:S(2)}) collective-permute-start(bf16[16,384]{1,0:T(8,128)(2,1)S(1)} %get-tuple-element.40), channel_id=1, source_target_pairs={{4,0},{8,4},{12,8},{5,1},{9,5},{13,9},{6,2},{10,6},{14,10},{7,3},{... | collective-permute-start | bytes 36872 | tf_op jit(solution)/shard_map/ppermute | solution.py:551
  118.0 2.4 %collective-permute-start.25 = (bf16[512,768]{1,0:T(8,128)(2,1)S(1)}, bf16[512,768]{1,0:T(8,128)(2,1)S(1)}, u32[]{:S(2)}, u32[]{:S(2)}) collective-permute-start(bf16[512,768]{1,0:T(8,128)(2,1)S(1)} %get-tuple-element.42), channel_id=1, source_target_pairs={{0,1},{1,0},{2,3},{3,2},{4,5},{5,4},{6,7},{7,6},{8,9},{9,8},{10,11... | collective-permute-start | bytes 2359304 | tf_op jit(solution)/shard_map/ppermute | solution.py:26
  120.6 11.2 %collective-permute-start.26 = (bf16[512,384]{1,0:T(8,128)(2,1)S(1)}, bf16[512,384]{1,0:T(8,128)(2,1)S(1)}, u32[]{:S(2)}, u32[]{:S(2)}) collective-permute-start(bf16[512,384]{1,0:T(8,128)(2,1)S(1)} %slice.17), channel_id=1, source_target_pairs={{0,2},{1,3},{2,0},{3,1},{4,6},{5,7},{6,4},{7,5},{8,10},{9,11},{10,... | collective-permute-start | bytes 1179656 | tf_op jit(solution)/shard_map/ppermute | solution.py:26
where the time goes:
time: 133 us
  waiting for transfers between devices  62.8 us (47%)
  Pallas kernels  45 us (34%)
  starting transfers between devices  23.5 us (18%)
    ppermute x25, waiting for transfers between devices, exchange(): return lax.ppermute(cells, axis, [(i, i ^ distance) for i in range(count)])  62.5 us
    pallas_call x13, Pallas kernels, kernel_call(): pl.pallas_call(body, in_specs=in_specs, out_specs=tuple((pl.BlockSpec(mem...  45 us
    ppermute x25, starting transfers between devices, exchange(): return lax.ppermute(cells, axis, [(i, i ^ distance) for i in range(count)])  18.7 us
    ppermute x1, starting transfers between devices, on_device(): left = lax.ppermute(tail, 'ctx', [(i, i + 1) for i in range(ctx - 1)])  3.5 us
  transfers between devices with their start and end apart: 27, of which 8 were waited for; matrix products, arithmetic and copies ran while one was open for 0% of the time, Pallas kernels for 30%

commit v1 on v0

--- a/solution.py
+++ b/solution.py
@@ -63,18 +63,18 @@
     )(cells, *done)
 
 
-def fold_kernel(order, which, count, me_ref, *refs):
-    gains, refs = refs[: len(order)], refs[len(order) :]
+def fold_kernel(order, which, count, me_ref, gains_ref, *refs):
     sources, (folded_ref, sums_ref), weights, done = refs[:count], refs[count : count + 2], refs[count + 2 : -1], refs[-1]
     copies = [pltpu.make_async_copy(sources[n], weights[n], done.at[n]) for n in range(count)]
     for copy in copies:
         copy.start()
-    width = gains[0].shape[1]
+    width = gains_ref.shape[1]
     columns = weights[0].shape[1]
     factors = []
-    for k in range(len(order)):
-        gain = jnp.transpose(jnp.broadcast_to(gains[k][which : which + 1, :], (PAIR, width)))
-        bias = jnp.broadcast_to(gains[k][which + 1 : which + 2, :], (8, width)).astype(BF16)
+    for r in order:
+        gains = gains_ref[pl.ds(pl.multiple_of((me_ref[0] ^ r) * 8, 8), 8), :]
+        gain = jnp.transpose(jnp.broadcast_to(gains[which : which + 1, :], (PAIR, width)))
+        bias = jnp.broadcast_to(gains[which + 1 : which + 2, :], (8, width)).astype(BF16)
         factors.append((gain, bias))
     for n, ref in enumerate(weights):
         copies[n].wait()
@@ -99,12 +99,11 @@
 def folded(me, order, which, gains, weights):
     rows, columns = weights[0].shape
     total = columns * len(weights)
-    first = 1 + len(gains)
-    spaces = {first + n: pltpu.HBM for n in range(len(weights))}
+    spaces = {2 + n: pltpu.HBM for n in range(len(weights))}
     return kernel_call(
         functools.partial(fold_kernel, order, which, len(weights)),
         [((rows, total), BF16), ((2, total), F32)],
-        [me, *gains, *weights],
+        [me, gains, *weights],
         spaces={0: pltpu.SMEM, **spaces},
         scratch=[pltpu.VMEM((rows, columns), BF16)] * len(weights) + [pltpu.SemaphoreType.DMA((len(weights),))],
     )
@@ -180,8 +179,7 @@
 
 
 def project_kernel(count, *refs):
-    blocks, (folded_ref, sums_ref), (query_ref, key_ref, value_ref) = refs[:count], refs[count : count + 2], refs[-4:-1]
-    sent_ref = refs[-1]
+    blocks, (folded_ref, sums_ref), (query_ref, key_ref, value_ref) = refs[:count], refs[count : count + 2], refs[-3:]
     mean, scale = row_statistics(blocks)
     cells = jnp.concatenate([ref[...] for ref in blocks], axis=1)
     low = lane_masks()
@@ -190,7 +188,6 @@
         keys, low_values, high_values = keys_values(projected)
         queries = projected[:, 2 * PAIR :] * SCORE_SCALE
         base = 2 * j * PAIR
-        sent_ref[:, base : base + 2 * PAIR] = projected[:, : 2 * PAIR].astype(BF16)
         key_ref[:, j * PAIR : (j + 1) * PAIR] = keys
         value_ref[:, base : base + PAIR] = low_values
         value_ref[:, base + PAIR : base + 2 * PAIR] = high_values
@@ -235,25 +232,27 @@
 
 def slot_kernel(count, last, query_rows, *refs):
     query_ref, old_ref, *refs = refs
-    if count:
-        blocks, (folded_ref, sums_ref) = refs[:count], refs[count : count + 2]
-        mean, scale = row_statistics(blocks)
-        cells = jnp.concatenate([ref[...] for ref in blocks], axis=1)
+    blocks, (folded_ref, sums_ref) = refs[:count], refs[count : count + 2]
+    part, key_ref, value_ref = refs[-3:]
+    if last:
+        attended = refs[-4]
     else:
-        sent_ref = refs[0]
-    if last:
-        attended, part = refs[-2:]
-    else:
-        state_ref, token_ref, part = refs[-3:]
+        state_ref, token_ref = refs[-5:-3]
         token_ref[...] = jnp.zeros_like(token_ref)
+    mean, scale = row_statistics(blocks)
+    cells = jnp.concatenate([ref[...] for ref in blocks], axis=1)
     pairs = query_ref.shape[1] // (2 * PAIR)
     for j in range(pairs):
-        if count:
-            projected = norm_product(cells, mean, scale, folded_ref, sums_ref, j * 3 * PAIR, 2 * PAIR)
-        else:
-            projected = sent_ref[:, 2 * j * PAIR : 2 * (j + 1) * PAIR].astype(F32)
-        keys, *values = keys_values(projected)
-        attend_pair(j, query_rows, query_ref, keys, values, part)
+        projected = norm_product(cells, mean, scale, folded_ref, sums_ref, j * 3 * PAIR, 2 * PAIR)
+        base = 2 * j * PAIR
+        (
+            key_ref[:, j * PAIR : (j + 1) * PAIR],
+            value_ref[:, base : base + PAIR],
+            value_ref[:, base + PAIR : base + 2 * PAIR],
+        ) = keys_values(projected)
+    for j in range(pairs):
+        values = [value_ref[:, n * PAIR : (n + 1) * PAIR] for n in (2 * j, 2 * j + 1)]
+        attend_pair(j, query_rows, query_ref, key_ref[:, j * PAIR : (j + 1) * PAIR], values, part)
     total = query_ref.shape[0]
     low = lane_masks()
     for start in range(0, total, query_rows):
@@ -412,11 +411,6 @@
     def other_core(blocks):
         return [exchange(block, "grid", 1) for block in blocks]
 
-    steps = [1 << k for k in range(1, ctx.bit_length() - 1)]
-    raw = {0: frames_in}
-    chips = {0: over_chips(frames_in)}
-    for distance in steps:
-        raw[distance] = exchange(frames_in, "ctx", distance)
     vectors = [norm1_gain, norm1_bias, norm2_gain, norm2_bias]
     (gains,) = kernel_call(
         stack_kernel,
@@ -425,8 +419,11 @@
         spaces={i: pltpu.HBM for i in range(len(vectors))},
         scratch=[pltpu.VMEM((width,), BF16)] * len(vectors) + [pltpu.SemaphoreType.DMA((len(vectors),))],
     )
-    gains = [gains] + over_chips(gains)
-    gains = gains + other_core(gains)
+    gains = lax.all_gather(gains, "grid", axis=0, tiled=True)
+    raw = {0: frames_in}
+    chips = {0: over_chips(frames_in)}
+    for k in reversed(range(ctx.bit_length() - 1)):
+        raw[1 << k] = exchange(frames_in, "ctx", 1 << k)
 
     w_query, w_key, w_value, w_glu_value, w_glu_gate = (
         pad_columns(weight, padded) for weight in (w_query, w_key, w_value, w_glu_value, w_glu_gate)
@@ -447,7 +444,6 @@
     qkv, qkv_sums = folded(place, order, 0, gains, (w_key, w_value, w_query))
     chips[0] = [after(block, qkv_sums) for block in chips[0]]
     glu, glu_sums = folded(place, order, 2, gains, (w_glu_value, w_glu_gate))
-    raw.update({s: after(block, qkv_sums) for s, block in raw.items() if s})
 
     parts = lax.axis_size("parts")
     part = lax.axis_index("parts").astype(jnp.int32).reshape(1)
@@ -464,36 +460,31 @@
     crossed = over_chips(after(half, *chips[0]))
     state_shape = ((frames, 4 * padded), F32)
     token_shape = ((8, 128), F32)
+    wide, narrow = ((frames, 2 * padded), BF16), ((frames, padded), BF16)
+    chips[1] = [exchange(block, "ctx", 1) for block in chips[0]]
     own = [frames_in] + chips[0]
-    blocks = own + other_core(own)
-    own_blocks = blocks
-    n = len(blocks)
-    queries, keys, values, sent = kernel_call(
+    own_blocks = own + other_core(own)
+    n = len(own_blocks)
+    early = [raw[s] for s in raw if s]
+    queries, keys, values = kernel_call(
         functools.partial(project_kernel, n),
-        [
-            ((frames, 2 * padded), BF16),
-            ((frames, padded), BF16),
-            ((frames, 2 * padded), BF16),
-            ((frames, 2 * padded), BF16),
-        ],
-        [*blocks, qkv, qkv_sums],
-    )
-    sent = exchange(sent, "ctx", 1)
-    sequence = [2, 1, *range(3, ctx)] if ctx > 2 else [1]
+        [wide, narrow, wide],
+        [*own_blocks, qkv, qkv_sums, *early],
+        spaces={n + 2 + i: pl.ANY for i in range(len(early))},
+    )
 
     def prepare(s):
-        if s > 1:
-            low = s & -s
-            if s != low:
-                raw[s] = exchange(raw[s ^ low], "ctx", low)
-            chips[s] = over_chips(raw[s])
-
-    for s in sequence[:1]:
+        low = s & -s
+        if s != low:
+            raw[s] = exchange(raw[s ^ low], "ctx", low)
+        chips[s] = over_chips(raw[s])
+
+    for s in range(2, min(ctx, 4)):
         prepare(s)
     state, token = kernel_call(
         functools.partial(first_kernel, query_rows),
         [state_shape, token_shape],
-        [queries, keys, values, raw.get(2, frames_in)],
+        [queries, keys, values, frames_in],
         spaces={3: pl.ANY},
     )
     crossed = [after(block, token) for block in crossed]
@@ -502,36 +493,27 @@
     for a, block in enumerate(crossed):
         pieces += [block, swapped[a]] if swapped else [block]
     pieces = pieces + other_core(pieces)
-    late = [crossed, swapped]
-    for index, s in enumerate(sequence):
-        last = index == len(sequence) - 1
-        for ahead in sequence[index + 1 : index + 3]:
-            if ahead not in chips:
-                prepare(ahead)
-        if s == 1:
-            operands = [queries, state, sent]
-            count = 0
-        else:
-            mine = [raw[s]] + [after(block, token) for block in chips[s]]
-            operands = [queries, state, *mine, *other_core(mine), qkv, qkv_sums]
-            count = n
-        behind = late.pop(0) if late else []
-        if index == 0:
-            behind = [*behind, *[raw[ahead] for ahead in sequence[1:3] if ahead > 1]]
-        outs = [((frames, padded), BF16)] if last else [state_shape, token_shape]
+    late = {1: [*crossed, *[raw[s] for s in (3,) if s < ctx]], 2: swapped}
+    for s in range(1, ctx):
+        last = s == ctx - 1
+        if s + 2 < ctx and s + 2 not in chips:
+            prepare(s + 2)
+        mine = [raw[s]] + [after(block, token) for block in chips[s]]
+        operands = [queries, state, *mine, *other_core(mine), qkv, qkv_sums]
+        behind = late.get(s, [])
         results = kernel_call(
-            functools.partial(slot_kernel, count, last, query_rows),
-            outs,
+            functools.partial(slot_kernel, n, last, query_rows),
+            [narrow] if last else [state_shape, token_shape],
             operands + behind,
             spaces={len(operands) + i: pl.ANY for i in range(len(behind))},
             aliases={} if last else {1: 0},
-            scratch=[pltpu.VMEM(*state_shape)],
+            scratch=[pltpu.VMEM(*shape) for shape in (state_shape, narrow, wide)],
         )
         if last:
             (attended,) = results
         else:
             state, token = results
-    attended = [attended] + over_chips(attended)
+    attended = [attended] + [after(block, glu_sums, w_p) for block in over_chips(attended)]
     attended = attended + other_core(attended)
     if width % PAIR:
         pieces = [by_distance(piece) for piece in pieces]

time: 133 us -> 110 us (0.83)
  waiting for transfers between devices: 62.8 us -> 34 us
  blocking collectives: 0 us -> 5.48 us
    ppermute x25, waiting for transfers between devices: 62.5 us -> 32.6 us  [exchange(): return lax.ppermute(cells, axis, [(i, i ^ distance) for i in range(count)])]
    all_gather x0 -> x1, blocking collectives: none -> 5.48 us  [on_device(): gains = lax.all_gather(gains, 'grid', axis=0, tiled=True)]
  transfers between devices with their start and end apart: 27 -> 27, of which waited for: 8 -> 13; matrix products, arithmetic and copies ran while one was open for 0% -> 0% of each run, Pallas kernels for 30% -> 35%
where the time goes in v1:
time: 110 us
  Pallas kernels  46 us (42%)
  waiting for transfers between devices  34 us (31%)
  starting transfers between devices  23 us (21%)
  blocking collectives  5.48 us (5%)
    pallas_call x13, Pallas kernels, kernel_call(): pl.pallas_call(body, in_specs=in_specs, out_specs=tuple((pl.BlockSpec(mem...  46 us
    ppermute x25, waiting for transfers between devices, exchange(): return lax.ppermute(cells, axis, [(i, i ^ distance) for i in range(count)])  32.6 us
    ppermute x25, starting transfers between devices, exchange(): return lax.ppermute(cells, axis, [(i, i ^ distance) for i in range(count)])  18.3 us
    all_gather x1, blocking collectives, on_device(): gains = lax.all_gather(gains, 'grid', axis=0, tiled=True)  5.48 us
    ppermute x1, starting transfers between devices, on_device(): left = lax.ppermute(tail, 'ctx', [(i, i + 1) for i in range(ctx - 1)])  3.41 us
  transfers between devices with their start and end apart: 27, of which 13 were waited for; matrix products, arithmetic and copies ran while one was open for 0% of the time, Pallas kernels for 35%

profile of v1, /device:TPU:0, one launch (start us, length us, event | category | flops | bytes accessed | tf_op | source)
XLA Modules:
  0.0 110.1 jit_solution(16984934778360308219)
XLA Ops:
  0.0 2.9 %collective-permute-start = (bf16[512,384]{1,0:T(8,128)(2,1)}, bf16[512,384]{1,0:T(8,128)(2,1)}, u32[]{:S(2)}, u32[]{:S(2)}) collective-permute-start(bf16[512,384]{1,0:T(8,128)(2,1)} %refs_4_.1), channel_id=1, source_target_pairs={{0,2},{1,3},{2,0},{3,1},{4,6},{5,7},{6,4},{7,5},{8,10},{9,11},{10,... | collective-permute-start | bytes 1179656 | tf_op jit(solution)/shard_map/ppermute | solution.py:26
  2.9 2.6 %collective-permute-start.3 = (bf16[512,384]{1,0:T(8,128)(2,1)}, bf16[512,384]{1,0:T(8,128)(2,1)}, u32[]{:S(2)}, u32[]{:S(2)}) collective-permute-start(bf16[512,384]{1,0:T(8,128)(2,1)} %refs_4_.1), channel_id=1, source_target_pairs={{0,8},{4,12},{8,0},{12,4},{1,9},{5,13},{9,1},{13,5},{2,10},{6,14},... | collective-permute-start | bytes 1179656 | tf_op jit(solution)/shard_map/ppermute | solution.py:26
  5.5 1.6 %collective-permute-start.4 = (bf16[512,384]{1,0:T(8,128)(2,1)}, bf16[512,384]{1,0:T(8,128)(2,1)}, u32[]{:S(2)}, u32[]{:S(2)}) collective-permute-start(bf16[512,384]{1,0:T(8,128)(2,1)} %refs_4_.1), channel_id=1, source_target_pairs={{0,4},{4,0},{8,12},{12,8},{1,5},{5,1},{9,13},{13,9},{2,6},{6,2},{1... | collective-permute-start | bytes 1179656 | tf_op jit(solution)/shard_map/ppermute | solution.py:26
  7.1 0.8 shard_map.145
  7.9 5.5 %all_gather.3.gains_ref = f32[32,384]{1,0:T(8,128)S(1)} all-gather(f32[8,384]{1,0:T(8,128)S(1)} %shard_map.145), channel_id=1, replica_groups=mesh['parts'=2,'ctx'=4,'grid'=4] {'grid'}, dimensions={0}, use_global_device_ids=true | all-gather | bytes 61440 | tf_op jit(solution)/shard_map/all_gather | solution.py:422
  13.4 3.0 %shard_map.146 = (bf16[1536,1152]{1,0:T(8,128)(2,1)S(1)}, f32[2,1152]{1,0:T(2,128)S(1)}) custom-call(s32[1]{0:T(128)} %bitcast.me_ref, f32[32,384]{1,0:T(8,128)S(1)} %all_gather.3.gains_ref, bf16[1536,384]{1,0:T(8,128)(2,1)} %refs_0_.5, bf16[1536,384]{1,0:T(8,128)(2,1)} %refs_1_.4, bf16[1536,384]{1,0:T(8,128)(2,1)} %refs_2_.3), custom_call_target="tpu_custom_call" | custom-call | flops 1000 | bytes 1000 | tf_op jit(solution)/shard_map/pallas_call | solution.py:38
  16.4 0.4 collective-permute-start.2
  16.8 1.8 %collective-permute-start.5 = (bf16[512,384]{1,0:T(8,128)(2,1)}, bf16[512,384]{1,0:T(8,128)(2,1)}, u32[]{:S(2)}, u32[]{:S(2)}) collective-permute-start(bf16[512,384]{1,0:T(8,128)(2,1)} %shard_map.147.refs_1_.refs_5_), channel_id=1, source_target_pairs={{0,4},{4,0},{8,12},{12,8},{1,5},{5,1},{9,13},{13,9},{2,6},{6,2},{1... | collective-permute-start | bytes 1179656 | tf_op jit(solution)/shard_map/ppermute | solution.py:26
  18.6 1.1 %shard_map.151.refs_0_ = bf16[192,1536]{1,0:T(8,128)(2,1)S(1)} custom-call(s32[1]{0:T(128)} %bitcast.1.part_ref, bf16[384,1536]{1,0:T(8,128)(2,1)} %refs_8_.1), custom_call_target="tpu_custom_call" | custom-call | flops 1000 | bytes 1000 | tf_op jit(solution)/shard_map/pallas_call | solution.py:38
  19.7 3.5 %collective-permute-done.3.refs_6_.refs_2_ = bf16[512,384]{1,0:T(8,128)(2,1)} collective-permute-done((bf16[512,384]{1,0:T(8,128)(2,1)}, bf16[512,384]{1,0:T(8,128)(2,1)}, u32[]{:S(2)}, u32[]{:S(2)}) %collective-permute-start.3) | collective-permute-done | bytes 393248 | tf_op jit(solution)/shard_map/ppermute | solution.py:26
  23.3 0.5 collective-permute-start.8
  23.8 0.1 collective-permute-done.4.refs_7_.refs_2_
  23.9 2.5 %collective-permute-start.9 = (bf16[512,384]{1,0:T(8,128)(2,1)}, bf16[512,384]{1,0:T(8,128)(2,1)S(1)}, u32[]{:S(2)}, u32[]{:S(2)}) collective-permute-start(bf16[512,384]{1,0:T(8,128)(2,1)} %collective-permute-done.3.refs_6_.refs_2_), channel_id=1, source_target_pairs={{0,4},{4,0},{8,12},{12,8},{1,5},{5,1},{9,13},{13,9},{2,6},{6,2},{1... | collective-permute-start | bytes 1179656 | tf_op jit(solution)/shard_map/ppermute | solution.py:26
  26.4 4.2 %shard_map.148 = (bf16[512,768]{1,0:T(8,128)(2,1)S(1)}, bf16[512,384]{1,0:T(8,128)(2,1)S(1)}, bf16[512,768]{1,0:T(8,128)(2,1)S(1)}) custom-call(bf16[512,384]{1,0:T(8,128)(2,1)S(1)} %copy-done.1, bf16[512,384]{1,0:T(8,128)(2,1)} %shard_map.147.refs_1_.refs_5_, bf16[512,384]{1,0:T(8,128)(2,1)} %collective-permute-done.1.refs_2_.refs_6_, ...), custom_call_target="tpu_custom_call" | custom-call | flops 1000 | bytes 1000 | tf_op jit(solution)/shard_map/pallas_call | solution.py:38
  30.6 3.7 %shard_map.149 = (f32[512,1536]{1,0:T(8,128)S(1)}, f32[8,128]{1,0:T(8,128)S(1)}) custom-call(bf16[512,768]{1,0:T(8,128)(2,1)S(1)} %get-tuple-element.26.query_ref.refs_0_, bf16[512,384]{1,0:T(8,128)(2,1)S(1)} %get-tuple-element.27.key_ref, bf16[512,768]{1,0:T(8,128)(2,1)S(1)} %get-tuple-element.28.value_ref, bf16[512,384]{1,0:T(8,128)(2,1)S(1)} %copy-done.1), custom_call_target="tpu_custom_call" | custom-call | flops 1000 | bytes 1000 | tf_op jit(solution)/shard_map/pallas_call | solution.py:38
  34.3 0.6 collective-permute-start.7
  34.9 0.5 collective-permute-start.10
  35.4 2.0 %collective-permute-done.8.refs_0_ = bf16[192,1536]{1,0:T(8,128)(2,1)S(1)} collective-permute-done((bf16[192,1536]{1,0:T(8,128)(2,1)S(1)}, bf16[192,1536]{1,0:T(8,128)(2,1)S(1)}, u32[]{:S(2)}, u32[]{:S(2)}) %collective-permute-start.8) | collective-permute-done | bytes 589856 | tf_op jit(solution)/shard_map/ppermute | solution.py:26
  37.4 1.5 %collective-permute-start.13 = (bf16[192,1536]{1,0:T(8,128)(2,1)S(1)}, bf16[192,1536]{1,0:T(8,128)(2,1)S(1)}, u32[]{:S(2)}, u32[]{:S(2)}) collective-permute-start(bf16[192,1536]{1,0:T(8,128)(2,1)S(1)} %shard_map.153.refs_8_.refs_9_), channel_id=1, source_target_pairs={{0,16},{16,0},{1,17},{17,1},{2,18},{18,2},{3,19},{19,3},{4,20},{20... | collective-permute-start | bytes 1769480 | tf_op jit(solution)/shard_map/ppermute | solution.py:26
  38.9 1.3 %collective-permute-done.9.refs_9_.refs_2_ = bf16[512,384]{1,0:T(8,128)(2,1)S(1)} collective-permute-done((bf16[512,384]{1,0:T(8,128)(2,1)}, bf16[512,384]{1,0:T(8,128)(2,1)S(1)}, u32[]{:S(2)}, u32[]{:S(2)}) %collective-permute-start.9) | collective-permute-done | bytes 393248 | tf_op jit(solution)/shard_map/ppermute | solution.py:26
  40.2 7.2 %shard_map.154 = (f32[512,1536]{1,0:T(8,128)S(1)}, f32[8,128]{1,0:T(8,128)S(1)}) custom-call(bf16[512,768]{1,0:T(8,128)(2,1)S(1)} %get-tuple-element.26.query_ref.refs_0_, f32[512,1536]{1,0:T(8,128)S(1)} %get-tuple-element.29.refs_1_, bf16[512,384]{1,0:T(8,128)(2,1)} %collective-permute-done.4.refs_7_.refs_2_, ...), custom_call_target="tpu_custom_call", output_to_operand_aliasing={{0}: (1, {})} | custom-call | flops 1000 | bytes 1000 | tf_op jit(solution)/shard_map/pallas_call | solution.py:38
  47.4 0.6 collective-permute-start.12
  48.0 0.5 collective-permute-start.14
  48.5 0.8 collective-permute-done.12.refs_5_
  49.3 1.3 %collective-permute-done.13.refs_8_.refs_10_ = bf16[192,1536]{1,0:T(8,128)(2,1)S(1)} collective-permute-done((bf16[192,1536]{1,0:T(8,128)(2,1)S(1)}, bf16[192,1536]{1,0:T(8,128)(2,1)S(1)}, u32[]{:S(2)}, u32[]{:S(2)}) %collective-permute-start.13) | collective-permute-done | bytes 589856 | tf_op jit(solution)/shard_map/ppermute | solution.py:26
  50.6 7.0 %shard_map.156 = (f32[512,1536]{1,0:T(8,128)S(1)}, f32[8,128]{1,0:T(8,128)S(1)}) custom-call(bf16[512,768]{1,0:T(8,128)(2,1)S(1)} %get-tuple-element.26.query_ref.refs_0_, f32[512,1536]{1,0:T(8,128)S(1)} %get-tuple-element.31.refs_1_, bf16[512,384]{1,0:T(8,128)(2,1)} %collective-permute-done.3.refs_6_.refs_2_, ...), custom_call_target="tpu_custom_call", output_to_operand_aliasing={{0}: (1, {})} | custom-call | flops 1000 | bytes 1000 | tf_op jit(solution)/shard_map/pallas_call | solution.py:38
  57.6 1.5 %collective-permute-done.14.refs_0_ = bf16[512,384]{1,0:T(8,128)(2,1)S(1)} collective-permute-done((bf16[512,384]{1,0:T(8,128)(2,1)S(1)}, bf16[512,384]{1,0:T(8,128)(2,1)S(1)}, u32[]{:S(2)}, u32[]{:S(2)}) %collective-permute-start.14) | collective-permute-done | bytes 393248 | tf_op jit(solution)/shard_map/ppermute | solution.py:26
  59.1 0.5 collective-permute-start.20
  59.6 1.2 %collective-permute-done.16.refs_5_ = bf16[512,384]{1,0:T(8,128)(2,1)S(1)} collective-permute-done((bf16[512,384]{1,0:T(8,128)(2,1)S(1)}, bf16[512,384]{1,0:T(8,128)(2,1)S(1)}, u32[]{:S(2)}, u32[]{:S(2)}) %collective-permute-start.16) | collective-permute-done | bytes 393248 | tf_op jit(solution)/shard_map/ppermute | solution.py:26
  60.8 5.7 %shard_map.158.refs_0_ = bf16[512,384]{1,0:T(8,128)(2,1)S(1)} custom-call(bf16[512,768]{1,0:T(8,128)(2,1)S(1)} %get-tuple-element.26.query_ref.refs_0_, f32[512,1536]{1,0:T(8,128)S(1)} %get-tuple-element.33.refs_1_, bf16[512,384]{1,0:T(8,128)(2,1)S(1)} %collective-permute-done.9.refs_9_.refs_2_, bf16[512,384]{1,0:T(8,128)(2,1)S(1)} %shard_map.157.refs_3_, ...), custom_call_target="tpu_custom_call" | custom-call | flops 1000 | bytes 1000 | tf_op jit(solution)/shard_map/pallas_call | solution.py:38
  66.5 0.6 collective-permute-start.17
  67.1 0.5 collective-permute-start.22
  67.6 1.3 %shard_map.160.refs_2_.w_ref = bf16[384,1536]{1,0:T(8,128)(2,1)S(1)} custom-call(s32[1]{0:T(128)} %bitcast.me_ref, bf16[384,1536]{1,0:T(8,128)(2,1)} %source_ref.3), custom_call_target="tpu_custom_call" | custom-call | flops 1000 | bytes 1000 | tf_op jit(solution)/shard_map/pallas_call | solution.py:38
  68.9 2.4 %shard_map.159 = (bf16[1536,768]{1,0:T(8,128)(2,1)S(1)}, f32[2,768]{1,0:T(2,128)S(1)}) custom-call(s32[1]{0:T(128)} %bitcast.me_ref, f32[32,384]{1,0:T(8,128)S(1)} %copy-done.3, bf16[1536,384]{1,0:T(8,128)(2,1)} %refs_0_.7, bf16[1536,384]{1,0:T(8,128)(2,1)} %refs_1_.5), custom_call_target="tpu_custom_call" | custom-call | flops 1000 | bytes 1000 | tf_op jit(solution)/shard_map/pallas_call | solution.py:38
  71.3 0.1 collective-permute-start.18
  71.4 6.3 %collective-permute-done.17.refs_0_ = bf16[512,384]{1,0:T(8,128)(2,1)S(1)} collective-permute-done((bf16[512,384]{1,0:T(8,128)(2,1)S(1)}, bf16[512,384]{1,0:T(8,128)(2,1)S(1)}, u32[]{:S(2)}, u32[]{:S(2)}) %collective-permute-start.17) | collective-permute-done | bytes 393248 | tf_op jit(solution)/shard_map/ppermute | solution.py:26
  77.8 1.6 %collective-permute-done.19.refs_3_ = bf16[512,384]{1,0:T(8,128)(2,1)S(1)} collective-permute-done((bf16[512,384]{1,0:T(8,128)(2,1)S(1)}, bf16[512,384]{1,0:T(8,128)(2,1)S(1)}, u32[]{:S(2)}, u32[]{:S(2)}) %collective-permute-start.19) | collective-permute-done | bytes 393248 | tf_op jit(solution)/shard_map/ppermute | solution.py:26
  79.5 5.9 %shard_map.162 = (bf16[512,384]{1,0:T(8,128)(2,1)S(1)}, bf16[512,384]{1,0:T(8,128)(2,1)S(1)}, bf16[16,384]{1,0:T(8,128)(2,1)S(1)}, bf16[16,384]{1,0:T(8,128)(2,1)S(1)}) custom-call(s32[1]{0:T(128)} %bitcast.me_ref, s32[1]{0:T(128)} %bitcast.1.part_ref, bf16[512,384]{1,0:T(8,128)(2,1)S(1)} %shard_map.158.refs_0_, bf16[512,384]{1,0:T(8,128)(2,1)S(1)} %shard_map.161.refs_1_, ...), custom_call_target="tpu_custom_call" | custom-call | flops 1000 | bytes 1000 | tf_op jit(solution)/shard_map/pallas_call | solution.py:38
  85.3 3.4 %collective-permute-start.23 = (bf16[16,384]{1,0:T(8,128)(2,1)S(1)}, bf16[16,384]{1,0:T(8,128)(2,1)S(1)}, u32[]{:S(2)}, u32[]{:S(2)}) collective-permute-start(bf16[16,384]{1,0:T(8,128)(2,1)S(1)} %get-tuple-element.39), channel_id=1, source_target_pairs={{0,4},{4,8},{8,12},{1,5},{5,9},{9,13},{2,6},{6,10},{10,14},{3,7},{... | collective-permute-start | bytes 36872 | tf_op jit(solution)/shard_map/ppermute | solution.py:532
  88.7 1.3 %collective-permute-start.24 = (bf16[16,384]{1,0:T(8,128)(2,1)S(1)}, bf16[16,384]{1,0:T(8,128)(2,1)S(1)}, u32[]{:S(2)}, u32[]{:S(2)}) collective-permute-start(bf16[16,384]{1,0:T(8,128)(2,1)S(1)} %get-tuple-element.40), channel_id=1, source_target_pairs={{4,0},{8,4},{12,8},{5,1},{9,5},{13,9},{6,2},{10,6},{14,10},{7,3},{... | collective-permute-start | bytes 36872 | tf_op jit(solution)/shard_map/ppermute | solution.py:533
  90.1 2.8 %shard_map.163.activated_ref = bf16[512,384]{1,0:T(8,128)(2,1)S(1)} custom-call(bf16[512,384]{1,0:T(8,128)(2,1)S(1)} %get-tuple-element.38.gated_ref, f32[31,384]{1,0:T(8,128)S(1)} %copy-done.4, f32[2,384]{1,0:T(2,128)S(1)} %pad_maximum_fusion.bn_ref), custom_call_target="tpu_custom_call" | custom-call | flops 1000 | bytes 1000 | tf_op jit(solution)/shard_map/pallas_call | solution.py:38
  92.9 1.5 %collective-permute-done.24.right_ref = bf16[16,384]{1,0:T(8,128)(2,1)S(1)} collective-permute-done((bf16[16,384]{1,0:T(8,128)(2,1)S(1)}, bf16[16,384]{1,0:T(8,128)(2,1)S(1)}, u32[]{:S(2)}, u32[]{:S(2)}) %collective-permute-start.24) | collective-permute-done | bytes 12320 | tf_op jit(solution)/shard_map/ppermute | solution.py:533
  94.3 1.1 shard_map.164
  95.5 2.3 %collective-permute-done.25 = bf16[512,768]{1,0:T(8,128)(2,1)S(1)} collective-permute-done((bf16[512,768]{1,0:T(8,128)(2,1)S(1)}, bf16[512,768]{1,0:T(8,128)(2,1)S(1)}, u32[]{:S(2)}, u32[]{:S(2)}) %collective-permute-start.25) | collective-permute-done | bytes 786464 | tf_op jit(solution)/shard_map/ppermute | solution.py:26
  97.7 0.2 convert_add_fusion
  98.0 0.6 collective-permute-start.26
  98.6 10.6 %collective-permute-done.26 = bf16[512,384]{1,0:T(8,128)(2,1)S(1)} collective-permute-done((bf16[512,384]{1,0:T(8,128)(2,1)S(1)}, bf16[512,384]{1,0:T(8,128)(2,1)S(1)}, u32[]{:S(2)}, u32[]{:S(2)}) %collective-permute-start.26) | collective-permute-done | bytes 393248 | tf_op jit(solution)/shard_map/ppermute | solution.py:26
  109.2 0.9 fusion.1
  (47 shorter events, 0.2 us)
Async XLA Ops:
  0.0 16.4 %collective-permute-start = (bf16[512,384]{1,0:T(8,128)(2,1)}, bf16[512,384]{1,0:T(8,128)(2,1)}, u32[]{:S(2)}, u32[]{:S(2)}) collective-permute-start(bf16[512,384]{1,0:T(8,128)(2,1)} %refs_4_.1), channel_id=1, source_target_pairs={{0,2},{1,3},{2,0},{3,1},{4,6},{5,7},{6,4},{7,5},{8,10},{9,11},{10,... | collective-permute-start | bytes 1179656 | tf_op jit(solution)/shard_map/ppermute | solution.py:26
  2.9 20.3 %collective-permute-start.3 = (bf16[512,384]{1,0:T(8,128)(2,1)}, bf16[512,384]{1,0:T(8,128)(2,1)}, u32[]{:S(2)}, u32[]{:S(2)}) collective-permute-start(bf16[512,384]{1,0:T(8,128)(2,1)} %refs_4_.1), channel_id=1, source_target_pairs={{0,8},{4,12},{8,0},{12,4},{1,9},{5,13},{9,1},{13,5},{2,10},{6,14},... | collective-permute-start | bytes 1179656 | tf_op jit(solution)/shard_map/ppermute | solution.py:26
  5.5 18.3 %collective-permute-start.4 = (bf16[512,384]{1,0:T(8,128)(2,1)}, bf16[512,384]{1,0:T(8,128)(2,1)}, u32[]{:S(2)}, u32[]{:S(2)}) collective-permute-start(bf16[512,384]{1,0:T(8,128)(2,1)} %refs_4_.1), channel_id=1, source_target_pairs={{0,4},{4,0},{8,12},{12,8},{1,5},{5,1},{9,13},{13,9},{2,6},{6,2},{1... | collective-permute-start | bytes 1179656 | tf_op jit(solution)/shard_map/ppermute | solution.py:26
  7.1 19.3 %collective-permute-start.1 = (bf16[512,384]{1,0:T(8,128)(2,1)}, bf16[512,384]{1,0:T(8,128)(2,1)}, u32[]{:S(2)}, u32[]{:S(2)}) collective-permute-start(bf16[512,384]{1,0:T(8,128)(2,1)} %refs_4_.1), channel_id=1, source_target_pairs={{0,1},{1,0},{2,3},{3,2},{4,5},{5,4},{6,7},{7,6},{8,9},{9,8},{10,11... | collective-permute-start | bytes 1179656 | tf_op jit(solution)/shard_map/ppermute | solution.py:26
  13.4 3.0 %copy-start.2 = (f32[32,384]{1,0:T(8,128)}, f32[32,384]{1,0:T(8,128)S(1)}, u32[]{:S(2)}) copy-start(f32[32,384]{1,0:T(8,128)S(1)} %all_gather.3.gains_ref) | copy-start | bytes 147460
  16.4 10.0 %collective-permute-start.2 = (bf16[512,384]{1,0:T(8,128)(2,1)}, bf16[512,384]{1,0:T(8,128)(2,1)}, u32[]{:S(2)}, u32[]{:S(2)}) collective-permute-start(bf16[512,384]{1,0:T(8,128)(2,1)} %shard_map.147.refs_1_.refs_5_), channel_id=1, source_target_pairs={{0,1},{1,0},{2,3},{3,2},{4,5},{5,4},{6,7},{7,6},{8,9},{9,8},{10,11... | collective-permute-start | bytes 1179656 | tf_op jit(solution)/shard_map/ppermute | solution.py:26
  16.8 17.5 %collective-permute-start.5 = (bf16[512,384]{1,0:T(8,128)(2,1)}, bf16[512,384]{1,0:T(8,128)(2,1)}, u32[]{:S(2)}, u32[]{:S(2)}) collective-permute-start(bf16[512,384]{1,0:T(8,128)(2,1)} %shard_map.147.refs_1_.refs_5_), channel_id=1, source_target_pairs={{0,4},{4,0},{8,12},{12,8},{1,5},{5,1},{9,13},{13,9},{2,6},{6,2},{1... | collective-permute-start | bytes 1179656 | tf_op jit(solution)/shard_map/ppermute | solution.py:26
  18.6 7.8 %copy-start.1 = (bf16[512,384]{1,0:T(8,128)(2,1)S(1)}, bf16[512,384]{1,0:T(8,128)(2,1)}, u32[]{:S(2)}) copy-start(bf16[512,384]{1,0:T(8,128)(2,1)} %refs_4_.1) | copy-start | bytes 1179652
  23.3 14.1 %collective-permute-start.8 = (bf16[192,1536]{1,0:T(8,128)(2,1)S(1)}, bf16[192,1536]{1,0:T(8,128)(2,1)S(1)}, u32[]{:S(2)}, u32[]{:S(2)}) collective-permute-start(bf16[192,1536]{1,0:T(8,128)(2,1)S(1)} %shard_map.152), channel_id=1, source_target_pairs={{0,2},{1,3},{2,0},{3,1},{4,6},{5,7},{6,4},{7,5},{8,10},{9,11},{10,... | collective-permute-start | bytes 1769480 | tf_op jit(solution)/shard_map/ppermute | solution.py:26
  23.9 16.3 %collective-permute-start.9 = (bf16[512,384]{1,0:T(8,128)(2,1)}, bf16[512,384]{1,0:T(8,128)(2,1)S(1)}, u32[]{:S(2)}, u32[]{:S(2)}) collective-permute-start(bf16[512,384]{1,0:T(8,128)(2,1)} %collective-permute-done.3.refs_6_.refs_2_), channel_id=1, source_target_pairs={{0,4},{4,0},{8,12},{12,8},{1,5},{5,1},{9,13},{13,9},{2,6},{6,2},{1... | collective-permute-start | bytes 1179656 | tf_op jit(solution)/shard_map/ppermute | solution.py:26
  26.4 13.8 %collective-permute-start.6 = (bf16[512,384]{1,0:T(8,128)(2,1)}, bf16[512,384]{1,0:T(8,128)(2,1)S(1)}, u32[]{:S(2)}, u32[]{:S(2)}) collective-permute-start(bf16[512,384]{1,0:T(8,128)(2,1)} %collective-permute-done.4.refs_7_.refs_2_), channel_id=1, source_target_pairs={{0,1},{1,0},{2,3},{3,2},{4,5},{5,4},{6,7},{7,6},{8,9},{9,8},{10,11... | collective-permute-start | bytes 1179656 | tf_op jit(solution)/shard_map/ppermute | solution.py:26
  34.3 5.9 %collective-permute-start.7 = (bf16[512,384]{1,0:T(8,128)(2,1)}, bf16[512,384]{1,0:T(8,128)(2,1)S(1)}, u32[]{:S(2)}, u32[]{:S(2)}) collective-permute-start(bf16[512,384]{1,0:T(8,128)(2,1)} %shard_map.150.refs_3_), channel_id=1, source_target_pairs={{0,1},{1,0},{2,3},{3,2},{4,5},{5,4},{6,7},{7,6},{8,9},{9,8},{10,11... | collective-permute-start | bytes 1179656 | tf_op jit(solution)/shard_map/ppermute | solution.py:26
  34.9 12.5 %collective-permute-start.10 = (bf16[512,384]{1,0:T(8,128)(2,1)}, bf16[512,384]{1,0:T(8,128)(2,1)S(1)}, u32[]{:S(2)}, u32[]{:S(2)}) collective-permute-start(bf16[512,384]{1,0:T(8,128)(2,1)} %collective-permute-done.3.refs_6_.refs_2_), channel_id=1, source_target_pairs={{0,2},{1,3},{2,0},{3,1},{4,6},{5,7},{6,4},{7,5},{8,10},{9,11},{10,... | collective-permute-start | bytes 1179656 | tf_op jit(solution)/shard_map/ppermute | solution.py:26
  37.4 13.2 %collective-permute-start.13 = (bf16[192,1536]{1,0:T(8,128)(2,1)S(1)}, bf16[192,1536]{1,0:T(8,128)(2,1)S(1)}, u32[]{:S(2)}, u32[]{:S(2)}) collective-permute-start(bf16[192,1536]{1,0:T(8,128)(2,1)S(1)} %shard_map.153.refs_8_.refs_9_), channel_id=1, source_target_pairs={{0,16},{16,0},{1,17},{17,1},{2,18},{18,2},{3,19},{19,3},{4,20},{20... | collective-permute-start | bytes 1769480 | tf_op jit(solution)/shard_map/ppermute | solution.py:26
  40.2 8.3 %collective-permute-start.11 = (bf16[512,384]{1,0:T(8,128)(2,1)}, bf16[512,384]{1,0:T(8,128)(2,1)S(1)}, u32[]{:S(2)}, u32[]{:S(2)}) collective-permute-start(bf16[512,384]{1,0:T(8,128)(2,1)} %collective-permute-done.3.refs_6_.refs_2_), channel_id=1, source_target_pairs={{0,1},{1,0},{2,3},{3,2},{4,5},{5,4},{6,7},{7,6},{8,9},{9,8},{10,11... | collective-permute-start | bytes 1179656 | tf_op jit(solution)/shard_map/ppermute | solution.py:26
  47.4 1.9 %collective-permute-start.12 = (bf16[512,384]{1,0:T(8,128)(2,1)S(1)}, bf16[512,384]{1,0:T(8,128)(2,1)S(1)}, u32[]{:S(2)}, u32[]{:S(2)}) collective-permute-start(bf16[512,384]{1,0:T(8,128)(2,1)S(1)} %shard_map.155.refs_3_), channel_id=1, source_target_pairs={{0,1},{1,0},{2,3},{3,2},{4,5},{5,4},{6,7},{7,6},{8,9},{9,8},{10,11... | collective-permute-start | bytes 1179656 | tf_op jit(solution)/shard_map/ppermute | solution.py:26
  48.0 11.1 %collective-permute-start.14 = (bf16[512,384]{1,0:T(8,128)(2,1)S(1)}, bf16[512,384]{1,0:T(8,128)(2,1)S(1)}, u32[]{:S(2)}, u32[]{:S(2)}) collective-permute-start(bf16[512,384]{1,0:T(8,128)(2,1)S(1)} %collective-permute-done.9.refs_9_.refs_2_), channel_id=1, source_target_pairs={{0,2},{1,3},{2,0},{3,1},{4,6},{5,7},{6,4},{7,5},{8,10},{9,11},{10,... | collective-permute-start | bytes 1179656 | tf_op jit(solution)/shard_map/ppermute | solution.py:26
  48.5 11.1 %collective-permute-start.15 = (bf16[512,384]{1,0:T(8,128)(2,1)S(1)}, bf16[512,384]{1,0:T(8,128)(2,1)S(1)}, u32[]{:S(2)}, u32[]{:S(2)}) collective-permute-start(bf16[512,384]{1,0:T(8,128)(2,1)S(1)} %collective-permute-done.9.refs_9_.refs_2_), channel_id=1, source_target_pairs={{0,1},{1,0},{2,3},{3,2},{4,5},{5,4},{6,7},{7,6},{8,9},{9,8},{10,11... | collective-permute-start | bytes 1179656 | tf_op jit(solution)/shard_map/ppermute | solution.py:26
  50.6 8.5 %copy-start = (bf16[384,1536]{1,0:T(8,128)(2,1)S(1)}, bf16[384,1536]{1,0:T(8,128)(2,1)}, u32[]{:S(2)}) copy-start(bf16[384,1536]{1,0:T(8,128)(2,1)} %refs_8_.1) | copy-start | bytes 3538948
  59.1 1.7 %collective-permute-start.16 = (bf16[512,384]{1,0:T(8,128)(2,1)S(1)}, bf16[512,384]{1,0:T(8,128)(2,1)S(1)}, u32[]{:S(2)}, u32[]{:S(2)}) collective-permute-start(bf16[512,384]{1,0:T(8,128)(2,1)S(1)} %shard_map.157.refs_3_), channel_id=1, source_target_pairs={{0,1},{1,0},{2,3},{3,2},{4,5},{5,4},{6,7},{7,6},{8,9},{9,8},{10,11... | collective-permute-start | bytes 1179656 | tf_op jit(solution)/shard_map/ppermute | solution.py:26
  59.1 18.7 %collective-permute-start.20 = (bf16[384,1536]{1,0:T(8,128)(2,1)S(1)}, bf16[384,1536]{1,0:T(8,128)(2,1)S(1)}, u32[]{:S(2)}, u32[]{:S(2)}) collective-permute-start(bf16[384,1536]{1,0:T(8,128)(2,1)S(1)} %copy-done), channel_id=1, source_target_pairs={{0,1},{1,0},{2,3},{3,2},{4,5},{5,4},{6,7},{7,6},{8,9},{9,8},{10,11... | collective-permute-start | bytes 3538952 | tf_op jit(solution)/shard_map/ppermute | solution.py:26
  66.5 2.4 %copy-start.3 = (f32[32,384]{1,0:T(8,128)S(1)}, f32[32,384]{1,0:T(8,128)}, u32[]{:S(2)}) copy-start(f32[32,384]{1,0:T(8,128)} %copy-done.2) | copy-start | bytes 147460
  66.5 11.2 %collective-permute-start.17 = (bf16[512,384]{1,0:T(8,128)(2,1)S(1)}, bf16[512,384]{1,0:T(8,128)(2,1)S(1)}, u32[]{:S(2)}, u32[]{:S(2)}) collective-permute-start(bf16[512,384]{1,0:T(8,128)(2,1)S(1)} %shard_map.158.refs_0_), channel_id=1, source_target_pairs={{0,2},{1,3},{2,0},{3,1},{4,6},{5,7},{6,4},{7,5},{8,10},{9,11},{10,... | collective-permute-start | bytes 1179656 | tf_op jit(solution)/shard_map/ppermute | solution.py:26
  67.1 10.7 %collective-permute-start.21 = (bf16[192,1536]{1,0:T(8,128)(2,1)S(1)}, bf16[192,1536]{1,0:T(8,128)(2,1)S(1)}, u32[]{:S(2)}, u32[]{:S(2)}) collective-permute-start(bf16[192,1536]{1,0:T(8,128)(2,1)S(1)} %shard_map.153.refs_8_.refs_9_), channel_id=1, source_target_pairs={{0,1},{1,0},{2,3},{3,2},{4,5},{5,4},{6,7},{7,6},{8,9},{9,8},{10,11... | collective-permute-start | bytes 1769480 | tf_op jit(solution)/shard_map/ppermute | solution.py:26
  67.1 10.7 %collective-permute-start.22 = (bf16[192,1536]{1,0:T(8,128)(2,1)S(1)}, bf16[192,1536]{1,0:T(8,128)(2,1)S(1)}, u32[]{:S(2)}, u32[]{:S(2)}) collective-permute-start(bf16[192,1536]{1,0:T(8,128)(2,1)S(1)} %collective-permute-done.13.refs_8_.refs_10_), channel_id=1, source_target_pairs={{0,1},{1,0},{2,3},{3,2},{4,5},{5,4},{6,7},{7,6},{8,9},{9,8},{10,11... | collective-permute-start | bytes 1769480 | tf_op jit(solution)/shard_map/ppermute | solution.py:26
  71.3 6.4 %copy-start.5 = (f32[384]{0:T(512)S(1)}, f32[384]{0:T(512)}, u32[]{:S(2)}) copy-start(f32[384]{0:T(512)} %param.28) | copy-start | bytes 4612
  71.3 6.4 %copy-start.6 = (f32[384]{0:T(512)S(1)}, f32[384]{0:T(512)}, u32[]{:S(2)}) copy-start(f32[384]{0:T(512)} %param.27) | copy-start | bytes 4612
  71.3 6.5 %collective-permute-start.18 = (bf16[512,384]{1,0:T(8,128)(2,1)S(1)}, bf16[512,384]{1,0:T(8,128)(2,1)S(1)}, u32[]{:S(2)}, u32[]{:S(2)}) collective-permute-start(bf16[512,384]{1,0:T(8,128)(2,1)S(1)} %shard_map.158.refs_0_), channel_id=1, source_target_pairs={{0,1},{1,0},{2,3},{3,2},{4,5},{5,4},{6,7},{7,6},{8,9},{9,8},{10,11... | collective-permute-start | bytes 1179656 | tf_op jit(solution)/shard_map/ppermute | solution.py:26
  77.7 1.7 %collective-permute-start.19 = (bf16[512,384]{1,0:T(8,128)(2,1)S(1)}, bf16[512,384]{1,0:T(8,128)(2,1)S(1)}, u32[]{:S(2)}, u32[]{:S(2)}) collective-permute-start(bf16[512,384]{1,0:T(8,128)(2,1)S(1)} %shard_map.161.refs_1_), channel_id=1, source_target_pairs={{0,1},{1,0},{2,3},{3,2},{4,5},{5,4},{6,7},{7,6},{8,9},{9,8},{10,11... | collective-permute-start | bytes 1179656 | tf_op jit(solution)/shard_map/ppermute | solution.py:26
  79.5 10.6 %copy-start.4 = (f32[31,384]{1,0:T(8,128)S(1)}, f32[31,384]{1,0:T(8,128)}, u32[]{:S(2)}) copy-start(f32[31,384]{1,0:T(8,128)} %taps_ref.3) | copy-start | bytes 142852
  85.3 7.5 %collective-permute-start.23 = (bf16[16,384]{1,0:T(8,128)(2,1)S(1)}, bf16[16,384]{1,0:T(8,128)(2,1)S(1)}, u32[]{:S(2)}, u32[]{:S(2)}) collective-permute-start(bf16[16,384]{1,0:T(8,128)(2,1)S(1)} %get-tuple-element.39), channel_id=1, source_target_pairs={{0,4},{4,8},{8,12},{1,5},{5,9},{9,13},{2,6},{6,10},{10,14},{3,7},{... | collective-permute-start | bytes 36872 | tf_op jit(solution)/shard_map/ppermute | solution.py:532
  88.7 5.6 %collective-permute-start.24 = (bf16[16,384]{1,0:T(8,128)(2,1)S(1)}, bf16[16,384]{1,0:T(8,128)(2,1)S(1)}, u32[]{:S(2)}, u32[]{:S(2)}) collective-permute-start(bf16[16,384]{1,0:T(8,128)(2,1)S(1)} %get-tuple-element.40), channel_id=1, source_target_pairs={{4,0},{8,4},{12,8},{5,1},{9,5},{13,9},{6,2},{10,6},{14,10},{7,3},{... | collective-permute-start | bytes 36872 | tf_op jit(solution)/shard_map/ppermute | solution.py:533
  95.4 2.4 %collective-permute-start.25 = (bf16[512,768]{1,0:T(8,128)(2,1)S(1)}, bf16[512,768]{1,0:T(8,128)(2,1)S(1)}, u32[]{:S(2)}, u32[]{:S(2)}) collective-permute-start(bf16[512,768]{1,0:T(8,128)(2,1)S(1)} %get-tuple-element.42), channel_id=1, source_target_pairs={{0,1},{1,0},{2,3},{3,2},{4,5},{5,4},{6,7},{7,6},{8,9},{9,8},{10,11... | collective-permute-start | bytes 2359304 | tf_op jit(solution)/shard_map/ppermute | solution.py:26
  98.0 11.2 %collective-permute-start.26 = (bf16[512,384]{1,0:T(8,128)(2,1)S(1)}, bf16[512,384]{1,0:T(8,128)(2,1)S(1)}, u32[]{:S(2)}, u32[]{:S(2)}) collective-permute-start(bf16[512,384]{1,0:T(8,128)(2,1)S(1)} %slice.17), channel_id=1, source_target_pairs={{0,2},{1,3},{2,0},{3,1},{4,6},{5,7},{6,4},{7,5},{8,10},{9,11},{10,... | collective-permute-start | bytes 1179656 | tf_op jit(solution)/shard_map/ppermute | solution.py:26

commit v2 on v1

--- a/solution.py
+++ b/solution.py
@@ -178,21 +178,26 @@
     )
 
 
-def project_kernel(count, *refs):
-    blocks, (folded_ref, sums_ref), (query_ref, key_ref, value_ref) = refs[:count], refs[count : count + 2], refs[-3:]
+def project_kernel(count, first, *refs):
+    blocks, (folded_ref, sums_ref, *refs) = refs[:count], refs[count:]
+    key_ref, value_ref = refs[-2:]
+    query_ref = refs[-3] if first else None
     mean, scale = row_statistics(blocks)
     cells = jnp.concatenate([ref[...] for ref in blocks], axis=1)
     low = lane_masks()
     for j in range(key_ref.shape[1] // PAIR):
-        projected = norm_product(cells, mean, scale, folded_ref, sums_ref, j * 3 * PAIR, 3 * PAIR)
-        keys, low_values, high_values = keys_values(projected)
-        queries = projected[:, 2 * PAIR :] * SCORE_SCALE
+        columns = (3 if first else 2) * PAIR
+        projected = norm_product(cells, mean, scale, folded_ref, sums_ref, j * 3 * PAIR, columns)
         base = 2 * j * PAIR
-        key_ref[:, j * PAIR : (j + 1) * PAIR] = keys
-        value_ref[:, base : base + PAIR] = low_values
-        value_ref[:, base + PAIR : base + 2 * PAIR] = high_values
-        query_ref[:, base : base + PAIR] = jnp.where(low, queries, 0.0).astype(BF16)
-        query_ref[:, base + PAIR : base + 2 * PAIR] = jnp.where(low, 0.0, queries).astype(BF16)
+        (
+            key_ref[:, j * PAIR : (j + 1) * PAIR],
+            value_ref[:, base : base + PAIR],
+            value_ref[:, base + PAIR : base + 2 * PAIR],
+        ) = keys_values(projected)
+        if first:
+            queries = projected[:, 2 * PAIR :] * SCORE_SCALE
+            query_ref[:, base : base + PAIR] = jnp.where(low, queries, 0.0).astype(BF16)
+            query_ref[:, base + PAIR : base + 2 * PAIR] = jnp.where(low, 0.0, queries).astype(BF16)
 
 
 def attend_pair(pair, query_rows, query_ref, keys, values, state_ref):
@@ -223,36 +228,21 @@
     return total, peak
 
 
-def first_kernel(query_rows, query_ref, key_ref, value_ref, _, state_ref, token_ref):
-    token_ref[...] = jnp.zeros_like(token_ref)
-    for j in range(key_ref.shape[1] // PAIR):
-        values = [value_ref[:, n * PAIR : (n + 1) * PAIR] for n in (2 * j, 2 * j + 1)]
-        attend_pair(j, query_rows, query_ref, key_ref[:, j * PAIR : (j + 1) * PAIR], values, state_ref)
-
-
-def slot_kernel(count, last, query_rows, *refs):
-    query_ref, old_ref, *refs = refs
-    blocks, (folded_ref, sums_ref) = refs[:count], refs[count : count + 2]
-    part, key_ref, value_ref = refs[-3:]
+def attend_kernel(first, last, query_rows, query_ref, key_ref, value_ref, *refs):
     if last:
-        attended = refs[-4]
+        old_ref, attended, part = refs[0], refs[-2], refs[-1]
+    elif first:
+        part, token_ref = refs[-2:]
     else:
-        state_ref, token_ref = refs[-5:-3]
+        old_ref, (state_ref, token_ref, part) = refs[0], refs[-3:]
+    if not last:
         token_ref[...] = jnp.zeros_like(token_ref)
-    mean, scale = row_statistics(blocks)
-    cells = jnp.concatenate([ref[...] for ref in blocks], axis=1)
     pairs = query_ref.shape[1] // (2 * PAIR)
-    for j in range(pairs):
-        projected = norm_product(cells, mean, scale, folded_ref, sums_ref, j * 3 * PAIR, 2 * PAIR)
-        base = 2 * j * PAIR
-        (
-            key_ref[:, j * PAIR : (j + 1) * PAIR],
-            value_ref[:, base : base + PAIR],
-            value_ref[:, base + PAIR : base + 2 * PAIR],
-        ) = keys_values(projected)
     for j in range(pairs):
         values = [value_ref[:, n * PAIR : (n + 1) * PAIR] for n in (2 * j, 2 * j + 1)]
         attend_pair(j, query_rows, query_ref, key_ref[:, j * PAIR : (j + 1) * PAIR], values, part)
+    if first:
+        return
     total = query_ref.shape[0]
     low = lane_masks()
     for start in range(0, total, query_rows):
@@ -457,7 +447,7 @@
         )
     else:
         half = w_out
-    crossed = over_chips(after(half, *chips[0]))
+    crossed = over_chips(half)
     state_shape = ((frames, 4 * padded), F32)
     token_shape = ((8, 128), F32)
     wide, narrow = ((frames, 2 * padded), BF16), ((frames, padded), BF16)
@@ -465,49 +455,54 @@
     own = [frames_in] + chips[0]
     own_blocks = own + other_core(own)
     n = len(own_blocks)
-    early = [raw[s] for s in raw if s]
+    early = [*[raw[s] for s in raw if s], *crossed]
     queries, keys, values = kernel_call(
-        functools.partial(project_kernel, n),
+        functools.partial(project_kernel, n, True),
         [wide, narrow, wide],
         [*own_blocks, qkv, qkv_sums, *early],
         spaces={n + 2 + i: pl.ANY for i in range(len(early))},
     )
-
-    def prepare(s):
-        low = s & -s
-        if s != low:
-            raw[s] = exchange(raw[s ^ low], "ctx", low)
-        chips[s] = over_chips(raw[s])
-
-    for s in range(2, min(ctx, 4)):
-        prepare(s)
-    state, token = kernel_call(
-        functools.partial(first_kernel, query_rows),
-        [state_shape, token_shape],
-        [queries, keys, values, frames_in],
-        spaces={3: pl.ANY},
-    )
-    crossed = [after(block, token) for block in crossed]
     swapped = [exchange(block, "parts", 1) for block in crossed] if parts == 2 else []
     pieces = [w_out]
     for a, block in enumerate(crossed):
         pieces += [block, swapped[a]] if swapped else [block]
     pieces = pieces + other_core(pieces)
-    late = {1: [*crossed, *[raw[s] for s in (3,) if s < ctx]], 2: swapped}
+
+    def prepare(s):
+        if 2 <= s < ctx:
+            low = s & -s
+            if s != low:
+                raw[s] = after(exchange(raw[s ^ low], "ctx", low), token)
+            chips[s] = over_chips(raw[s])
+
+    prepare(2)
+    state, token = kernel_call(
+        functools.partial(attend_kernel, True, False, query_rows),
+        [state_shape, token_shape],
+        [queries, keys, values],
+    )
+    moved = {1: [after(block, keys) for block in chips[1]]}
     for s in range(1, ctx):
         last = s == ctx - 1
-        if s + 2 < ctx and s + 2 not in chips:
-            prepare(s + 2)
-        mine = [raw[s]] + [after(block, token) for block in chips[s]]
-        operands = [queries, state, *mine, *other_core(mine), qkv, qkv_sums]
-        behind = late.get(s, [])
+        prepare(s + 2)
+        if not last:
+            moved[s + 1] = [after(block, token) for block in chips[s + 1]]
+        mine = [raw[s]] + moved[s]
+        keys, values = kernel_call(
+            functools.partial(project_kernel, n, False),
+            [narrow, wide],
+            [*mine, *other_core(mine), qkv, qkv_sums],
+        )
+        behind = [raw[s + 2]] if s + 2 < ctx else swapped
+        if s > 1 and not last:
+            behind = behind + moved[s + 1]
         results = kernel_call(
-            functools.partial(slot_kernel, n, last, query_rows),
+            functools.partial(attend_kernel, False, last, query_rows),
             [narrow] if last else [state_shape, token_shape],
-            operands + behind,
-            spaces={len(operands) + i: pl.ANY for i in range(len(behind))},
-            aliases={} if last else {1: 0},
-            scratch=[pltpu.VMEM(*shape) for shape in (state_shape, narrow, wide)],
+            [queries, keys, values, state, *behind],
+            spaces={4 + i: pl.ANY for i in range(len(behind))},
+            aliases={} if last else {3: 0},
+            scratch=[pltpu.VMEM(*state_shape)],
         )
         if last:
             (attended,) = results

time: 110 us -> 120 us (1.091)
  blocking collectives: 5.48 us -> 16.5 us
  Pallas kernels: 46 us -> 42.7 us
  waiting for transfers between devices: 34 us -> 36.2 us
    all_gather x1, blocking collectives: 5.48 us -> 16.5 us  [on_device(): gains = lax.all_gather(gains, 'grid', axis=0, tiled=True)]
    pallas_call x13 -> x16, Pallas kernels: 46 us -> 42.7 us  [kernel_call(): pl.pallas_call(body, in_specs=in_specs, out_specs=tuple((pl.BlockSpec(mem...]
    ppermute x25, waiting for transfers between devices: 32.6 us -> 34.8 us  [exchange(): return lax.ppermute(cells, axis, [(i, i ^ distance) for i in range(count)])]
  transfers between devices with their start and end apart: 27 -> 27, of which waited for: 13 -> 9; matrix products, arithmetic and copies ran while one was open for 0% -> 0% of each run, Pallas kernels for 35% -> 31%
where the time goes in v2:
time: 120 us; the launch traced here: 119 us
  Pallas kernels  42.7 us (36%)
  waiting for transfers between devices  36.2 us (30%)
  starting transfers between devices  22.5 us (19%)
  blocking collectives  16.5 us (14%)
    pallas_call x16, Pallas kernels, kernel_call(): pl.pallas_call(body, in_specs=in_specs, out_specs=tuple((pl.BlockSpec(mem...  42.7 us
    ppermute x25, waiting for transfers between devices, exchange(): return lax.ppermute(cells, axis, [(i, i ^ distance) for i in range(count)])  34.8 us
    ppermute x25, starting transfers between devices, exchange(): return lax.ppermute(cells, axis, [(i, i ^ distance) for i in range(count)])  17.7 us
    all_gather x1, blocking collectives, on_device(): gains = lax.all_gather(gains, 'grid', axis=0, tiled=True)  16.5 us
    ppermute x1, starting transfers between devices, on_device(): left = lax.ppermute(tail, 'ctx', [(i, i + 1) for i in range(ctx - 1)])  3.47 us
  transfers between devices with their start and end apart: 27, of which 9 were waited for; matrix products, arithmetic and copies ran while one was open for 0% of the time, Pallas kernels for 31%

profile of v2, /device:TPU:0, one launch (start us, length us, event | category | flops | bytes accessed | tf_op | source)
XLA Modules:
  0.0 119.4 jit_solution(3142739984433621121)
XLA Ops:
  0.0 2.9 %collective-permute-start = (bf16[512,384]{1,0:T(8,128)(2,1)}, bf16[512,384]{1,0:T(8,128)(2,1)S(1)}, u32[]{:S(2)}, u32[]{:S(2)}) collective-permute-start(bf16[512,384]{1,0:T(8,128)(2,1)} %refs_4_.1), channel_id=1, source_target_pairs={{0,2},{1,3},{2,0},{3,1},{4,6},{5,7},{6,4},{7,5},{8,10},{9,11},{10,... | collective-permute-start | bytes 1179656 | tf_op jit(solution)/shard_map/ppermute | solution.py:26
  2.9 2.6 %collective-permute-start.3 = (bf16[512,384]{1,0:T(8,128)(2,1)}, bf16[512,384]{1,0:T(8,128)(2,1)S(1)}, u32[]{:S(2)}, u32[]{:S(2)}) collective-permute-start(bf16[512,384]{1,0:T(8,128)(2,1)} %refs_4_.1), channel_id=1, source_target_pairs={{0,8},{4,12},{8,0},{12,4},{1,9},{5,13},{9,1},{13,5},{2,10},{6,14},... | collective-permute-start | bytes 1179656 | tf_op jit(solution)/shard_map/ppermute | solution.py:26
  5.5 1.1 shard_map.148
  6.6 0.6 collective-permute-start.5
  7.2 1.6 %collective-permute-start.4 = (bf16[512,384]{1,0:T(8,128)(2,1)S(1)}, bf16[512,384]{1,0:T(8,128)(2,1)S(1)}, u32[]{:S(2)}, u32[]{:S(2)}) collective-permute-start(bf16[512,384]{1,0:T(8,128)(2,1)S(1)} %copy-done.1), channel_id=1, source_target_pairs={{0,4},{4,0},{8,12},{12,8},{1,5},{5,1},{9,13},{13,9},{2,6},{6,2},{1... | collective-permute-start | bytes 1179656 | tf_op jit(solution)/shard_map/ppermute | solution.py:26
  8.8 0.8 shard_map.145
  9.6 16.5 %all_gather.3.gains_ref = f32[32,384]{1,0:T(8,128)S(1)} all-gather(f32[8,384]{1,0:T(8,128)S(1)} %shard_map.145), channel_id=1, replica_groups=mesh['parts'=2,'ctx'=4,'grid'=4] {'grid'}, dimensions={0}, use_global_device_ids=true | all-gather | bytes 61440 | tf_op jit(solution)/shard_map/all_gather | solution.py:412
  26.1 3.0 %shard_map.146 = (bf16[1536,1152]{1,0:T(8,128)(2,1)S(1)}, f32[2,1152]{1,0:T(2,128)S(1)}) custom-call(s32[1]{0:T(128)} %bitcast.me_ref, f32[32,384]{1,0:T(8,128)S(1)} %all_gather.3.gains_ref, bf16[1536,384]{1,0:T(8,128)(2,1)} %refs_0_.5, bf16[1536,384]{1,0:T(8,128)(2,1)} %refs_1_.4, bf16[1536,384]{1,0:T(8,128)(2,1)} %refs_2_.3), custom_call_target="tpu_custom_call" | custom-call | flops 1000 | bytes 1000 | tf_op jit(solution)/shard_map/pallas_call | solution.py:38
  29.1 0.4 collective-permute-start.2
  29.5 1.8 %collective-permute-start.8 = (bf16[512,384]{1,0:T(8,128)(2,1)S(1)}, bf16[512,384]{1,0:T(8,128)(2,1)S(1)}, u32[]{:S(2)}, u32[]{:S(2)}) collective-permute-start(bf16[512,384]{1,0:T(8,128)(2,1)S(1)} %shard_map.147.refs_1_.refs_5_), channel_id=1, source_target_pairs={{0,4},{4,0},{8,12},{12,8},{1,5},{5,1},{9,13},{13,9},{2,6},{6,2},{1... | collective-permute-start | bytes 1179656 | tf_op jit(solution)/shard_map/ppermute | solution.py:26
  31.2 0.3 collective-permute-start.6
  31.5 1.7 %collective-permute-start.13 = (bf16[512,384]{1,0:T(8,128)(2,1)S(1)}, bf16[512,384]{1,0:T(8,128)(2,1)S(1)}, u32[]{:S(2)}, u32[]{:S(2)}) collective-permute-start(bf16[512,384]{1,0:T(8,128)(2,1)S(1)} %collective-permute-done.3.refs_6_.refs_0_), channel_id=1, source_target_pairs={{0,2},{1,3},{2,0},{3,1},{4,6},{5,7},{6,4},{7,5},{8,10},{9,11},{10,... | collective-permute-start | bytes 1179656 | tf_op jit(solution)/shard_map/ppermute | solution.py:26
  33.2 3.0 %shard_map.149 = (bf16[512,768]{1,0:T(8,128)(2,1)S(1)}, bf16[512,384]{1,0:T(8,128)(2,1)S(1)}, bf16[512,768]{1,0:T(8,128)(2,1)S(1)}) custom-call(bf16[512,384]{1,0:T(8,128)(2,1)S(1)} %copy-done.1, bf16[512,384]{1,0:T(8,128)(2,1)S(1)} %shard_map.147.refs_1_.refs_5_, bf16[512,384]{1,0:T(8,128)(2,1)S(1)} %collective-permute-done.1.refs_2_.refs_6_, ...), custom_call_target="tpu_custom_call" | custom-call | flops 1000 | bytes 1000 | tf_op jit(solution)/shard_map/pallas_call | solution.py:38
  36.2 5.2 %collective-permute-done.8.refs_0_ = bf16[512,384]{1,0:T(8,128)(2,1)S(1)} collective-permute-done((bf16[512,384]{1,0:T(8,128)(2,1)S(1)}, bf16[512,384]{1,0:T(8,128)(2,1)S(1)}, u32[]{:S(2)}, u32[]{:S(2)}) %collective-permute-start.8) | collective-permute-done | bytes 393248 | tf_op jit(solution)/shard_map/ppermute | solution.py:26
  41.4 3.8 %shard_map.150 = (f32[512,1536]{1,0:T(8,128)S(1)}, f32[8,128]{1,0:T(8,128)S(1)}) custom-call(bf16[512,768]{1,0:T(8,128)(2,1)S(1)} %get-tuple-element.31.query_ref, bf16[512,384]{1,0:T(8,128)(2,1)S(1)} %get-tuple-element.32.key_ref.refs_1_, bf16[512,768]{1,0:T(8,128)(2,1)S(1)} %get-tuple-element.33.value_ref), custom_call_target="tpu_custom_call" | custom-call | flops 1000 | bytes 1000 | tf_op jit(solution)/shard_map/pallas_call | solution.py:38
  45.2 3.9 %collective-permute-done.6.refs_0_ = bf16[512,384]{1,0:T(8,128)(2,1)S(1)} collective-permute-done((bf16[512,384]{1,0:T(8,128)(2,1)S(1)}, bf16[512,384]{1,0:T(8,128)(2,1)S(1)}, u32[]{:S(2)}, u32[]{:S(2)}) %collective-permute-start.6) | collective-permute-done | bytes 393248 | tf_op jit(solution)/shard_map/ppermute | solution.py:26
  49.1 1.7 %collective-permute-start.7 = (bf16[512,384]{1,0:T(8,128)(2,1)S(1)}, bf16[512,384]{1,0:T(8,128)(2,1)S(1)}, u32[]{:S(2)}, u32[]{:S(2)}) collective-permute-start(bf16[512,384]{1,0:T(8,128)(2,1)S(1)} %shard_map.151.refs_1_.refs_0_), channel_id=1, source_target_pairs={{0,2},{1,3},{2,0},{3,1},{4,6},{5,7},{6,4},{7,5},{8,10},{9,11},{10,... | collective-permute-start | bytes 1179656 | tf_op jit(solution)/shard_map/ppermute | solution.py:26
  50.8 1.5 %collective-permute-start.16 = (bf16[192,1536]{1,0:T(8,128)(2,1)S(1)}, bf16[192,1536]{1,0:T(8,128)(2,1)S(1)}, u32[]{:S(2)}, u32[]{:S(2)}) collective-permute-start(bf16[192,1536]{1,0:T(8,128)(2,1)S(1)} %collective-permute-done.5.refs_8_.refs_9_), channel_id=1, source_target_pairs={{0,16},{16,0},{1,17},{17,1},{2,18},{18,2},{3,19},{19,3},{4,20},{20... | collective-permute-start | bytes 1769480 | tf_op jit(solution)/shard_map/ppermute | solution.py:26
  52.3 0.2 collective-permute-start.11
  52.5 0.3 collective-permute-start.15
  52.8 1.9 %shard_map.153 = (bf16[512,384]{1,0:T(8,128)(2,1)S(1)}, bf16[512,768]{1,0:T(8,128)(2,1)S(1)}) custom-call(bf16[512,384]{1,0:T(8,128)(2,1)S(1)} %collective-permute-done.4.refs_7_.refs_0_, bf16[512,384]{1,0:T(8,128)(2,1)S(1)} %shard_map.152.refs_1_, bf16[512,384]{1,0:T(8,128)(2,1)S(1)} %collective-permute-done.9.refs_2_, ...), custom_call_target="tpu_custom_call" | custom-call | flops 1000 | bytes 1000 | tf_op jit(solution)/shard_map/pallas_call | solution.py:38
  54.7 4.4 %shard_map.154 = (f32[512,1536]{1,0:T(8,128)S(1)}, f32[8,128]{1,0:T(8,128)S(1)}) custom-call(bf16[512,768]{1,0:T(8,128)(2,1)S(1)} %get-tuple-element.31.query_ref, bf16[512,384]{1,0:T(8,128)(2,1)S(1)} %get-tuple-element.35.key_ref, bf16[512,768]{1,0:T(8,128)(2,1)S(1)} %get-tuple-element.36.value_ref, ...), custom_call_target="tpu_custom_call", output_to_operand_aliasing={{0}: (3, {})} | custom-call | flops 1000 | bytes 1000 | tf_op jit(solution)/shard_map/pallas_call | solution.py:38
  59.1 0.4 collective-permute-done.7.refs_0_
  59.5 0.5 collective-permute-start.20
  60.0 1.9 %shard_map.158 = (bf16[512,384]{1,0:T(8,128)(2,1)S(1)}, bf16[512,768]{1,0:T(8,128)(2,1)S(1)}) custom-call(bf16[512,384]{1,0:T(8,128)(2,1)S(1)} %collective-permute-done.3.refs_6_.refs_0_, bf16[512,384]{1,0:T(8,128)(2,1)S(1)} %shard_map.157.refs_1_, bf16[512,384]{1,0:T(8,128)(2,1)S(1)} %collective-permute-done.14.refs_2_, ...), custom_call_target="tpu_custom_call" | custom-call | flops 1000 | bytes 1000 | tf_op jit(solution)/shard_map/pallas_call | solution.py:38
  61.9 4.6 %collective-permute-done.16.refs_1_.refs_10_ = bf16[192,1536]{1,0:T(8,128)(2,1)S(1)} collective-permute-done((bf16[192,1536]{1,0:T(8,128)(2,1)S(1)}, bf16[192,1536]{1,0:T(8,128)(2,1)S(1)}, u32[]{:S(2)}, u32[]{:S(2)}) %collective-permute-start.16) | collective-permute-done | bytes 589856 | tf_op jit(solution)/shard_map/ppermute | solution.py:26
  66.5 4.7 %shard_map.159 = (f32[512,1536]{1,0:T(8,128)S(1)}, f32[8,128]{1,0:T(8,128)}) custom-call(bf16[512,768]{1,0:T(8,128)(2,1)S(1)} %get-tuple-element.31.query_ref, bf16[512,384]{1,0:T(8,128)(2,1)S(1)} %get-tuple-element.41.key_ref, bf16[512,768]{1,0:T(8,128)(2,1)S(1)} %get-tuple-element.42.value_ref, ...), custom_call_target="tpu_custom_call", output_to_operand_aliasing={{0}: (3, {})} | custom-call | flops 1000 | bytes 1000 | tf_op jit(solution)/shard_map/pallas_call | solution.py:38
  71.2 1.9 %shard_map.156 = (bf16[512,384]{1,0:T(8,128)(2,1)S(1)}, bf16[512,768]{1,0:T(8,128)(2,1)S(1)}) custom-call(bf16[512,384]{1,0:T(8,128)(2,1)S(1)} %shard_map.151.refs_1_.refs_0_, bf16[512,384]{1,0:T(8,128)(2,1)S(1)} %shard_map.155.refs_1_.refs_2_, bf16[512,384]{1,0:T(8,128)(2,1)S(1)} %collective-permute-done.11.refs_2_, ...), custom_call_target="tpu_custom_call" | custom-call | flops 1000 | bytes 1000 | tf_op jit(solution)/shard_map/pallas_call | solution.py:38
  73.1 4.3 %shard_map.160.refs_0_ = bf16[512,384]{1,0:T(8,128)(2,1)S(1)} custom-call(bf16[512,768]{1,0:T(8,128)(2,1)S(1)} %get-tuple-element.31.query_ref, bf16[512,384]{1,0:T(8,128)(2,1)S(1)} %get-tuple-element.39.key_ref, bf16[512,768]{1,0:T(8,128)(2,1)S(1)} %get-tuple-element.40.value_ref, f32[512,1536]{1,0:T(8,128)S(1)} %get-tuple-element.44.refs_0_, ...), custom_call_target="tpu_custom_call" | custom-call | flops 1000 | bytes 1000 | tf_op jit(solution)/shard_map/pallas_call | solution.py:38
  77.4 0.4 collective-permute-start.17
  77.8 0.5 collective-permute-start.22
  78.4 1.3 %shard_map.162.refs_2_.w_ref = bf16[384,1536]{1,0:T(8,128)(2,1)S(1)} custom-call(s32[1]{0:T(128)} %bitcast.me_ref, bf16[384,1536]{1,0:T(8,128)(2,1)} %source_ref.3), custom_call_target="tpu_custom_call" | custom-call | flops 1000 | bytes 1000 | tf_op jit(solution)/shard_map/pallas_call | solution.py:38
  79.6 2.4 %shard_map.161 = (bf16[1536,768]{1,0:T(8,128)(2,1)S(1)}, f32[2,768]{1,0:T(2,128)S(1)}) custom-call(s32[1]{0:T(128)} %bitcast.me_ref, f32[32,384]{1,0:T(8,128)S(1)} %all_gather.3.gains_ref, bf16[1536,384]{1,0:T(8,128)(2,1)} %refs_0_.7, bf16[1536,384]{1,0:T(8,128)(2,1)} %refs_1_.5), custom_call_target="tpu_custom_call" | custom-call | flops 1000 | bytes 1000 | tf_op jit(solution)/shard_map/pallas_call | solution.py:38
  82.1 0.1 collective-permute-start.18
  82.2 6.0 %collective-permute-done.17.refs_0_ = bf16[512,384]{1,0:T(8,128)(2,1)S(1)} collective-permute-done((bf16[512,384]{1,0:T(8,128)(2,1)S(1)}, bf16[512,384]{1,0:T(8,128)(2,1)S(1)}, u32[]{:S(2)}, u32[]{:S(2)}) %collective-permute-start.17) | collective-permute-done | bytes 393248 | tf_op jit(solution)/shard_map/ppermute | solution.py:26
  88.3 1.6 %collective-permute-done.19.refs_3_ = bf16[512,384]{1,0:T(8,128)(2,1)S(1)} collective-permute-done((bf16[512,384]{1,0:T(8,128)(2,1)S(1)}, bf16[512,384]{1,0:T(8,128)(2,1)S(1)}, u32[]{:S(2)}, u32[]{:S(2)}) %collective-permute-start.19) | collective-permute-done | bytes 393248 | tf_op jit(solution)/shard_map/ppermute | solution.py:26
  90.0 4.6 %shard_map.164 = (bf16[512,384]{1,0:T(8,128)(2,1)S(1)}, bf16[512,384]{1,0:T(8,128)(2,1)S(1)}, bf16[16,384]{1,0:T(8,128)(2,1)S(1)}, bf16[16,384]{1,0:T(8,128)(2,1)S(1)}) custom-call(s32[1]{0:T(128)} %bitcast.me_ref, s32[1]{0:T(128)} %bitcast.1.part_ref, bf16[512,384]{1,0:T(8,128)(2,1)S(1)} %shard_map.160.refs_0_, bf16[512,384]{1,0:T(8,128)(2,1)S(1)} %shard_map.163.refs_1_, ...), custom_call_target="tpu_custom_call" | custom-call | flops 1000 | bytes 1000 | tf_op jit(solution)/shard_map/pallas_call | solution.py:38
  94.6 3.5 %collective-permute-start.23 = (bf16[16,384]{1,0:T(8,128)(2,1)S(1)}, bf16[16,384]{1,0:T(8,128)(2,1)S(1)}, u32[]{:S(2)}, u32[]{:S(2)}) collective-permute-start(bf16[16,384]{1,0:T(8,128)(2,1)S(1)} %get-tuple-element.49), channel_id=1, source_target_pairs={{0,4},{4,8},{8,12},{1,5},{5,9},{9,13},{2,6},{6,10},{10,14},{3,7},{... | collective-permute-start | bytes 36872 | tf_op jit(solution)/shard_map/ppermute | solution.py:527
  98.0 1.3 %collective-permute-start.24 = (bf16[16,384]{1,0:T(8,128)(2,1)S(1)}, bf16[16,384]{1,0:T(8,128)(2,1)S(1)}, u32[]{:S(2)}, u32[]{:S(2)}) collective-permute-start(bf16[16,384]{1,0:T(8,128)(2,1)S(1)} %get-tuple-element.50), channel_id=1, source_target_pairs={{4,0},{8,4},{12,8},{5,1},{9,5},{13,9},{6,2},{10,6},{14,10},{7,3},{... | collective-permute-start | bytes 36872 | tf_op jit(solution)/shard_map/ppermute | solution.py:528
  99.4 2.8 %shard_map.165.activated_ref = bf16[512,384]{1,0:T(8,128)(2,1)S(1)} custom-call(bf16[512,384]{1,0:T(8,128)(2,1)S(1)} %get-tuple-element.48.gated_ref, f32[31,384]{1,0:T(8,128)S(1)} %copy-done.2, f32[2,384]{1,0:T(2,128)S(1)} %pad_maximum_fusion.bn_ref), custom_call_target="tpu_custom_call" | custom-call | flops 1000 | bytes 1000 | tf_op jit(solution)/shard_map/pallas_call | solution.py:38
  102.2 1.5 %collective-permute-done.24.right_ref = bf16[16,384]{1,0:T(8,128)(2,1)S(1)} collective-permute-done((bf16[16,384]{1,0:T(8,128)(2,1)S(1)}, bf16[16,384]{1,0:T(8,128)(2,1)S(1)}, u32[]{:S(2)}, u32[]{:S(2)}) %collective-permute-start.24) | collective-permute-done | bytes 12320 | tf_op jit(solution)/shard_map/ppermute | solution.py:528
  103.6 1.1 shard_map.166
  104.7 0.1 collective-permute-start.25
  104.8 2.3 %collective-permute-done.25 = bf16[512,768]{1,0:T(8,128)(2,1)S(1)} collective-permute-done((bf16[512,768]{1,0:T(8,128)(2,1)S(1)}, bf16[512,768]{1,0:T(8,128)(2,1)S(1)}, u32[]{:S(2)}, u32[]{:S(2)}) %collective-permute-start.25) | collective-permute-done | bytes 786464 | tf_op jit(solution)/shard_map/ppermute | solution.py:26
  107.1 0.2 convert_add_fusion
  107.3 0.6 collective-permute-start.26
  107.9 10.6 %collective-permute-done.26 = bf16[512,384]{1,0:T(8,128)(2,1)S(1)} collective-permute-done((bf16[512,384]{1,0:T(8,128)(2,1)S(1)}, bf16[512,384]{1,0:T(8,128)(2,1)S(1)}, u32[]{:S(2)}, u32[]{:S(2)}) %collective-permute-start.26) | collective-permute-done | bytes 393248 | tf_op jit(solution)/shard_map/ppermute | solution.py:26
  118.5 0.9 fusion.1
  (45 shorter events, 0.2 us)
Async XLA Ops:
  0.0 7.2 %copy-start.1 = (bf16[512,384]{1,0:T(8,128)(2,1)S(1)}, bf16[512,384]{1,0:T(8,128)(2,1)}, u32[]{:S(2)}) copy-start(bf16[512,384]{1,0:T(8,128)(2,1)} %refs_4_.1) | copy-start | bytes 1179652
  0.0 29.1 %collective-permute-start = (bf16[512,384]{1,0:T(8,128)(2,1)}, bf16[512,384]{1,0:T(8,128)(2,1)S(1)}, u32[]{:S(2)}, u32[]{:S(2)}) collective-permute-start(bf16[512,384]{1,0:T(8,128)(2,1)} %refs_4_.1), channel_id=1, source_target_pairs={{0,2},{1,3},{2,0},{3,1},{4,6},{5,7},{6,4},{7,5},{8,10},{9,11},{10,... | collective-permute-start | bytes 1179656 | tf_op jit(solution)/shard_map/ppermute | solution.py:26
  2.9 26.5 %collective-permute-start.1 = (bf16[512,384]{1,0:T(8,128)(2,1)}, bf16[512,384]{1,0:T(8,128)(2,1)S(1)}, u32[]{:S(2)}, u32[]{:S(2)}) collective-permute-start(bf16[512,384]{1,0:T(8,128)(2,1)} %refs_4_.1), channel_id=1, source_target_pairs={{0,1},{1,0},{2,3},{3,2},{4,5},{5,4},{6,7},{7,6},{8,9},{9,8},{10,11... | collective-permute-start | bytes 1179656 | tf_op jit(solution)/shard_map/ppermute | solution.py:26
  2.9 28.3 %collective-permute-start.3 = (bf16[512,384]{1,0:T(8,128)(2,1)}, bf16[512,384]{1,0:T(8,128)(2,1)S(1)}, u32[]{:S(2)}, u32[]{:S(2)}) collective-permute-start(bf16[512,384]{1,0:T(8,128)(2,1)} %refs_4_.1), channel_id=1, source_target_pairs={{0,8},{4,12},{8,0},{12,4},{1,9},{5,13},{9,1},{13,5},{2,10},{6,14},... | collective-permute-start | bytes 1179656 | tf_op jit(solution)/shard_map/ppermute | solution.py:26
  6.6 26.6 %collective-permute-start.5 = (bf16[192,1536]{1,0:T(8,128)(2,1)S(1)}, bf16[192,1536]{1,0:T(8,128)(2,1)S(1)}, u32[]{:S(2)}, u32[]{:S(2)}) collective-permute-start(bf16[192,1536]{1,0:T(8,128)(2,1)S(1)} %shard_map.148), channel_id=1, source_target_pairs={{0,2},{1,3},{2,0},{3,1},{4,6},{5,7},{6,4},{7,5},{8,10},{9,11},{10,... | collective-permute-start | bytes 1769480 | tf_op jit(solution)/shard_map/ppermute | solution.py:26
  7.2 24.3 %collective-permute-start.4 = (bf16[512,384]{1,0:T(8,128)(2,1)S(1)}, bf16[512,384]{1,0:T(8,128)(2,1)S(1)}, u32[]{:S(2)}, u32[]{:S(2)}) collective-permute-start(bf16[512,384]{1,0:T(8,128)(2,1)S(1)} %copy-done.1), channel_id=1, source_target_pairs={{0,4},{4,0},{8,12},{12,8},{1,5},{5,1},{9,13},{13,9},{2,6},{6,2},{1... | collective-permute-start | bytes 1179656 | tf_op jit(solution)/shard_map/ppermute | solution.py:26
  29.1 4.1 %collective-permute-start.2 = (bf16[512,384]{1,0:T(8,128)(2,1)S(1)}, bf16[512,384]{1,0:T(8,128)(2,1)S(1)}, u32[]{:S(2)}, u32[]{:S(2)}) collective-permute-start(bf16[512,384]{1,0:T(8,128)(2,1)S(1)} %shard_map.147.refs_1_.refs_5_), channel_id=1, source_target_pairs={{0,1},{1,0},{2,3},{3,2},{4,5},{5,4},{6,7},{7,6},{8,9},{9,8},{10,11... | collective-permute-start | bytes 1179656 | tf_op jit(solution)/shard_map/ppermute | solution.py:26
  29.5 12.0 %collective-permute-start.8 = (bf16[512,384]{1,0:T(8,128)(2,1)S(1)}, bf16[512,384]{1,0:T(8,128)(2,1)S(1)}, u32[]{:S(2)}, u32[]{:S(2)}) collective-permute-start(bf16[512,384]{1,0:T(8,128)(2,1)S(1)} %shard_map.147.refs_1_.refs_5_), channel_id=1, source_target_pairs={{0,4},{4,0},{8,12},{12,8},{1,5},{5,1},{9,13},{13,9},{2,6},{6,2},{1... | collective-permute-start | bytes 1179656 | tf_op jit(solution)/shard_map/ppermute | solution.py:26
  31.2 17.9 %collective-permute-start.6 = (bf16[512,384]{1,0:T(8,128)(2,1)S(1)}, bf16[512,384]{1,0:T(8,128)(2,1)S(1)}, u32[]{:S(2)}, u32[]{:S(2)}) collective-permute-start(bf16[512,384]{1,0:T(8,128)(2,1)S(1)} %collective-permute-done.3.refs_6_.refs_0_), channel_id=1, source_target_pairs={{0,4},{4,0},{8,12},{12,8},{1,5},{5,1},{9,13},{13,9},{2,6},{6,2},{1... | collective-permute-start | bytes 1179656 | tf_op jit(solution)/shard_map/ppermute | solution.py:26
  31.5 19.3 %collective-permute-start.13 = (bf16[512,384]{1,0:T(8,128)(2,1)S(1)}, bf16[512,384]{1,0:T(8,128)(2,1)S(1)}, u32[]{:S(2)}, u32[]{:S(2)}) collective-permute-start(bf16[512,384]{1,0:T(8,128)(2,1)S(1)} %collective-permute-done.3.refs_6_.refs_0_), channel_id=1, source_target_pairs={{0,2},{1,3},{2,0},{3,1},{4,6},{5,7},{6,4},{7,5},{8,10},{9,11},{10,... | collective-permute-start | bytes 1179656 | tf_op jit(solution)/shard_map/ppermute | solution.py:26
  33.2 19.1 %collective-permute-start.9 = (bf16[512,384]{1,0:T(8,128)(2,1)S(1)}, bf16[512,384]{1,0:T(8,128)(2,1)S(1)}, u32[]{:S(2)}, u32[]{:S(2)}) collective-permute-start(bf16[512,384]{1,0:T(8,128)(2,1)S(1)} %collective-permute-done.4.refs_7_.refs_0_), channel_id=1, source_target_pairs={{0,1},{1,0},{2,3},{3,2},{4,5},{5,4},{6,7},{7,6},{8,9},{9,8},{10,11... | collective-permute-start | bytes 1179656 | tf_op jit(solution)/shard_map/ppermute | solution.py:26
  41.4 11.1 %collective-permute-start.10 = (bf16[512,384]{1,0:T(8,128)(2,1)S(1)}, bf16[512,384]{1,0:T(8,128)(2,1)S(1)}, u32[]{:S(2)}, u32[]{:S(2)}) collective-permute-start(bf16[512,384]{1,0:T(8,128)(2,1)S(1)} %shard_map.152.refs_1_), channel_id=1, source_target_pairs={{0,1},{1,0},{2,3},{3,2},{4,5},{5,4},{6,7},{7,6},{8,9},{9,8},{10,11... | collective-permute-start | bytes 1179656 | tf_op jit(solution)/shard_map/ppermute | solution.py:26
  49.1 10.4 %collective-permute-start.7 = (bf16[512,384]{1,0:T(8,128)(2,1)S(1)}, bf16[512,384]{1,0:T(8,128)(2,1)S(1)}, u32[]{:S(2)}, u32[]{:S(2)}) collective-permute-start(bf16[512,384]{1,0:T(8,128)(2,1)S(1)} %shard_map.151.refs_1_.refs_0_), channel_id=1, source_target_pairs={{0,2},{1,3},{2,0},{3,1},{4,6},{5,7},{6,4},{7,5},{8,10},{9,11},{10,... | collective-permute-start | bytes 1179656 | tf_op jit(solution)/shard_map/ppermute | solution.py:26
  50.8 8.7 %collective-permute-start.14 = (bf16[512,384]{1,0:T(8,128)(2,1)S(1)}, bf16[512,384]{1,0:T(8,128)(2,1)S(1)}, u32[]{:S(2)}, u32[]{:S(2)}) collective-permute-start(bf16[512,384]{1,0:T(8,128)(2,1)S(1)} %collective-permute-done.3.refs_6_.refs_0_), channel_id=1, source_target_pairs={{0,1},{1,0},{2,3},{3,2},{4,5},{5,4},{6,7},{7,6},{8,9},{9,8},{10,11... | collective-permute-start | bytes 1179656 | tf_op jit(solution)/shard_map/ppermute | solution.py:26
  50.8 15.7 %collective-permute-start.16 = (bf16[192,1536]{1,0:T(8,128)(2,1)S(1)}, bf16[192,1536]{1,0:T(8,128)(2,1)S(1)}, u32[]{:S(2)}, u32[]{:S(2)}) collective-permute-start(bf16[192,1536]{1,0:T(8,128)(2,1)S(1)} %collective-permute-done.5.refs_8_.refs_9_), channel_id=1, source_target_pairs={{0,16},{16,0},{1,17},{17,1},{2,18},{18,2},{3,19},{19,3},{4,20},{20... | collective-permute-start | bytes 1769480 | tf_op jit(solution)/shard_map/ppermute | solution.py:26
  52.3 18.9 %collective-permute-start.11 = (bf16[512,384]{1,0:T(8,128)(2,1)S(1)}, bf16[512,384]{1,0:T(8,128)(2,1)S(1)}, u32[]{:S(2)}, u32[]{:S(2)}) collective-permute-start(bf16[512,384]{1,0:T(8,128)(2,1)S(1)} %shard_map.151.refs_1_.refs_0_), channel_id=1, source_target_pairs={{0,1},{1,0},{2,3},{3,2},{4,5},{5,4},{6,7},{7,6},{8,9},{9,8},{10,11... | collective-permute-start | bytes 1179656 | tf_op jit(solution)/shard_map/ppermute | solution.py:26
  52.5 7.5 %collective-permute-start.15 = (bf16[512,384]{1,0:T(8,128)(2,1)S(1)}, bf16[512,384]{1,0:T(8,128)(2,1)S(1)}, u32[]{:S(2)}, u32[]{:S(2)}) collective-permute-start(bf16[512,384]{1,0:T(8,128)(2,1)S(1)} %shard_map.157.refs_1_), channel_id=1, source_target_pairs={{0,1},{1,0},{2,3},{3,2},{4,5},{5,4},{6,7},{7,6},{8,9},{9,8},{10,11... | collective-permute-start | bytes 1179656 | tf_op jit(solution)/shard_map/ppermute | solution.py:26
  54.7 4.8 %copy-start = (bf16[384,1536]{1,0:T(8,128)(2,1)S(1)}, bf16[384,1536]{1,0:T(8,128)(2,1)}, u32[]{:S(2)}) copy-start(bf16[384,1536]{1,0:T(8,128)(2,1)} %refs_8_.1) | copy-start | bytes 3538948
  59.5 11.7 %collective-permute-start.12 = (bf16[512,384]{1,0:T(8,128)(2,1)S(1)}, bf16[512,384]{1,0:T(8,128)(2,1)S(1)}, u32[]{:S(2)}, u32[]{:S(2)}) collective-permute-start(bf16[512,384]{1,0:T(8,128)(2,1)S(1)} %shard_map.155.refs_1_.refs_2_), channel_id=1, source_target_pairs={{0,1},{1,0},{2,3},{3,2},{4,5},{5,4},{6,7},{7,6},{8,9},{9,8},{10,11... | collective-permute-start | bytes 1179656 | tf_op jit(solution)/shard_map/ppermute | solution.py:26
  59.5 28.7 %collective-permute-start.20 = (bf16[384,1536]{1,0:T(8,128)(2,1)S(1)}, bf16[384,1536]{1,0:T(8,128)(2,1)S(1)}, u32[]{:S(2)}, u32[]{:S(2)}) collective-permute-start(bf16[384,1536]{1,0:T(8,128)(2,1)S(1)} %copy-done), channel_id=1, source_target_pairs={{0,1},{1,0},{2,3},{3,2},{4,5},{5,4},{6,7},{7,6},{8,9},{9,8},{10,11... | collective-permute-start | bytes 3538952 | tf_op jit(solution)/shard_map/ppermute | solution.py:26
  77.4 10.8 %collective-permute-start.17 = (bf16[512,384]{1,0:T(8,128)(2,1)S(1)}, bf16[512,384]{1,0:T(8,128)(2,1)S(1)}, u32[]{:S(2)}, u32[]{:S(2)}) collective-permute-start(bf16[512,384]{1,0:T(8,128)(2,1)S(1)} %shard_map.160.refs_0_), channel_id=1, source_target_pairs={{0,2},{1,3},{2,0},{3,1},{4,6},{5,7},{6,4},{7,5},{8,10},{9,11},{10,... | collective-permute-start | bytes 1179656 | tf_op jit(solution)/shard_map/ppermute | solution.py:26
  77.8 10.4 %collective-permute-start.21 = (bf16[192,1536]{1,0:T(8,128)(2,1)S(1)}, bf16[192,1536]{1,0:T(8,128)(2,1)S(1)}, u32[]{:S(2)}, u32[]{:S(2)}) collective-permute-start(bf16[192,1536]{1,0:T(8,128)(2,1)S(1)} %collective-permute-done.5.refs_8_.refs_9_), channel_id=1, source_target_pairs={{0,1},{1,0},{2,3},{3,2},{4,5},{5,4},{6,7},{7,6},{8,9},{9,8},{10,11... | collective-permute-start | bytes 1769480 | tf_op jit(solution)/shard_map/ppermute | solution.py:26
  77.8 10.4 %collective-permute-start.22 = (bf16[192,1536]{1,0:T(8,128)(2,1)S(1)}, bf16[192,1536]{1,0:T(8,128)(2,1)S(1)}, u32[]{:S(2)}, u32[]{:S(2)}) collective-permute-start(bf16[192,1536]{1,0:T(8,128)(2,1)S(1)} %collective-permute-done.16.refs_1_.refs_10_), channel_id=1, source_target_pairs={{0,1},{1,0},{2,3},{3,2},{4,5},{5,4},{6,7},{7,6},{8,9},{9,8},{10,11... | collective-permute-start | bytes 1769480 | tf_op jit(solution)/shard_map/ppermute | solution.py:26
  82.1 6.2 %copy-start.3 = (f32[384]{0:T(512)S(1)}, f32[384]{0:T(512)}, u32[]{:S(2)}) copy-start(f32[384]{0:T(512)} %param.28) | copy-start | bytes 4612
  82.1 6.1 %copy-start.4 = (f32[384]{0:T(512)S(1)}, f32[384]{0:T(512)}, u32[]{:S(2)}) copy-start(f32[384]{0:T(512)} %param.27) | copy-start | bytes 4612
  82.1 6.2 %collective-permute-start.18 = (bf16[512,384]{1,0:T(8,128)(2,1)S(1)}, bf16[512,384]{1,0:T(8,128)(2,1)S(1)}, u32[]{:S(2)}, u32[]{:S(2)}) collective-permute-start(bf16[512,384]{1,0:T(8,128)(2,1)S(1)} %shard_map.160.refs_0_), channel_id=1, source_target_pairs={{0,1},{1,0},{2,3},{3,2},{4,5},{5,4},{6,7},{7,6},{8,9},{9,8},{10,11... | collective-permute-start | bytes 1179656 | tf_op jit(solution)/shard_map/ppermute | solution.py:26
  88.2 1.7 %collective-permute-start.19 = (bf16[512,384]{1,0:T(8,128)(2,1)S(1)}, bf16[512,384]{1,0:T(8,128)(2,1)S(1)}, u32[]{:S(2)}, u32[]{:S(2)}) collective-permute-start(bf16[512,384]{1,0:T(8,128)(2,1)S(1)} %shard_map.163.refs_1_), channel_id=1, source_target_pairs={{0,1},{1,0},{2,3},{3,2},{4,5},{5,4},{6,7},{7,6},{8,9},{9,8},{10,11... | collective-permute-start | bytes 1179656 | tf_op jit(solution)/shard_map/ppermute | solution.py:26
  90.0 9.4 %copy-start.2 = (f32[31,384]{1,0:T(8,128)S(1)}, f32[31,384]{1,0:T(8,128)}, u32[]{:S(2)}) copy-start(f32[31,384]{1,0:T(8,128)} %taps_ref.3) | copy-start | bytes 142852
  94.6 7.6 %collective-permute-start.23 = (bf16[16,384]{1,0:T(8,128)(2,1)S(1)}, bf16[16,384]{1,0:T(8,128)(2,1)S(1)}, u32[]{:S(2)}, u32[]{:S(2)}) collective-permute-start(bf16[16,384]{1,0:T(8,128)(2,1)S(1)} %get-tuple-element.49), channel_id=1, source_target_pairs={{0,4},{4,8},{8,12},{1,5},{5,9},{9,13},{2,6},{6,10},{10,14},{3,7},{... | collective-permute-start | bytes 36872 | tf_op jit(solution)/shard_map/ppermute | solution.py:527
  98.0 5.6 %collective-permute-start.24 = (bf16[16,384]{1,0:T(8,128)(2,1)S(1)}, bf16[16,384]{1,0:T(8,128)(2,1)S(1)}, u32[]{:S(2)}, u32[]{:S(2)}) collective-permute-start(bf16[16,384]{1,0:T(8,128)(2,1)S(1)} %get-tuple-element.50), channel_id=1, source_target_pairs={{4,0},{8,4},{12,8},{5,1},{9,5},{13,9},{6,2},{10,6},{14,10},{7,3},{... | collective-permute-start | bytes 36872 | tf_op jit(solution)/shard_map/ppermute | solution.py:528
  104.7 2.4 %collective-permute-start.25 = (bf16[512,768]{1,0:T(8,128)(2,1)S(1)}, bf16[512,768]{1,0:T(8,128)(2,1)S(1)}, u32[]{:S(2)}, u32[]{:S(2)}) collective-permute-start(bf16[512,768]{1,0:T(8,128)(2,1)S(1)} %get-tuple-element.52), channel_id=1, source_target_pairs={{0,1},{1,0},{2,3},{3,2},{4,5},{5,4},{6,7},{7,6},{8,9},{9,8},{10,11... | collective-permute-start | bytes 2359304 | tf_op jit(solution)/shard_map/ppermute | solution.py:26
  107.3 11.2 %collective-permute-start.26 = (bf16[512,384]{1,0:T(8,128)(2,1)S(1)}, bf16[512,384]{1,0:T(8,128)(2,1)S(1)}, u32[]{:S(2)}, u32[]{:S(2)}) collective-permute-start(bf16[512,384]{1,0:T(8,128)(2,1)S(1)} %slice.17), channel_id=1, source_target_pairs={{0,2},{1,3},{2,0},{3,1},{4,6},{5,7},{6,4},{7,5},{8,10},{9,11},{10,... | collective-permute-start | bytes 1179656 | tf_op jit(solution)/shard_map/ppermute | solution.py:26

commit v3 on v2

--- a/solution.py
+++ b/solution.py
@@ -200,13 +200,21 @@
             query_ref[:, base + PAIR : base + 2 * PAIR] = jnp.where(low, 0.0, queries).astype(BF16)
 
 
-def attend_pair(pair, query_rows, query_ref, keys, values, state_ref):
-    total = query_ref.shape[0]
-    for start in range(0, total, query_rows):
-        rows = slice(start, start + query_rows)
+def chunks_of(spans, rows):
+    pieces, local = [], 0
+    for start, size in spans:
+        step = math.gcd(size, rows)
+        for offset in range(0, size, step):
+            pieces.append((slice(start + offset, start + offset + step), slice(local, local + step)))
+            local += step
+    return pieces
+
+
+def attend_pair(pair, chunks, query_ref, keys, values, state_ref):
+    for source, rows in chunks:
         for head in range(2):
             index = 2 * pair + head
-            queries = query_ref[rows, index * PAIR : (index + 1) * PAIR]
+            queries = query_ref[source, index * PAIR : (index + 1) * PAIR]
             scores = lax.dot_general(
                 queries, keys, (((1,), (1,)), ((), ())), preferred_element_type=F32
             )
@@ -215,20 +223,20 @@
             sums = jnp.dot(soft, values[head], preferred_element_type=F32)
             state_ref[rows, 2 * index * PAIR : (2 * index + 1) * PAIR] = sums
             state_ref[rows, (2 * index + 1) * PAIR : (2 * index + 2) * PAIR] = jnp.broadcast_to(
-                peak, (query_rows, PAIR)
+                peak, (peak.shape[0], PAIR)
             )
 
 
-def merge_head(old_ref, part_ref, rows, index):
+def merge_head(old_ref, part_ref, source, rows, index):
     sums = slice(2 * index * PAIR, (2 * index + 1) * PAIR)
     peaks = slice((2 * index + 1) * PAIR, (2 * index + 2) * PAIR)
-    old_peak, part_peak = old_ref[rows, peaks], part_ref[rows, peaks]
+    old_peak, part_peak = old_ref[source, peaks], part_ref[rows, peaks]
     peak = jnp.maximum(old_peak, part_peak)
-    total = old_ref[rows, sums] * jnp.exp2(old_peak - peak) + part_ref[rows, sums] * jnp.exp2(part_peak - peak)
+    total = old_ref[source, sums] * jnp.exp2(old_peak - peak) + part_ref[rows, sums] * jnp.exp2(part_peak - peak)
     return total, peak
 
 
-def attend_kernel(first, last, query_rows, query_ref, key_ref, value_ref, *refs):
+def attend_kernel(first, last, chunks, query_ref, key_ref, value_ref, *refs):
     if last:
         old_ref, attended, part = refs[0], refs[-2], refs[-1]
     elif first:
@@ -240,15 +248,13 @@
     pairs = query_ref.shape[1] // (2 * PAIR)
     for j in range(pairs):
         values = [value_ref[:, n * PAIR : (n + 1) * PAIR] for n in (2 * j, 2 * j + 1)]
-        attend_pair(j, query_rows, query_ref, key_ref[:, j * PAIR : (j + 1) * PAIR], values, part)
+        attend_pair(j, chunks, query_ref, key_ref[:, j * PAIR : (j + 1) * PAIR], values, part)
     if first:
         return
-    total = query_ref.shape[0]
     low = lane_masks()
-    for start in range(0, total, query_rows):
-        rows = slice(start, start + query_rows)
+    for source, rows in chunks:
         for j in range(pairs):
-            heads = [merge_head(old_ref, part, rows, 2 * j + head) for head in range(2)]
+            heads = [merge_head(old_ref, part, source, rows, 2 * j + head) for head in range(2)]
             if last:
                 (one, _), (two, _) = heads
                 both = jnp.where(low, one, two)
@@ -261,9 +267,10 @@
                     state_ref[rows, at + PAIR : at + 2 * PAIR] = peak
 
 
-def middle_kernel(count, order, me_ref, part_ref, *refs):
+def middle_kernel(count, order, spans, me_ref, part_ref, *refs):
     attended, frames_refs, refs = refs[:count], refs[count : 2 * count], refs[2 * count :]
     *pieces, folded_ref, sums_ref, own_ref, out_ref, head_ref, tail_ref, middle = refs
+    total = out_ref.shape[0]
     width = frames_refs[0].shape[1]
     cells = jnp.concatenate([ref[:, :width] for ref in attended], axis=1)
     swap = part_ref[0] != 0
@@ -289,9 +296,8 @@
         share = jnp.dot(cells, both, preferred_element_type=F32)
         for n in range(2):
             cols = slice((k + n) * width, (k + n + 1) * width)
-            middle[:, cols] = (
-                frames_refs[k + n][...].astype(F32) + share[:, n * width : (n + 1) * width]
-            ).astype(BF16)
+            own = jnp.concatenate([frames_refs[k + n][start : start + size, :] for start, size in spans], axis=0)
+            middle[:, cols] = (own.astype(F32) + share[:, n * width : (n + 1) * width]).astype(BF16)
     own_ref[...] = middle[:, :width]
     mean, scale = row_statistics((middle,))
     cells = middle[...]
@@ -300,7 +306,6 @@
         out_ref[:, j * PAIR : (j + 1) * PAIR] = (
             both[:, :PAIR] / (1.0 + jnp.exp(-both[:, PAIR:]))
         ).astype(BF16)
-    total = out_ref.shape[0]
     head_ref[...] = out_ref[:HALO, :]
     tail_ref[...] = out_ref[total - HALO :, :]
 
@@ -322,41 +327,42 @@
     return (value / (1.0 + jnp.exp(-value))).astype(BF16)
 
 
-def conv_inner_kernel(gated_ref, taps_ref, bn_ref, activated_ref, padded):
-    total, width = gated_ref.shape
-    piece = 32
-    padded[HALO : HALO + total, :] = gated_ref[...].astype(F32)
-    for col in range(0, width, PAIR):
-        cols = slice(col, col + PAIR)
-        taps = [taps_ref[j : j + 1, cols] for j in range(KERNEL)]
-        scale, shift = bn_ref[0:1, cols], bn_ref[1:2, cols]
-
-        def block(index, carry):
-            start = pl.multiple_of(HALO + index * piece, HALO)
-            activated_ref[pl.ds(start, piece), cols] = conv_rows(padded, start, piece, cols, taps, scale, shift)
-            return carry
-
-        lax.fori_loop(0, total // piece - 1, block, 0, unroll=3)
-
-
-def conv_outer_kernel(gated_ref, left_ref, right_ref, taps_ref, bn_ref, activated_ref, w_ref, keep_ref, send_ref, padded):
-    total, width = gated_ref.shape
+def conv_kernel(outer, first_ref, second_ref, *refs):
+    if outer:
+        left_ref, right_ref, *refs = refs
+    taps_ref, bn_ref, w_ref, keep_ref, send_ref, padded, activated = refs
+    total, width = first_ref.shape
     half = keep_ref.shape[1]
-    ends = []
-    for first, rows in (
-        (True, (left_ref[...], gated_ref[: 2 * HALO, :])),
-        (False, (gated_ref[total - 2 * HALO :, :], right_ref[...])),
-    ):
-        padded[...] = jnp.concatenate([part.astype(F32) for part in rows], axis=0)
-        parts = []
+    piece, quarter = 32, total // 2
+    if outer:
+        runs = (
+            (left_ref[...], first_ref[:quarter, :], second_ref[:HALO, :]),
+            (second_ref[total - HALO :, :], first_ref[quarter:, :], right_ref[...]),
+        )
+    else:
+        runs = ((first_ref[quarter - HALO : quarter, :], second_ref[...], first_ref[quarter : quarter + HALO, :]),)
+    at = 0
+    for before, rows, behind in runs:
+        count = rows.shape[0]
+        padded[0:HALO, :] = before.astype(F32)
+        padded[HALO : HALO + count, :] = rows.astype(F32)
+        padded[HALO + count : 2 * HALO + count, :] = behind.astype(F32)
         for col in range(0, width, PAIR):
             cols = slice(col, col + PAIR)
             taps = [taps_ref[j : j + 1, cols] for j in range(KERNEL)]
-            parts.append(conv_rows(padded, 0, HALO, cols, taps, bn_ref[0:1, cols], bn_ref[1:2, cols]))
-        ends.append(jnp.concatenate(parts, axis=1))
-    share = jnp.concatenate([ends[0], activated_ref[HALO : total - HALO, :], ends[1]], axis=0)
+            scale, shift = bn_ref[0:1, cols], bn_ref[1:2, cols]
+
+            def block(index, carry, at=at):
+                start = pl.multiple_of(index * piece, piece)
+                target = pl.multiple_of(at + index * piece, piece)
+                activated[pl.ds(target, piece), cols] = conv_rows(padded, start, piece, cols, taps, scale, shift)
+                return carry
+
+            lax.fori_loop(0, count // piece, block, 0, unroll=4)
+        at += count
+    share = activated[...]
+    send_ref[...] = jnp.dot(share, w_ref[:, half:], preferred_element_type=F32).astype(BF16)
     keep_ref[...] = jnp.dot(share, w_ref[:, :half], preferred_element_type=F32).astype(BF16)
-    send_ref[...] = jnp.dot(share, w_ref[:, half:], preferred_element_type=F32).astype(BF16)
 
 
 def pad_columns(weight, width):
@@ -388,7 +394,7 @@
     place = me.astype(jnp.int32).reshape(1)
     order = list(range(0, grid, CORES)) + list(range(1, grid, CORES))
     padded = -(-width // PAIR) * PAIR
-    query_rows = math.gcd(frames, 256)
+    query_rows, every = 256, ((0, frames),)
 
     def by_distance(cells):
         return jnp.concatenate(
@@ -447,7 +453,7 @@
         )
     else:
         half = w_out
-    crossed = over_chips(half)
+    crossed = over_chips(after(half, gains))
     state_shape = ((frames, 4 * padded), F32)
     token_shape = ((8, 128), F32)
     wide, narrow = ((frames, 2 * padded), BF16), ((frames, padded), BF16)
@@ -455,6 +461,7 @@
     own = [frames_in] + chips[0]
     own_blocks = own + other_core(own)
     n = len(own_blocks)
+    raw.update({s: after(block, glu_sums, w_p) for s, block in raw.items() if s > 1})
     early = [*[raw[s] for s in raw if s], *crossed]
     queries, keys, values = kernel_call(
         functools.partial(project_kernel, n, True),
@@ -477,7 +484,7 @@
 
     prepare(2)
     state, token = kernel_call(
-        functools.partial(attend_kernel, True, False, query_rows),
+        functools.partial(attend_kernel, True, False, chunks_of(every, query_rows)),
         [state_shape, token_shape],
         [queries, keys, values],
     )
@@ -493,57 +500,69 @@
             [narrow, wide],
             [*mine, *other_core(mine), qkv, qkv_sums],
         )
-        behind = [raw[s + 2]] if s + 2 < ctx else swapped
-        if s > 1 and not last:
+        if last:
+            break
+        behind = [raw[s + 2]] if s + 2 < ctx else []
+        if s > 1:
             behind = behind + moved[s + 1]
-        results = kernel_call(
-            functools.partial(attend_kernel, False, last, query_rows),
-            [narrow] if last else [state_shape, token_shape],
+        state, token = kernel_call(
+            functools.partial(attend_kernel, False, False, chunks_of(every, query_rows)),
+            [state_shape, token_shape],
             [queries, keys, values, state, *behind],
             spaces={4 + i: pl.ANY for i in range(len(behind))},
-            aliases={} if last else {3: 0},
+            aliases={3: 0},
             scratch=[pltpu.VMEM(*state_shape)],
         )
-        if last:
-            (attended,) = results
-        else:
-            state, token = results
-    attended = [attended] + [after(block, glu_sums, w_p) for block in over_chips(attended)]
-    attended = attended + other_core(attended)
+    rows, quarter = frames // 2, frames // 4
+    spans = (((0, quarter), (3 * quarter, quarter)), ((quarter, rows),))
+    attended = []
+    for h in range(2):
+        (mine,) = kernel_call(
+            functools.partial(attend_kernel, False, True, chunks_of(spans[h], query_rows)),
+            [((rows, padded), BF16)],
+            [queries, keys, values, state, *swapped],
+            spaces={4 + i: pl.ANY for i in range(len(swapped))},
+            scratch=[pltpu.VMEM((rows, 4 * padded), F32)],
+        )
+        attended.append([mine] + over_chips(mine))
     if width % PAIR:
         pieces = [by_distance(piece) for piece in pieces]
-    middle, gated, head, tail = kernel_call(
-        functools.partial(middle_kernel, n, order),
-        [
-            ((frames, width), BF16),
-            ((frames, padded), BF16),
-            ((HALO, padded), BF16),
-            ((HALO, padded), BF16),
-        ],
-        [place, part, *attended, *own_blocks, *pieces, glu, glu_sums],
-        spaces={0: pltpu.SMEM, 1: pltpu.SMEM},
-        scratch=[pltpu.VMEM((frames, grid * width), BF16)],
-    )
-    left = lax.ppermute(tail, "ctx", [(i, i + 1) for i in range(ctx - 1)])
-    right = lax.ppermute(head, "ctx", [(i + 1, i) for i in range(ctx - 1)])
-    (activated,) = kernel_call(
-        conv_inner_kernel,
-        [((frames, padded), BF16)],
-        [gated, taps, bn],
-        scratch=[pltpu.VMEM((frames + 2 * HALO, padded), F32)],
-    )
-    keep, send = kernel_call(
-        conv_outer_kernel,
-        [((frames, grid // CORES * width), BF16)] * 2,
-        [gated, left, right, taps, bn, activated, w_p],
-        scratch=[pltpu.VMEM((3 * HALO, padded), F32)],
-    )
-    pair_sum = keep.astype(F32) + exchange(send, "grid", 1).astype(F32)
-    result = middle.astype(F32) + pair_sum[:, :width]
-    for a in range(1, grid // CORES):
-        share = pair_sum[:, a * width : (a + 1) * width].astype(BF16)
-        result = result + exchange(share, "grid", CORES * a).astype(F32)
-    return result.astype(BF16)
+    middle, gated = [], []
+    for h in range(2):
+        mine = attended[h]
+        done = gated[0] if h else attended[1][0]
+        mine = mine[:1] + [after(block, done) for block in mine[1:]]
+        results = kernel_call(
+            functools.partial(middle_kernel, n, order, spans[h]),
+            [((rows, width), BF16), ((rows, padded), BF16), ((HALO, padded), BF16), ((HALO, padded), BF16)],
+            [place, part, *mine, *other_core(mine), *own_blocks, *pieces, glu, glu_sums],
+            spaces={0: pltpu.SMEM, 1: pltpu.SMEM},
+            scratch=[pltpu.VMEM((rows, grid * width), BF16)],
+        )
+        middle.append(results[0])
+        gated.append(results[1])
+        if h == 0:
+            left = lax.ppermute(results[3], "ctx", [(i, i + 1) for i in range(ctx - 1)])
+            right = lax.ppermute(results[2], "ctx", [(i + 1, i) for i in range(ctx - 1)])
+    outs = [None, None]
+    for h, around in ((1, []), (0, [left, right])):
+        keep, send = kernel_call(
+            functools.partial(conv_kernel, h == 0),
+            [((rows, grid // CORES * width), BF16)] * 2,
+            [*gated, *around, taps, bn, w_p],
+            scratch=[pltpu.VMEM((rows + 2 * HALO, padded), F32), pltpu.VMEM((rows, padded), BF16)],
+        )
+        theirs = exchange(send, "grid", 1)
+
+        def pair_sum(a):
+            cols = slice(a * width, (a + 1) * width)
+            return keep[:, cols].astype(F32) + theirs[:, cols].astype(F32)
+
+        result = middle[h].astype(F32) + pair_sum(0)
+        for a in range(1, grid // CORES):
+            result = result + exchange(pair_sum(a).astype(BF16), "grid", CORES * a).astype(F32)
+        outs[h] = result.astype(BF16)
+    return jnp.concatenate([outs[0][:quarter], outs[1], outs[0][quarter:]], axis=0)
 
 
 def solution(mesh):

time: 120 us -> 116 us (0.967)
  blocking collectives: 16.5 us -> 7.07 us
  starting transfers between devices: 22.5 us -> 25.1 us
  Pallas kernels: 42.7 us -> 44.9 us
    all_gather x1, blocking collectives: 16.5 us -> 7.07 us  [on_device(): gains = lax.all_gather(gains, 'grid', axis=0, tiled=True)]
    ppermute x25 -> x30, starting transfers between devices: 17.7 us -> 22.3 us  [exchange(): return lax.ppermute(cells, axis, [(i, i ^ distance) for i in range(count)])]
    pallas_call x16 -> x18, Pallas kernels: 42.7 us -> 44.9 us  [kernel_call(): pl.pallas_call(body, in_specs=in_specs, out_specs=tuple((pl.BlockSpec(mem...]
    ppermute x2, starting transfers between devices: 4.76 us -> 2.75 us  [the longest x1 1.46 us: on_device(): left = lax.ppermute(results[3], 'ctx', [(i, i + 1) for i in range(ctx - 1)])]
    ppermute x25 -> x30, waiting for transfers between devices: 34.8 us -> 35.1 us  [exchange(): return lax.ppermute(cells, axis, [(i, i ^ distance) for i in range(count)])]
  transfers between devices with their start and end apart: 27 -> 32, of which waited for: 9 -> 11; matrix products, arithmetic and copies ran while one was open for 0% -> 0% of each run, Pallas kernels for 31% -> 37%
where the time goes in v3:
time: 116 us; the launch traced here: 115 us
  Pallas kernels  44.9 us (39%)
  waiting for transfers between devices  36.9 us (32%)
  starting transfers between devices  25.1 us (22%)
  blocking collectives  7.07 us (6%)
    pallas_call x18, Pallas kernels, kernel_call(): pl.pallas_call(body, in_specs=in_specs, out_specs=tuple((pl.BlockSpec(mem...  44.9 us
    ppermute x30, waiting for transfers between devices, exchange(): return lax.ppermute(cells, axis, [(i, i ^ distance) for i in range(count)])  35.1 us
    ppermute x30, starting transfers between devices, exchange(): return lax.ppermute(cells, axis, [(i, i ^ distance) for i in range(count)])  22.3 us
    all_gather x1, blocking collectives, on_device(): gains = lax.all_gather(gains, 'grid', axis=0, tiled=True)  7.07 us
  transfers between devices with their start and end apart: 32, of which 11 were waited for; matrix products, arithmetic and copies ran while one was open for 0% of the time, Pallas kernels for 37%

profile of v3, /device:TPU:0, one launch (start us, length us, event | category | flops | bytes accessed | tf_op | source)
XLA Modules:
  0.0 115.4 jit_solution(12692989922174569335)
XLA Ops:
  0.0 2.9 %collective-permute-start = (bf16[512,384]{1,0:T(8,128)(2,1)}, bf16[512,384]{1,0:T(8,128)(2,1)S(1)}, u32[]{:S(2)}, u32[]{:S(2)}) collective-permute-start(bf16[512,384]{1,0:T(8,128)(2,1)} %refs_4_.3), channel_id=1, source_target_pairs={{0,2},{1,3},{2,0},{3,1},{4,6},{5,7},{6,4},{7,5},{8,10},{9,11},{10,... | collective-permute-start | bytes 1179656 | tf_op jit(solution)/shard_map/ppermute | solution.py:26
  2.9 2.6 %collective-permute-start.3 = (bf16[512,384]{1,0:T(8,128)(2,1)}, bf16[512,384]{1,0:T(8,128)(2,1)S(1)}, u32[]{:S(2)}, u32[]{:S(2)}) collective-permute-start(bf16[512,384]{1,0:T(8,128)(2,1)} %refs_4_.3), channel_id=1, source_target_pairs={{0,8},{4,12},{8,0},{12,4},{1,9},{5,13},{9,1},{13,5},{2,10},{6,14},... | collective-permute-start | bytes 1179656 | tf_op jit(solution)/shard_map/ppermute | solution.py:26
  5.5 0.8 shard_map.145
  6.3 7.1 %all_gather.3.gains_ref.refs_1_ = f32[32,384]{1,0:T(8,128)S(1)} all-gather(f32[8,384]{1,0:T(8,128)S(1)} %shard_map.145), channel_id=1, replica_groups=mesh['parts'=2,'ctx'=4,'grid'=4] {'grid'}, dimensions={0}, use_global_device_ids=true | all-gather | bytes 61440 | tf_op jit(solution)/shard_map/all_gather | solution.py:418
  13.4 1.1 shard_map.151.refs_0_
  14.5 1.8 %collective-permute-start.5 = (bf16[192,1536]{1,0:T(8,128)(2,1)S(1)}, bf16[192,1536]{1,0:T(8,128)(2,1)S(1)}, u32[]{:S(2)}, u32[]{:S(2)}) collective-permute-start(bf16[192,1536]{1,0:T(8,128)(2,1)S(1)} %shard_map.152), channel_id=1, source_target_pairs={{0,2},{1,3},{2,0},{3,1},{4,6},{5,7},{6,4},{7,5},{8,10},{9,11},{10,... | collective-permute-start | bytes 1769480 | tf_op jit(solution)/shard_map/ppermute | solution.py:26
  16.4 1.6 %collective-permute-start.4 = (bf16[512,384]{1,0:T(8,128)(2,1)S(1)}, bf16[512,384]{1,0:T(8,128)(2,1)S(1)}, u32[]{:S(2)}, u32[]{:S(2)}) collective-permute-start(bf16[512,384]{1,0:T(8,128)(2,1)S(1)} %copy-done.1), channel_id=1, source_target_pairs={{0,4},{4,0},{8,12},{12,8},{1,5},{5,1},{9,13},{13,9},{2,6},{6,2},{1... | collective-permute-start | bytes 1179656 | tf_op jit(solution)/shard_map/ppermute | solution.py:26
  18.0 3.0 %shard_map.146 = (bf16[1536,1152]{1,0:T(8,128)(2,1)S(1)}, f32[2,1152]{1,0:T(2,128)S(1)}) custom-call(s32[1]{0:T(128)} %bitcast.me_ref, f32[32,384]{1,0:T(8,128)S(1)} %all_gather.3.gains_ref.refs_1_, bf16[1536,384]{1,0:T(8,128)(2,1)} %refs_0_.6, bf16[1536,384]{1,0:T(8,128)(2,1)} %refs_1_.4, bf16[1536,384]{1,0:T(8,128)(2,1)} %refs_2_.4), custom_call_target="tpu_custom_call" | custom-call | flops 1000 | bytes 1000 | tf_op jit(solution)/shard_map/pallas_call | solution.py:38
  21.2 2.0 %collective-permute-done.3.refs_0_ = bf16[512,384]{1,0:T(8,128)(2,1)S(1)} collective-permute-done((bf16[512,384]{1,0:T(8,128)(2,1)}, bf16[512,384]{1,0:T(8,128)(2,1)S(1)}, u32[]{:S(2)}, u32[]{:S(2)}) %collective-permute-start.3) | collective-permute-done | bytes 393248 | tf_op jit(solution)/shard_map/ppermute | solution.py:26
  23.2 0.7 collective-permute-start.8
  23.9 1.3 %shard_map.149.refs_2_.refs_4_ = bf16[384,1536]{1,0:T(8,128)(2,1)S(1)} custom-call(s32[1]{0:T(128)} %bitcast.me_ref, bf16[384,1536]{1,0:T(8,128)(2,1)} %source_ref.2), custom_call_target="tpu_custom_call" | custom-call | flops 1000 | bytes 1000 | tf_op jit(solution)/shard_map/pallas_call | solution.py:38
  25.1 2.4 %shard_map.148 = (bf16[1536,768]{1,0:T(8,128)(2,1)S(1)}, f32[2,768]{1,0:T(2,128)S(1)}) custom-call(s32[1]{0:T(128)} %bitcast.me_ref, f32[32,384]{1,0:T(8,128)S(1)} %all_gather.3.gains_ref.refs_1_, bf16[1536,384]{1,0:T(8,128)(2,1)} %refs_0_.7, bf16[1536,384]{1,0:T(8,128)(2,1)} %refs_1_.5), custom_call_target="tpu_custom_call" | custom-call | flops 1000 | bytes 1000 | tf_op jit(solution)/shard_map/pallas_call | solution.py:38
  27.6 1.4 %collective-permute-start.6 = (bf16[512,384]{1,0:T(8,128)(2,1)S(1)}, bf16[512,384]{1,0:T(8,128)(2,1)S(1)}, u32[]{:S(2)}, u32[]{:S(2)}) collective-permute-start(bf16[512,384]{1,0:T(8,128)(2,1)S(1)} %shard_map.150.refs_6_.refs_0_), channel_id=1, source_target_pairs={{0,4},{4,0},{8,12},{12,8},{1,5},{5,1},{9,13},{13,9},{2,6},{6,2},{1... | collective-permute-start | bytes 1179656 | tf_op jit(solution)/shard_map/ppermute | solution.py:26
  29.0 2.5 %collective-permute-done.4.refs_7_.refs_0_ = bf16[512,384]{1,0:T(8,128)(2,1)S(1)} collective-permute-done((bf16[512,384]{1,0:T(8,128)(2,1)S(1)}, bf16[512,384]{1,0:T(8,128)(2,1)S(1)}, u32[]{:S(2)}, u32[]{:S(2)}) %collective-permute-start.4) | collective-permute-done | bytes 393248 | tf_op jit(solution)/shard_map/ppermute | solution.py:26
  31.6 0.5 collective-permute-start.13
  32.1 3.0 %shard_map.153 = (bf16[512,768]{1,0:T(8,128)(2,1)S(1)}, bf16[512,384]{1,0:T(8,128)(2,1)S(1)}, bf16[512,768]{1,0:T(8,128)(2,1)S(1)}) custom-call(bf16[512,384]{1,0:T(8,128)(2,1)S(1)} %copy-done.1, bf16[512,384]{1,0:T(8,128)(2,1)S(1)} %shard_map.147.refs_1_.refs_5_, bf16[512,384]{1,0:T(8,128)(2,1)S(1)} %collective-permute-done.1.refs_2_.refs_6_, ...), custom_call_target="tpu_custom_call" | custom-call | flops 1000 | bytes 1000 | tf_op jit(solution)/shard_map/pallas_call | solution.py:38
  35.1 4.9 %collective-permute-done.8.refs_0_ = bf16[512,384]{1,0:T(8,128)(2,1)S(1)} collective-permute-done((bf16[512,384]{1,0:T(8,128)(2,1)S(1)}, bf16[512,384]{1,0:T(8,128)(2,1)S(1)}, u32[]{:S(2)}, u32[]{:S(2)}) %collective-permute-start.8) | collective-permute-done | bytes 393248 | tf_op jit(solution)/shard_map/ppermute | solution.py:26
  40.5 3.7 %shard_map.154 = (f32[512,1536]{1,0:T(8,128)S(1)}, f32[8,128]{1,0:T(8,128)S(1)}) custom-call(bf16[512,768]{1,0:T(8,128)(2,1)S(1)} %get-tuple-element.36.query_ref, bf16[512,384]{1,0:T(8,128)(2,1)S(1)} %get-tuple-element.37.key_ref.refs_1_, bf16[512,768]{1,0:T(8,128)(2,1)S(1)} %get-tuple-element.38.value_ref), custom_call_target="tpu_custom_call" | custom-call | flops 1000 | bytes 1000 | tf_op jit(solution)/shard_map/pallas_call | solution.py:38
  44.2 4.1 %collective-permute-done.6.refs_0_ = bf16[512,384]{1,0:T(8,128)(2,1)S(1)} collective-permute-done((bf16[512,384]{1,0:T(8,128)(2,1)S(1)}, bf16[512,384]{1,0:T(8,128)(2,1)S(1)}, u32[]{:S(2)}, u32[]{:S(2)}) %collective-permute-start.6) | collective-permute-done | bytes 393248 | tf_op jit(solution)/shard_map/ppermute | solution.py:26
  48.3 0.5 collective-permute-start.7
  48.9 1.6 %collective-permute-start.16 = (bf16[192,1536]{1,0:T(8,128)(2,1)S(1)}, bf16[192,1536]{1,0:T(8,128)(2,1)S(1)}, u32[]{:S(2)}, u32[]{:S(2)}) collective-permute-start(bf16[192,1536]{1,0:T(8,128)(2,1)S(1)} %collective-permute-done.5.refs_8_.refs_9_), channel_id=1, source_target_pairs={{0,16},{16,0},{1,17},{17,1},{2,18},{18,2},{3,19},{19,3},{4,20},{20... | collective-permute-start | bytes 1769480 | tf_op jit(solution)/shard_map/ppermute | solution.py:26
  50.6 1.9 %shard_map.157 = (bf16[512,384]{1,0:T(8,128)(2,1)S(1)}, bf16[512,768]{1,0:T(8,128)(2,1)S(1)}) custom-call(bf16[512,384]{1,0:T(8,128)(2,1)S(1)} %collective-permute-done.4.refs_7_.refs_0_, bf16[512,384]{1,0:T(8,128)(2,1)S(1)} %shard_map.156.refs_1_, bf16[512,384]{1,0:T(8,128)(2,1)S(1)} %collective-permute-done.9.refs_2_, ...), custom_call_target="tpu_custom_call" | custom-call | flops 1000 | bytes 1000 | tf_op jit(solution)/shard_map/pallas_call | solution.py:38
  52.5 4.4 %shard_map.158 = (f32[512,1536]{1,0:T(8,128)S(1)}, f32[8,128]{1,0:T(8,128)S(1)}) custom-call(bf16[512,768]{1,0:T(8,128)(2,1)S(1)} %get-tuple-element.36.query_ref, bf16[512,384]{1,0:T(8,128)(2,1)S(1)} %get-tuple-element.40.key_ref, bf16[512,768]{1,0:T(8,128)(2,1)S(1)} %get-tuple-element.41.value_ref, ...), custom_call_target="tpu_custom_call", output_to_operand_aliasing={{0}: (3, {})} | custom-call | flops 1000 | bytes 1000 | tf_op jit(solution)/shard_map/pallas_call | solution.py:38
  56.9 2.5 %collective-permute-done.7.refs_0_ = bf16[512,384]{1,0:T(8,128)(2,1)S(1)} collective-permute-done((bf16[512,384]{1,0:T(8,128)(2,1)S(1)}, bf16[512,384]{1,0:T(8,128)(2,1)S(1)}, u32[]{:S(2)}, u32[]{:S(2)}) %collective-permute-start.7) | collective-permute-done | bytes 393248 | tf_op jit(solution)/shard_map/ppermute | solution.py:26
  59.4 0.5 collective-permute-start.12
  60.0 4.6 %collective-permute-done.16.refs_1_.refs_10_ = bf16[192,1536]{1,0:T(8,128)(2,1)S(1)} collective-permute-done((bf16[192,1536]{1,0:T(8,128)(2,1)S(1)}, bf16[192,1536]{1,0:T(8,128)(2,1)S(1)}, u32[]{:S(2)}, u32[]{:S(2)}) %collective-permute-start.16) | collective-permute-done | bytes 589856 | tf_op jit(solution)/shard_map/ppermute | solution.py:26
  64.6 1.8 %shard_map.162 = (bf16[512,384]{1,0:T(8,128)(2,1)S(1)}, bf16[512,768]{1,0:T(8,128)(2,1)S(1)}) custom-call(bf16[512,384]{1,0:T(8,128)(2,1)S(1)} %shard_map.150.refs_6_.refs_0_, bf16[512,384]{1,0:T(8,128)(2,1)S(1)} %shard_map.161.refs_1_, bf16[512,384]{1,0:T(8,128)(2,1)S(1)} %collective-permute-done.14.refs_2_, ...), custom_call_target="tpu_custom_call" | custom-call | flops 1000 | bytes 1000 | tf_op jit(solution)/shard_map/pallas_call | solution.py:38
  66.4 4.7 %shard_map.163 = (f32[512,1536]{1,0:T(8,128)S(1)}, f32[8,128]{1,0:T(8,128)}) custom-call(bf16[512,768]{1,0:T(8,128)(2,1)S(1)} %get-tuple-element.36.query_ref, bf16[512,384]{1,0:T(8,128)(2,1)S(1)} %get-tuple-element.46.key_ref, bf16[512,768]{1,0:T(8,128)(2,1)S(1)} %get-tuple-element.47.value_ref, ...), custom_call_target="tpu_custom_call", output_to_operand_aliasing={{0}: (3, {})} | custom-call | flops 1000 | bytes 1000 | tf_op jit(solution)/shard_map/pallas_call | solution.py:38
  71.1 1.9 %shard_map.160 = (bf16[512,384]{1,0:T(8,128)(2,1)S(1)}, bf16[512,768]{1,0:T(8,128)(2,1)S(1)}) custom-call(bf16[512,384]{1,0:T(8,128)(2,1)S(1)} %shard_map.155.refs_1_.refs_0_, bf16[512,384]{1,0:T(8,128)(2,1)S(1)} %shard_map.159.refs_1_, bf16[512,384]{1,0:T(8,128)(2,1)S(1)} %collective-permute-done.11.refs_2_, ...), custom_call_target="tpu_custom_call" | custom-call | flops 1000 | bytes 1000 | tf_op jit(solution)/shard_map/pallas_call | solution.py:38
  73.0 3.6 %shard_map.164.refs_0_ = bf16[256,384]{1,0:T(8,128)(2,1)S(1)} custom-call(bf16[512,768]{1,0:T(8,128)(2,1)S(1)} %get-tuple-element.36.query_ref, bf16[512,384]{1,0:T(8,128)(2,1)S(1)} %get-tuple-element.44.key_ref, bf16[512,768]{1,0:T(8,128)(2,1)S(1)} %get-tuple-element.45.value_ref, f32[512,1536]{1,0:T(8,128)S(1)} %get-tuple-element.49.refs_0_, ...), custom_call_target="tpu_custom_call" | custom-call | flops 1000 | bytes 1000 | tf_op jit(solution)/shard_map/pallas_call | solution.py:38
  76.6 1.6 %collective-permute-start.17 = (bf16[256,384]{1,0:T(8,128)(2,1)S(1)}, bf16[256,384]{1,0:T(8,128)(2,1)S(1)}, u32[]{:S(2)}, u32[]{:S(2)}) collective-permute-start(bf16[256,384]{1,0:T(8,128)(2,1)S(1)} %shard_map.164.refs_0_), channel_id=1, source_target_pairs={{0,2},{1,3},{2,0},{3,1},{4,6},{5,7},{6,4},{7,5},{8,10},{9,11},{10,... | collective-permute-start | bytes 589832 | tf_op jit(solution)/shard_map/ppermute | solution.py:26
  78.4 2.1 %shard_map.165.refs_1_.refs_0_ = bf16[256,384]{1,0:T(8,128)(2,1)S(1)} custom-call(bf16[512,768]{1,0:T(8,128)(2,1)S(1)} %get-tuple-element.36.query_ref, bf16[512,384]{1,0:T(8,128)(2,1)S(1)} %get-tuple-element.44.key_ref, bf16[512,768]{1,0:T(8,128)(2,1)S(1)} %get-tuple-element.45.value_ref, f32[512,1536]{1,0:T(8,128)S(1)} %get-tuple-element.49.refs_0_, ...), custom_call_target="tpu_custom_call" | custom-call | flops 1000 | bytes 1000 | tf_op jit(solution)/shard_map/pallas_call | solution.py:38
  80.5 3.4 %collective-permute-done.17.refs_0_ = bf16[256,384]{1,0:T(8,128)(2,1)S(1)} collective-permute-done((bf16[256,384]{1,0:T(8,128)(2,1)S(1)}, bf16[256,384]{1,0:T(8,128)(2,1)S(1)}, u32[]{:S(2)}, u32[]{:S(2)}) %collective-permute-start.17) | collective-permute-done | bytes 196640 | tf_op jit(solution)/shard_map/ppermute | solution.py:26
  84.0 1.6 %collective-permute-start.23 = (bf16[256,384]{1,0:T(8,128)(2,1)S(1)}, bf16[256,384]{1,0:T(8,128)(2,1)S(1)}, u32[]{:S(2)}, u32[]{:S(2)}) collective-permute-start(bf16[256,384]{1,0:T(8,128)(2,1)S(1)} %shard_map.165.refs_1_.refs_0_), channel_id=1, source_target_pairs={{0,2},{1,3},{2,0},{3,1},{4,6},{5,7},{6,4},{7,5},{8,10},{9,11},{10,... | collective-permute-start | bytes 589832 | tf_op jit(solution)/shard_map/ppermute | solution.py:26
  85.8 2.5 %shard_map.167 = (bf16[256,384]{1,0:T(8,128)(2,1)S(1)}, bf16[256,384]{1,0:T(8,128)(2,1)S(1)}, bf16[16,384]{1,0:T(8,128)(2,1)S(1)}, bf16[16,384]{1,0:T(8,128)(2,1)S(1)}) custom-call(s32[1]{0:T(128)} %bitcast.me_ref, s32[1]{0:T(128)} %bitcast.1.part_ref, bf16[256,384]{1,0:T(8,128)(2,1)S(1)} %shard_map.164.refs_0_, bf16[256,384]{1,0:T(8,128)(2,1)S(1)} %shard_map.166.refs_1_, ...), custom_call_target="tpu_custom_call" | custom-call | flops 1000 | bytes 1000 | tf_op jit(solution)/shard_map/pallas_call | solution.py:38
  88.3 3.0 %collective-permute-done.23.refs_0_ = bf16[256,384]{1,0:T(8,128)(2,1)S(1)} collective-permute-done((bf16[256,384]{1,0:T(8,128)(2,1)S(1)}, bf16[256,384]{1,0:T(8,128)(2,1)S(1)}, u32[]{:S(2)}, u32[]{:S(2)}) %collective-permute-start.23) | collective-permute-done | bytes 196640 | tf_op jit(solution)/shard_map/ppermute | solution.py:26
  91.3 1.5 %collective-permute-start.26 = (bf16[16,384]{1,0:T(8,128)(2,1)S(1)}, bf16[16,384]{1,0:T(8,128)(2,1)S(1)}, u32[]{:S(2)}, u32[]{:S(2)}) collective-permute-start(bf16[16,384]{1,0:T(8,128)(2,1)S(1)} %get-tuple-element.54), channel_id=1, source_target_pairs={{0,4},{4,8},{8,12},{1,5},{5,9},{9,13},{2,6},{6,10},{10,14},{3,7},{... | collective-permute-start | bytes 36872 | tf_op jit(solution)/shard_map/ppermute | solution.py:545
  92.8 1.3 %collective-permute-start.27 = (bf16[16,384]{1,0:T(8,128)(2,1)S(1)}, bf16[16,384]{1,0:T(8,128)(2,1)S(1)}, u32[]{:S(2)}, u32[]{:S(2)}) collective-permute-start(bf16[16,384]{1,0:T(8,128)(2,1)S(1)} %get-tuple-element.55), channel_id=1, source_target_pairs={{4,0},{8,4},{12,8},{5,1},{9,5},{13,9},{6,2},{10,6},{14,10},{7,3},{... | collective-permute-start | bytes 36872 | tf_op jit(solution)/shard_map/ppermute | solution.py:546
  94.2 3.1 %shard_map.169 = (bf16[256,384]{1,0:T(8,128)(2,1)S(1)}, bf16[256,384]{1,0:T(8,128)(2,1)S(1)}, bf16[16,384]{1,0:T(8,128)(2,1)}, bf16[16,384]{1,0:T(8,128)(2,1)}) custom-call(s32[1]{0:T(128)} %bitcast.me_ref, s32[1]{0:T(128)} %bitcast.1.part_ref, bf16[256,384]{1,0:T(8,128)(2,1)S(1)} %shard_map.165.refs_1_.refs_0_, bf16[256,384]{1,0:T(8,128)(2,1)S(1)} %shard_map.168.refs_1_, ...), custom_call_target="tpu_custom_call" | custom-call | flops 1000 | bytes 1000 | tf_op jit(solution)/shard_map/pallas_call | solution.py:38
  97.3 1.7 %collective-permute-done.27.refs_1_ = bf16[16,384]{1,0:T(8,128)(2,1)S(1)} collective-permute-done((bf16[16,384]{1,0:T(8,128)(2,1)S(1)}, bf16[16,384]{1,0:T(8,128)(2,1)S(1)}, u32[]{:S(2)}, u32[]{:S(2)}) %collective-permute-start.27) | collective-permute-done | bytes 12320 | tf_op jit(solution)/shard_map/ppermute | solution.py:546
  99.0 1.7 %shard_map.170 = (bf16[256,768]{1,0:T(8,128)(2,1)S(1)}, bf16[256,768]{1,0:T(8,128)(2,1)S(1)}) custom-call(bf16[256,384]{1,0:T(8,128)(2,1)S(1)} %get-tuple-element.52.refs_1_.first_ref, bf16[256,384]{1,0:T(8,128)(2,1)S(1)} %get-tuple-element.53.second_ref, bf16[16,384]{1,0:T(8,128)(2,1)S(1)} %collective-permute-done.26.refs_0_, ...), custom_call_target="tpu_custom_call" | custom-call | flops 1000 | bytes 1000 | tf_op jit(solution)/shard_map/pallas_call | solution.py:38
  100.8 2.0 %shard_map.171 = (bf16[256,768]{1,0:T(8,128)(2,1)S(1)}, bf16[256,768]{1,0:T(8,128)(2,1)S(1)}) custom-call(bf16[256,384]{1,0:T(8,128)(2,1)S(1)} %get-tuple-element.52.refs_1_.first_ref, bf16[256,384]{1,0:T(8,128)(2,1)S(1)} %get-tuple-element.53.second_ref, f32[31,384]{1,0:T(8,128)S(1)} %copy-done.2, f32[2,384]{1,0:T(2,128)S(1)} %pad_maximum_fusion.1.refs_3_.refs_1_, ...), custom_call_target="tpu_custom_call" | custom-call | flops 1000 | bytes 1000 | tf_op jit(solution)/shard_map/pallas_call | solution.py:38
  102.8 0.6 collective-permute-start.30
  103.4 1.6 %collective-permute-start.29 = (bf16[256,384]{1,0:T(8,128)(2,1)S(1)}, bf16[256,384]{1,0:T(8,128)(2,1)S(1)}, u32[]{:S(2)}, u32[]{:S(2)}) collective-permute-start(bf16[256,384]{1,0:T(8,128)(2,1)S(1)} %add_convert_fusion.3), channel_id=1, source_target_pairs={{0,2},{1,3},{2,0},{3,1},{4,6},{5,7},{6,4},{7,5},{8,10},{9,11},{10,... | collective-permute-start | bytes 589832 | tf_op jit(solution)/shard_map/ppermute | solution.py:26
  105.0 1.3 %collective-permute-start.31 = (bf16[256,384]{1,0:T(8,128)(2,1)S(1)}, bf16[256,384]{1,0:T(8,128)(2,1)S(1)}, u32[]{:S(2)}, u32[]{:S(2)}) collective-permute-start(bf16[256,384]{1,0:T(8,128)(2,1)S(1)} %add_convert_fusion.1), channel_id=1, source_target_pairs={{0,2},{1,3},{2,0},{3,1},{4,6},{5,7},{6,4},{7,5},{8,10},{9,11},{10,... | collective-permute-start | bytes 589832 | tf_op jit(solution)/shard_map/ppermute | solution.py:26
  106.3 4.9 %collective-permute-done.29 = bf16[256,384]{1,0:T(8,128)(2,1)S(1)} collective-permute-done((bf16[256,384]{1,0:T(8,128)(2,1)S(1)}, bf16[256,384]{1,0:T(8,128)(2,1)S(1)}, u32[]{:S(2)}, u32[]{:S(2)}) %collective-permute-start.29) | collective-permute-done | bytes 196640 | tf_op jit(solution)/shard_map/ppermute | solution.py:26
  111.4 3.1 %collective-permute-done.31 = bf16[256,384]{1,0:T(8,128)(2,1)S(1)} collective-permute-done((bf16[256,384]{1,0:T(8,128)(2,1)S(1)}, bf16[256,384]{1,0:T(8,128)(2,1)S(1)}, u32[]{:S(2)}, u32[]{:S(2)}) %collective-permute-start.31) | collective-permute-done | bytes 196640 | tf_op jit(solution)/shard_map/ppermute | solution.py:26
  114.6 0.8 pad_maximum_fusion
  (63 shorter events, 2.0 us)
Async XLA Ops:
  0.0 20.9 %collective-permute-start = (bf16[512,384]{1,0:T(8,128)(2,1)}, bf16[512,384]{1,0:T(8,128)(2,1)S(1)}, u32[]{:S(2)}, u32[]{:S(2)}) collective-permute-start(bf16[512,384]{1,0:T(8,128)(2,1)} %refs_4_.3), channel_id=1, source_target_pairs={{0,2},{1,3},{2,0},{3,1},{4,6},{5,7},{6,4},{7,5},{8,10},{9,11},{10,... | collective-permute-start | bytes 1179656 | tf_op jit(solution)/shard_map/ppermute | solution.py:26
  2.9 20.2 %collective-permute-start.3 = (bf16[512,384]{1,0:T(8,128)(2,1)}, bf16[512,384]{1,0:T(8,128)(2,1)S(1)}, u32[]{:S(2)}, u32[]{:S(2)}) collective-permute-start(bf16[512,384]{1,0:T(8,128)(2,1)} %refs_4_.3), channel_id=1, source_target_pairs={{0,8},{4,12},{8,0},{12,4},{1,9},{5,13},{9,1},{13,5},{2,10},{6,14},... | collective-permute-start | bytes 1179656 | tf_op jit(solution)/shard_map/ppermute | solution.py:26
  13.4 3.0 %copy-start.1 = (bf16[512,384]{1,0:T(8,128)(2,1)S(1)}, bf16[512,384]{1,0:T(8,128)(2,1)}, u32[]{:S(2)}) copy-start(bf16[512,384]{1,0:T(8,128)(2,1)} %refs_4_.3) | copy-start | bytes 1179652
  14.5 17.0 %collective-permute-start.5 = (bf16[192,1536]{1,0:T(8,128)(2,1)S(1)}, bf16[192,1536]{1,0:T(8,128)(2,1)S(1)}, u32[]{:S(2)}, u32[]{:S(2)}) collective-permute-start(bf16[192,1536]{1,0:T(8,128)(2,1)S(1)} %shard_map.152), channel_id=1, source_target_pairs={{0,2},{1,3},{2,0},{3,1},{4,6},{5,7},{6,4},{7,5},{8,10},{9,11},{10,... | collective-permute-start | bytes 1769480 | tf_op jit(solution)/shard_map/ppermute | solution.py:26
  16.3 11.3 %collective-permute-start.1 = (bf16[512,384]{1,0:T(8,128)(2,1)S(1)}, bf16[512,384]{1,0:T(8,128)(2,1)S(1)}, u32[]{:S(2)}, u32[]{:S(2)}) collective-permute-start(bf16[512,384]{1,0:T(8,128)(2,1)S(1)} %copy-done.1), channel_id=1, source_target_pairs={{0,1},{1,0},{2,3},{3,2},{4,5},{5,4},{6,7},{7,6},{8,9},{9,8},{10,11... | collective-permute-start | bytes 1179656 | tf_op jit(solution)/shard_map/ppermute | solution.py:26
  16.4 15.2 %collective-permute-start.4 = (bf16[512,384]{1,0:T(8,128)(2,1)S(1)}, bf16[512,384]{1,0:T(8,128)(2,1)S(1)}, u32[]{:S(2)}, u32[]{:S(2)}) collective-permute-start(bf16[512,384]{1,0:T(8,128)(2,1)S(1)} %copy-done.1), channel_id=1, source_target_pairs={{0,4},{4,0},{8,12},{12,8},{1,5},{5,1},{9,13},{13,9},{2,6},{6,2},{1... | collective-permute-start | bytes 1179656 | tf_op jit(solution)/shard_map/ppermute | solution.py:26
  20.9 11.1 %collective-permute-start.2 = (bf16[512,384]{1,0:T(8,128)(2,1)S(1)}, bf16[512,384]{1,0:T(8,128)(2,1)S(1)}, u32[]{:S(2)}, u32[]{:S(2)}) collective-permute-start(bf16[512,384]{1,0:T(8,128)(2,1)S(1)} %shard_map.147.refs_1_.refs_5_), channel_id=1, source_target_pairs={{0,1},{1,0},{2,3},{3,2},{4,5},{5,4},{6,7},{7,6},{8,9},{9,8},{10,11... | collective-permute-start | bytes 1179656 | tf_op jit(solution)/shard_map/ppermute | solution.py:26
  23.2 16.8 %collective-permute-start.8 = (bf16[512,384]{1,0:T(8,128)(2,1)S(1)}, bf16[512,384]{1,0:T(8,128)(2,1)S(1)}, u32[]{:S(2)}, u32[]{:S(2)}) collective-permute-start(bf16[512,384]{1,0:T(8,128)(2,1)S(1)} %shard_map.147.refs_1_.refs_5_), channel_id=1, source_target_pairs={{0,4},{4,0},{8,12},{12,8},{1,5},{5,1},{9,13},{13,9},{2,6},{6,2},{1... | collective-permute-start | bytes 1179656 | tf_op jit(solution)/shard_map/ppermute | solution.py:26
  27.6 20.7 %collective-permute-start.6 = (bf16[512,384]{1,0:T(8,128)(2,1)S(1)}, bf16[512,384]{1,0:T(8,128)(2,1)S(1)}, u32[]{:S(2)}, u32[]{:S(2)}) collective-permute-start(bf16[512,384]{1,0:T(8,128)(2,1)S(1)} %shard_map.150.refs_6_.refs_0_), channel_id=1, source_target_pairs={{0,4},{4,0},{8,12},{12,8},{1,5},{5,1},{9,13},{13,9},{2,6},{6,2},{1... | collective-permute-start | bytes 1179656 | tf_op jit(solution)/shard_map/ppermute | solution.py:26
  31.5 17.3 %collective-permute-start.9 = (bf16[512,384]{1,0:T(8,128)(2,1)S(1)}, bf16[512,384]{1,0:T(8,128)(2,1)S(1)}, u32[]{:S(2)}, u32[]{:S(2)}) collective-permute-start(bf16[512,384]{1,0:T(8,128)(2,1)S(1)} %collective-permute-done.4.refs_7_.refs_0_), channel_id=1, source_target_pairs={{0,1},{1,0},{2,3},{3,2},{4,5},{5,4},{6,7},{7,6},{8,9},{9,8},{10,11... | collective-permute-start | bytes 1179656 | tf_op jit(solution)/shard_map/ppermute | solution.py:26
  31.6 17.3 %collective-permute-start.13 = (bf16[512,384]{1,0:T(8,128)(2,1)S(1)}, bf16[512,384]{1,0:T(8,128)(2,1)S(1)}, u32[]{:S(2)}, u32[]{:S(2)}) collective-permute-start(bf16[512,384]{1,0:T(8,128)(2,1)S(1)} %shard_map.150.refs_6_.refs_0_), channel_id=1, source_target_pairs={{0,2},{1,3},{2,0},{3,1},{4,6},{5,7},{6,4},{7,5},{8,10},{9,11},{10,... | collective-permute-start | bytes 1179656 | tf_op jit(solution)/shard_map/ppermute | solution.py:26
  35.1 4.9 %copy-start = (bf16[384,1536]{1,0:T(8,128)(2,1)S(1)}, bf16[384,1536]{1,0:T(8,128)(2,1)}, u32[]{:S(2)}) copy-start(bf16[384,1536]{1,0:T(8,128)(2,1)} %refs_8_.3) | copy-start | bytes 3538948
  40.0 10.5 %collective-permute-start.10 = (bf16[512,384]{1,0:T(8,128)(2,1)S(1)}, bf16[512,384]{1,0:T(8,128)(2,1)S(1)}, u32[]{:S(2)}, u32[]{:S(2)}) collective-permute-start(bf16[512,384]{1,0:T(8,128)(2,1)S(1)} %shard_map.156.refs_1_), channel_id=1, source_target_pairs={{0,1},{1,0},{2,3},{3,2},{4,5},{5,4},{6,7},{7,6},{8,9},{9,8},{10,11... | collective-permute-start | bytes 1179656 | tf_op jit(solution)/shard_map/ppermute | solution.py:26
  40.0 44.0 %collective-permute-start.20 = (bf16[384,1536]{1,0:T(8,128)(2,1)S(1)}, bf16[384,1536]{1,0:T(8,128)(2,1)S(1)}, u32[]{:S(2)}, u32[]{:S(2)}) collective-permute-start(bf16[384,1536]{1,0:T(8,128)(2,1)S(1)} %copy-done), channel_id=1, source_target_pairs={{0,1},{1,0},{2,3},{3,2},{4,5},{5,4},{6,7},{7,6},{8,9},{9,8},{10,11... | collective-permute-start | bytes 3538952 | tf_op jit(solution)/shard_map/ppermute | solution.py:26
  48.3 11.1 %collective-permute-start.7 = (bf16[512,384]{1,0:T(8,128)(2,1)S(1)}, bf16[512,384]{1,0:T(8,128)(2,1)S(1)}, u32[]{:S(2)}, u32[]{:S(2)}) collective-permute-start(bf16[512,384]{1,0:T(8,128)(2,1)S(1)} %shard_map.155.refs_1_.refs_0_), channel_id=1, source_target_pairs={{0,2},{1,3},{2,0},{3,1},{4,6},{5,7},{6,4},{7,5},{8,10},{9,11},{10,... | collective-permute-start | bytes 1179656 | tf_op jit(solution)/shard_map/ppermute | solution.py:26
  48.8 10.6 %collective-permute-start.14 = (bf16[512,384]{1,0:T(8,128)(2,1)S(1)}, bf16[512,384]{1,0:T(8,128)(2,1)S(1)}, u32[]{:S(2)}, u32[]{:S(2)}) collective-permute-start(bf16[512,384]{1,0:T(8,128)(2,1)S(1)} %shard_map.150.refs_6_.refs_0_), channel_id=1, source_target_pairs={{0,1},{1,0},{2,3},{3,2},{4,5},{5,4},{6,7},{7,6},{8,9},{9,8},{10,11... | collective-permute-start | bytes 1179656 | tf_op jit(solution)/shard_map/ppermute | solution.py:26
  48.9 15.7 %collective-permute-start.16 = (bf16[192,1536]{1,0:T(8,128)(2,1)S(1)}, bf16[192,1536]{1,0:T(8,128)(2,1)S(1)}, u32[]{:S(2)}, u32[]{:S(2)}) collective-permute-start(bf16[192,1536]{1,0:T(8,128)(2,1)S(1)} %collective-permute-done.5.refs_8_.refs_9_), channel_id=1, source_target_pairs={{0,16},{16,0},{1,17},{17,1},{2,18},{18,2},{3,19},{19,3},{4,20},{20... | collective-permute-start | bytes 1769480 | tf_op jit(solution)/shard_map/ppermute | solution.py:26
  50.5 9.5 %collective-permute-start.15 = (bf16[512,384]{1,0:T(8,128)(2,1)S(1)}, bf16[512,384]{1,0:T(8,128)(2,1)S(1)}, u32[]{:S(2)}, u32[]{:S(2)}) collective-permute-start(bf16[512,384]{1,0:T(8,128)(2,1)S(1)} %shard_map.161.refs_1_), channel_id=1, source_target_pairs={{0,1},{1,0},{2,3},{3,2},{4,5},{5,4},{6,7},{7,6},{8,9},{9,8},{10,11... | collective-permute-start | bytes 1179656 | tf_op jit(solution)/shard_map/ppermute | solution.py:26
  59.4 11.7 %collective-permute-start.11 = (bf16[512,384]{1,0:T(8,128)(2,1)S(1)}, bf16[512,384]{1,0:T(8,128)(2,1)S(1)}, u32[]{:S(2)}, u32[]{:S(2)}) collective-permute-start(bf16[512,384]{1,0:T(8,128)(2,1)S(1)} %shard_map.155.refs_1_.refs_0_), channel_id=1, source_target_pairs={{0,1},{1,0},{2,3},{3,2},{4,5},{5,4},{6,7},{7,6},{8,9},{9,8},{10,11... | collective-permute-start | bytes 1179656 | tf_op jit(solution)/shard_map/ppermute | solution.py:26
  59.4 11.7 %collective-permute-start.12 = (bf16[512,384]{1,0:T(8,128)(2,1)S(1)}, bf16[512,384]{1,0:T(8,128)(2,1)S(1)}, u32[]{:S(2)}, u32[]{:S(2)}) collective-permute-start(bf16[512,384]{1,0:T(8,128)(2,1)S(1)} %shard_map.159.refs_1_), channel_id=1, source_target_pairs={{0,1},{1,0},{2,3},{3,2},{4,5},{5,4},{6,7},{7,6},{8,9},{9,8},{10,11... | collective-permute-start | bytes 1179656 | tf_op jit(solution)/shard_map/ppermute | solution.py:26
  60.0 25.6 %collective-permute-start.21 = (bf16[192,1536]{1,0:T(8,128)(2,1)S(1)}, bf16[192,1536]{1,0:T(8,128)(2,1)S(1)}, u32[]{:S(2)}, u32[]{:S(2)}) collective-permute-start(bf16[192,1536]{1,0:T(8,128)(2,1)S(1)} %collective-permute-done.5.refs_8_.refs_9_), channel_id=1, source_target_pairs={{0,1},{1,0},{2,3},{3,2},{4,5},{5,4},{6,7},{7,6},{8,9},{9,8},{10,11... | collective-permute-start | bytes 1769480 | tf_op jit(solution)/shard_map/ppermute | solution.py:26
  64.6 21.2 %collective-permute-start.22 = (bf16[192,1536]{1,0:T(8,128)(2,1)S(1)}, bf16[192,1536]{1,0:T(8,128)(2,1)S(1)}, u32[]{:S(2)}, u32[]{:S(2)}) collective-permute-start(bf16[192,1536]{1,0:T(8,128)(2,1)S(1)} %collective-permute-done.16.refs_1_.refs_10_), channel_id=1, source_target_pairs={{0,1},{1,0},{2,3},{3,2},{4,5},{5,4},{6,7},{7,6},{8,9},{9,8},{10,11... | collective-permute-start | bytes 1769480 | tf_op jit(solution)/shard_map/ppermute | solution.py:26
  76.6 7.4 %collective-permute-start.17 = (bf16[256,384]{1,0:T(8,128)(2,1)S(1)}, bf16[256,384]{1,0:T(8,128)(2,1)S(1)}, u32[]{:S(2)}, u32[]{:S(2)}) collective-permute-start(bf16[256,384]{1,0:T(8,128)(2,1)S(1)} %shard_map.164.refs_0_), channel_id=1, source_target_pairs={{0,2},{1,3},{2,0},{3,1},{4,6},{5,7},{6,4},{7,5},{8,10},{9,11},{10,... | collective-permute-start | bytes 589832 | tf_op jit(solution)/shard_map/ppermute | solution.py:26
  78.2 7.6 %collective-permute-start.18 = (bf16[256,384]{1,0:T(8,128)(2,1)S(1)}, bf16[256,384]{1,0:T(8,128)(2,1)S(1)}, u32[]{:S(2)}, u32[]{:S(2)}) collective-permute-start(bf16[256,384]{1,0:T(8,128)(2,1)S(1)} %shard_map.164.refs_0_), channel_id=1, source_target_pairs={{0,1},{1,0},{2,3},{3,2},{4,5},{5,4},{6,7},{7,6},{8,9},{9,8},{10,11... | collective-permute-start | bytes 589832 | tf_op jit(solution)/shard_map/ppermute | solution.py:26
  84.0 1.8 %collective-permute-start.19 = (bf16[256,384]{1,0:T(8,128)(2,1)S(1)}, bf16[256,384]{1,0:T(8,128)(2,1)S(1)}, u32[]{:S(2)}, u32[]{:S(2)}) collective-permute-start(bf16[256,384]{1,0:T(8,128)(2,1)S(1)} %shard_map.166.refs_1_), channel_id=1, source_target_pairs={{0,1},{1,0},{2,3},{3,2},{4,5},{5,4},{6,7},{7,6},{8,9},{9,8},{10,11... | collective-permute-start | bytes 589832 | tf_op jit(solution)/shard_map/ppermute | solution.py:26
  84.0 7.3 %collective-permute-start.23 = (bf16[256,384]{1,0:T(8,128)(2,1)S(1)}, bf16[256,384]{1,0:T(8,128)(2,1)S(1)}, u32[]{:S(2)}, u32[]{:S(2)}) collective-permute-start(bf16[256,384]{1,0:T(8,128)(2,1)S(1)} %shard_map.165.refs_1_.refs_0_), channel_id=1, source_target_pairs={{0,2},{1,3},{2,0},{3,1},{4,6},{5,7},{6,4},{7,5},{8,10},{9,11},{10,... | collective-permute-start | bytes 589832 | tf_op jit(solution)/shard_map/ppermute | solution.py:26
  85.6 8.5 %collective-permute-start.24 = (bf16[256,384]{1,0:T(8,128)(2,1)S(1)}, bf16[256,384]{1,0:T(8,128)(2,1)S(1)}, u32[]{:S(2)}, u32[]{:S(2)}) collective-permute-start(bf16[256,384]{1,0:T(8,128)(2,1)S(1)} %shard_map.165.refs_1_.refs_0_), channel_id=1, source_target_pairs={{0,1},{1,0},{2,3},{3,2},{4,5},{5,4},{6,7},{7,6},{8,9},{9,8},{10,11... | collective-permute-start | bytes 589832 | tf_op jit(solution)/shard_map/ppermute | solution.py:26
  85.8 5.5 %copy-start.3 = (f32[384]{0:T(512)S(1)}, f32[384]{0:T(512)}, u32[]{:S(2)}) copy-start(f32[384]{0:T(512)} %param.28) | copy-start | bytes 4612
  85.8 5.5 %copy-start.4 = (f32[384]{0:T(512)S(1)}, f32[384]{0:T(512)}, u32[]{:S(2)}) copy-start(f32[384]{0:T(512)} %param.27) | copy-start | bytes 4612
  91.3 2.8 %collective-permute-start.25 = (bf16[256,384]{1,0:T(8,128)(2,1)S(1)}, bf16[256,384]{1,0:T(8,128)(2,1)S(1)}, u32[]{:S(2)}, u32[]{:S(2)}) collective-permute-start(bf16[256,384]{1,0:T(8,128)(2,1)S(1)} %shard_map.168.refs_1_), channel_id=1, source_target_pairs={{0,1},{1,0},{2,3},{3,2},{4,5},{5,4},{6,7},{7,6},{8,9},{9,8},{10,11... | collective-permute-start | bytes 589832 | tf_op jit(solution)/shard_map/ppermute | solution.py:26
  91.3 6.0 %collective-permute-start.26 = (bf16[16,384]{1,0:T(8,128)(2,1)S(1)}, bf16[16,384]{1,0:T(8,128)(2,1)S(1)}, u32[]{:S(2)}, u32[]{:S(2)}) collective-permute-start(bf16[16,384]{1,0:T(8,128)(2,1)S(1)} %get-tuple-element.54), channel_id=1, source_target_pairs={{0,4},{4,8},{8,12},{1,5},{5,9},{9,13},{2,6},{6,10},{10,14},{3,7},{... | collective-permute-start | bytes 36872 | tf_op jit(solution)/shard_map/ppermute | solution.py:545
  92.8 6.2 %collective-permute-start.27 = (bf16[16,384]{1,0:T(8,128)(2,1)S(1)}, bf16[16,384]{1,0:T(8,128)(2,1)S(1)}, u32[]{:S(2)}, u32[]{:S(2)}) collective-permute-start(bf16[16,384]{1,0:T(8,128)(2,1)S(1)} %get-tuple-element.55), channel_id=1, source_target_pairs={{4,0},{8,4},{12,8},{5,1},{9,5},{13,9},{6,2},{10,6},{14,10},{7,3},{... | collective-permute-start | bytes 36872 | tf_op jit(solution)/shard_map/ppermute | solution.py:546
  94.1 4.9 %copy-start.2 = (f32[31,384]{1,0:T(8,128)S(1)}, f32[31,384]{1,0:T(8,128)}, u32[]{:S(2)}) copy-start(f32[31,384]{1,0:T(8,128)} %refs_0_.9) | copy-start | bytes 142852
  100.7 2.7 %collective-permute-start.28 = (bf16[256,768]{1,0:T(8,128)(2,1)S(1)}, bf16[256,768]{1,0:T(8,128)(2,1)S(1)}, u32[]{:S(2)}, u32[]{:S(2)}) collective-permute-start(bf16[256,768]{1,0:T(8,128)(2,1)S(1)} %get-tuple-element.57), channel_id=1, source_target_pairs={{0,1},{1,0},{2,3},{3,2},{4,5},{5,4},{6,7},{7,6},{8,9},{9,8},{10,11... | collective-permute-start | bytes 1179656 | tf_op jit(solution)/shard_map/ppermute | solution.py:26
  102.8 2.2 %collective-permute-start.30 = (bf16[256,768]{1,0:T(8,128)(2,1)S(1)}, bf16[256,768]{1,0:T(8,128)(2,1)S(1)}, u32[]{:S(2)}, u32[]{:S(2)}) collective-permute-start(bf16[256,768]{1,0:T(8,128)(2,1)S(1)} %get-tuple-element.60), channel_id=1, source_target_pairs={{0,1},{1,0},{2,3},{3,2},{4,5},{5,4},{6,7},{7,6},{8,9},{9,8},{10,11... | collective-permute-start | bytes 1179656 | tf_op jit(solution)/shard_map/ppermute | solution.py:26
  103.4 7.8 %collective-permute-start.29 = (bf16[256,384]{1,0:T(8,128)(2,1)S(1)}, bf16[256,384]{1,0:T(8,128)(2,1)S(1)}, u32[]{:S(2)}, u32[]{:S(2)}) collective-permute-start(bf16[256,384]{1,0:T(8,128)(2,1)S(1)} %add_convert_fusion.3), channel_id=1, source_target_pairs={{0,2},{1,3},{2,0},{3,1},{4,6},{5,7},{6,4},{7,5},{8,10},{9,11},{10,... | collective-permute-start | bytes 589832 | tf_op jit(solution)/shard_map/ppermute | solution.py:26
  105.0 9.5 %collective-permute-start.31 = (bf16[256,384]{1,0:T(8,128)(2,1)S(1)}, bf16[256,384]{1,0:T(8,128)(2,1)S(1)}, u32[]{:S(2)}, u32[]{:S(2)}) collective-permute-start(bf16[256,384]{1,0:T(8,128)(2,1)S(1)} %add_convert_fusion.1), channel_id=1, source_target_pairs={{0,2},{1,3},{2,0},{3,1},{4,6},{5,7},{6,4},{7,5},{8,10},{9,11},{10,... | collective-permute-start | bytes 589832 | tf_op jit(solution)/shard_map/ppermute | solution.py:26

commit v4 on v3

--- a/solution.py
+++ b/solution.py
@@ -438,7 +438,7 @@
     taps = pad_columns(depth_kernel, padded)
     bn = pad_columns(jnp.stack([bn_scale, bn_shift]), padded)
     qkv, qkv_sums = folded(place, order, 0, gains, (w_key, w_value, w_query))
-    chips[0] = [after(block, qkv_sums) for block in chips[0]]
+    chips[0] = [after(block, gains) for block in chips[0]]
     glu, glu_sums = folded(place, order, 2, gains, (w_glu_value, w_glu_gate))
 
     parts = lax.axis_size("parts")
@@ -453,7 +453,7 @@
         )
     else:
         half = w_out
-    crossed = over_chips(after(half, gains))
+    crossed = over_chips(after(half, *chips[0]))
     state_shape = ((frames, 4 * padded), F32)
     token_shape = ((8, 128), F32)
     wide, narrow = ((frames, 2 * padded), BF16), ((frames, padded), BF16)
@@ -461,39 +461,31 @@
     own = [frames_in] + chips[0]
     own_blocks = own + other_core(own)
     n = len(own_blocks)
-    raw.update({s: after(block, glu_sums, w_p) for s, block in raw.items() if s > 1})
-    early = [*[raw[s] for s in raw if s], *crossed]
+    early = [*[raw[s] for s in raw if s], *crossed, *chips[1]]
     queries, keys, values = kernel_call(
         functools.partial(project_kernel, n, True),
         [wide, narrow, wide],
         [*own_blocks, qkv, qkv_sums, *early],
         spaces={n + 2 + i: pl.ANY for i in range(len(early))},
     )
-    swapped = [exchange(block, "parts", 1) for block in crossed] if parts == 2 else []
-    pieces = [w_out]
-    for a, block in enumerate(crossed):
-        pieces += [block, swapped[a]] if swapped else [block]
-    pieces = pieces + other_core(pieces)
-
-    def prepare(s):
+    def prepare(s, done):
         if 2 <= s < ctx:
             low = s & -s
             if s != low:
-                raw[s] = after(exchange(raw[s ^ low], "ctx", low), token)
+                raw[s] = after(exchange(raw[s ^ low], "ctx", low), done)
             chips[s] = over_chips(raw[s])
 
-    prepare(2)
+    prepare(2, None)
     state, token = kernel_call(
         functools.partial(attend_kernel, True, False, chunks_of(every, query_rows)),
         [state_shape, token_shape],
         [queries, keys, values],
     )
-    moved = {1: [after(block, keys) for block in chips[1]]}
+    crossed = [after(block, token) for block in crossed]
+    swapped = [exchange(block, "parts", 1) for block in crossed] if parts == 2 else []
+    moved = {1: chips[1]}
     for s in range(1, ctx):
         last = s == ctx - 1
-        prepare(s + 2)
-        if not last:
-            moved[s + 1] = [after(block, token) for block in chips[s + 1]]
         mine = [raw[s]] + moved[s]
         keys, values = kernel_call(
             functools.partial(project_kernel, n, False),
@@ -502,9 +494,10 @@
         )
         if last:
             break
+        prepare(s + 2, token)
+        moved[s + 1] = [after(block, token) for block in chips[s + 1]]
         behind = [raw[s + 2]] if s + 2 < ctx else []
-        if s > 1:
-            behind = behind + moved[s + 1]
+        behind += moved[s + 1] + ([glu_sums, w_p] if s == 1 else [])
         state, token = kernel_call(
             functools.partial(attend_kernel, False, False, chunks_of(every, query_rows)),
             [state_shape, token_shape],
@@ -520,11 +513,15 @@
         (mine,) = kernel_call(
             functools.partial(attend_kernel, False, True, chunks_of(spans[h], query_rows)),
             [((rows, padded), BF16)],
-            [queries, keys, values, state, *swapped],
-            spaces={4 + i: pl.ANY for i in range(len(swapped))},
+            [queries, keys, values, state],
             scratch=[pltpu.VMEM((rows, 4 * padded), F32)],
         )
         attended.append([mine] + over_chips(mine))
+    swapped = [after(block, attended[0][0]) for block in swapped]
+    pieces = [w_out]
+    for a, block in enumerate(crossed):
+        pieces += [block, swapped[a]] if swapped else [block]
+    pieces = pieces + other_core(pieces)
     if width % PAIR:
         pieces = [by_distance(piece) for piece in pieces]
     middle, gated = [], []

time: 116 us -> 109 us (0.940)
  waiting for transfers between devices: 36.9 us -> 27.5 us
  blocking collectives: 7.07 us -> 5.23 us
  local copies, waits for them, and re-layouts: 0.06 us -> 1.47 us
  Pallas kernels: 44.9 us -> 46.3 us
  starting transfers between devices: 25.1 us -> 26.4 us
    ppermute x30, waiting for transfers between devices: 35.1 us -> 26.4 us  [exchange(): return lax.ppermute(cells, axis, [(i, i ^ distance) for i in range(count)])]
    ppermute x1, starting transfers between devices: 1.46 us -> 3.34 us  [on_device(): left = lax.ppermute(results[3], 'ctx', [(i, i + 1) for i in range(ctx - 1)])]
    all_gather x1, blocking collectives: 7.07 us -> 5.23 us  [on_device(): gains = lax.all_gather(gains, 'grid', axis=0, tiled=True)]
    unnamed x10 -> x16, local copies, waits for them, and re-layouts: 0.03 us -> 1.45 us
    pallas_call x18, Pallas kernels: 44.9 us -> 46.3 us  [kernel_call(): pl.pallas_call(body, in_specs=in_specs, out_specs=tuple((pl.BlockSpec(mem...]
  transfers between devices with their start and end apart: 32 -> 32, of which waited for: 11 -> 8; matrix products, arithmetic and copies ran while one was open for 0% -> 0% of each run, Pallas kernels for 37% -> 41%
where the time goes in v4:
time: 109 us; the launch traced here: 108 us
  Pallas kernels  46.3 us (42%)
  waiting for transfers between devices  27.5 us (25%)
  starting transfers between devices  26.4 us (24%)
  blocking collectives  5.23 us (5%)
  local copies, waits for them, and re-layouts  1.47 us (1%)
  other arithmetic  1.13 us (1%)
    pallas_call x18, Pallas kernels, kernel_call(): pl.pallas_call(body, in_specs=in_specs, out_specs=tuple((pl.BlockSpec(mem...  46.3 us
    ppermute x30, waiting for transfers between devices, exchange(): return lax.ppermute(cells, axis, [(i, i ^ distance) for i in range(count)])  26.4 us
    ppermute x30, starting transfers between devices, exchange(): return lax.ppermute(cells, axis, [(i, i ^ distance) for i in range(count)])  21.8 us
    all_gather x1, blocking collectives, on_device(): gains = lax.all_gather(gains, 'grid', axis=0, tiled=True)  5.23 us
    ppermute x1, starting transfers between devices, on_device(): left = lax.ppermute(results[3], 'ctx', [(i, i + 1) for i in range(ctx - 1)])  3.34 us
  transfers between devices with their start and end apart: 32, of which 8 were waited for; matrix products, arithmetic and copies ran while one was open for 0% of the time, Pallas kernels for 41%

profile of v4, /device:TPU:0, one launch (start us, length us, event | category | flops | bytes accessed | tf_op | source)
XLA Modules:
  0.0 108.4 jit_solution(4281608757158829447)
XLA Ops:
  0.0 2.9 %collective-permute-start = (bf16[512,384]{1,0:T(8,128)(2,1)}, bf16[512,384]{1,0:T(8,128)(2,1)S(1)}, u32[]{:S(2)}, u32[]{:S(2)}) collective-permute-start(bf16[512,384]{1,0:T(8,128)(2,1)} %refs_4_.3), channel_id=1, source_target_pairs={{0,2},{1,3},{2,0},{3,1},{4,6},{5,7},{6,4},{7,5},{8,10},{9,11},{10,... | collective-permute-start | bytes 1179656 | tf_op jit(solution)/shard_map/ppermute | solution.py:26
  2.9 2.6 %collective-permute-start.3 = (bf16[512,384]{1,0:T(8,128)(2,1)}, bf16[512,384]{1,0:T(8,128)(2,1)S(1)}, u32[]{:S(2)}, u32[]{:S(2)}) collective-permute-start(bf16[512,384]{1,0:T(8,128)(2,1)} %refs_4_.3), channel_id=1, source_target_pairs={{0,8},{4,12},{8,0},{12,4},{1,9},{5,13},{9,1},{13,5},{2,10},{6,14},... | collective-permute-start | bytes 1179656 | tf_op jit(solution)/shard_map/ppermute | solution.py:26
  5.5 1.6 %collective-permute-start.4 = (bf16[512,384]{1,0:T(8,128)(2,1)}, bf16[512,384]{1,0:T(8,128)(2,1)}, u32[]{:S(2)}, u32[]{:S(2)}) collective-permute-start(bf16[512,384]{1,0:T(8,128)(2,1)} %refs_4_.3), channel_id=1, source_target_pairs={{0,4},{4,0},{8,12},{12,8},{1,5},{5,1},{9,13},{13,9},{2,6},{6,2},{1... | collective-permute-start | bytes 1179656 | tf_op jit(solution)/shard_map/ppermute | solution.py:26
  7.1 1.1 shard_map.148.refs_0_
  8.2 0.8 shard_map.145
  9.0 5.2 %all_gather.3.refs_1_.gains_ref = f32[32,384]{1,0:T(8,128)S(1)} all-gather(f32[8,384]{1,0:T(8,128)S(1)} %shard_map.145), channel_id=1, replica_groups=mesh['parts'=2,'ctx'=4,'grid'=4] {'grid'}, dimensions={0}, use_global_device_ids=true | all-gather | bytes 61440 | tf_op jit(solution)/shard_map/all_gather | solution.py:418
  14.2 0.6 copy-done.2
  14.8 0.9 collective-permute-start.5
  15.8 1.6 %collective-permute-start.6 = (bf16[512,384]{1,0:T(8,128)(2,1)S(1)}, bf16[512,384]{1,0:T(8,128)(2,1)}, u32[]{:S(2)}, u32[]{:S(2)}) collective-permute-start(bf16[512,384]{1,0:T(8,128)(2,1)S(1)} %shard_map.146.refs_1_.refs_5_), channel_id=1, source_target_pairs={{0,4},{4,0},{8,12},{12,8},{1,5},{5,1},{9,13},{13,9},{2,6},{6,2},{1... | collective-permute-start | bytes 1179656 | tf_op jit(solution)/shard_map/ppermute | solution.py:26
  17.4 6.7 %collective-permute-done.3.refs_6_.refs_0_ = bf16[512,384]{1,0:T(8,128)(2,1)S(1)} collective-permute-done((bf16[512,384]{1,0:T(8,128)(2,1)}, bf16[512,384]{1,0:T(8,128)(2,1)S(1)}, u32[]{:S(2)}, u32[]{:S(2)}) %collective-permute-start.3) | collective-permute-done | bytes 393248 | tf_op jit(solution)/shard_map/ppermute | solution.py:26
  24.1 0.7 collective-permute-start.7
  24.8 0.6 collective-permute-start.11
  25.4 0.8 copy-done.3
  26.2 3.0 %shard_map.147 = (bf16[1536,1152]{1,0:T(8,128)(2,1)S(1)}, f32[2,1152]{1,0:T(2,128)S(1)}) custom-call(s32[1]{0:T(128)} %bitcast.me_ref, f32[32,384]{1,0:T(8,128)S(1)} %copy-done.3, bf16[1536,384]{1,0:T(8,128)(2,1)} %refs_0_.6, bf16[1536,384]{1,0:T(8,128)(2,1)} %refs_1_.4, bf16[1536,384]{1,0:T(8,128)(2,1)} %refs_2_.4), custom_call_target="tpu_custom_call" | custom-call | flops 1000 | bytes 1000 | tf_op jit(solution)/shard_map/pallas_call | solution.py:38
  29.3 3.7 %collective-permute-done.6.refs_9_.refs_1_ = bf16[512,384]{1,0:T(8,128)(2,1)} collective-permute-done((bf16[512,384]{1,0:T(8,128)(2,1)S(1)}, bf16[512,384]{1,0:T(8,128)(2,1)}, u32[]{:S(2)}, u32[]{:S(2)}) %collective-permute-start.6) | collective-permute-done | bytes 393248 | tf_op jit(solution)/shard_map/ppermute | solution.py:26
  33.0 3.0 %shard_map.150 = (bf16[512,768]{1,0:T(8,128)(2,1)S(1)}, bf16[512,384]{1,0:T(8,128)(2,1)S(1)}, bf16[512,768]{1,0:T(8,128)(2,1)S(1)}) custom-call(bf16[512,384]{1,0:T(8,128)(2,1)S(1)} %copy-done.1, bf16[512,384]{1,0:T(8,128)(2,1)S(1)} %shard_map.146.refs_1_.refs_5_, bf16[512,384]{1,0:T(8,128)(2,1)S(1)} %collective-permute-done.1.refs_2_.refs_6_, ...), custom_call_target="tpu_custom_call" | custom-call | flops 1000 | bytes 1000 | tf_op jit(solution)/shard_map/pallas_call | solution.py:38
  36.0 3.8 %shard_map.151 = (f32[512,1536]{1,0:T(8,128)S(1)}, f32[8,128]{1,0:T(8,128)S(1)}) custom-call(bf16[512,768]{1,0:T(8,128)(2,1)S(1)} %get-tuple-element.35.query_ref, bf16[512,384]{1,0:T(8,128)(2,1)S(1)} %get-tuple-element.36.key_ref, bf16[512,768]{1,0:T(8,128)(2,1)S(1)} %get-tuple-element.37.value_ref), custom_call_target="tpu_custom_call" | custom-call | flops 1000 | bytes 1000 | tf_op jit(solution)/shard_map/pallas_call | solution.py:38
  39.8 1.4 %collective-permute-done.7.refs_0_ = bf16[512,384]{1,0:T(8,128)(2,1)S(1)} collective-permute-done((bf16[512,384]{1,0:T(8,128)(2,1)S(1)}, bf16[512,384]{1,0:T(8,128)(2,1)S(1)}, u32[]{:S(2)}, u32[]{:S(2)}) %collective-permute-start.7) | collective-permute-done | bytes 393248 | tf_op jit(solution)/shard_map/ppermute | solution.py:26
  41.2 0.5 collective-permute-start.8
  41.6 0.5 collective-permute-start.20
  42.2 1.6 %collective-permute-start.19 = (bf16[192,1536]{1,0:T(8,128)(2,1)S(1)}, bf16[192,1536]{1,0:T(8,128)(2,1)S(1)}, u32[]{:S(2)}, u32[]{:S(2)}) collective-permute-start(bf16[192,1536]{1,0:T(8,128)(2,1)S(1)} %shard_map.165.refs_9_), channel_id=1, source_target_pairs={{0,16},{16,0},{1,17},{17,1},{2,18},{18,2},{3,19},{19,3},{4,20},{20... | collective-permute-start | bytes 1769480 | tf_op jit(solution)/shard_map/ppermute | solution.py:26
  43.7 1.3 %shard_map.156.refs_4_.refs_2_ = bf16[384,1536]{1,0:T(8,128)(2,1)S(1)} custom-call(s32[1]{0:T(128)} %bitcast.me_ref, bf16[384,1536]{1,0:T(8,128)(2,1)} %source_ref.3), custom_call_target="tpu_custom_call" | custom-call | flops 1000 | bytes 1000 | tf_op jit(solution)/shard_map/pallas_call | solution.py:38
  45.0 2.4 %shard_map.155 = (bf16[1536,768]{1,0:T(8,128)(2,1)S(1)}, f32[2,768]{1,0:T(2,128)S(1)}) custom-call(s32[1]{0:T(128)} %bitcast.me_ref, f32[32,384]{1,0:T(8,128)S(1)} %copy-done.4, bf16[1536,384]{1,0:T(8,128)(2,1)} %refs_0_.8, bf16[1536,384]{1,0:T(8,128)(2,1)} %refs_1_.5), custom_call_target="tpu_custom_call" | custom-call | flops 1000 | bytes 1000 | tf_op jit(solution)/shard_map/pallas_call | solution.py:38
  47.6 3.1 %shard_map.153 = (bf16[512,384]{1,0:T(8,128)(2,1)S(1)}, bf16[512,768]{1,0:T(8,128)(2,1)S(1)}) custom-call(bf16[512,384]{1,0:T(8,128)(2,1)} %collective-permute-done.4.refs_7_.refs_0_, bf16[512,384]{1,0:T(8,128)(2,1)} %collective-permute-done.6.refs_9_.refs_1_, bf16[512,384]{1,0:T(8,128)(2,1)} %collective-permute-done.9.refs_2_, ...), custom_call_target="tpu_custom_call" | custom-call | flops 1000 | bytes 1000 | tf_op jit(solution)/shard_map/pallas_call | solution.py:38
  50.7 4.4 %shard_map.157 = (f32[512,1536]{1,0:T(8,128)S(1)}, f32[8,128]{1,0:T(8,128)S(1)}) custom-call(bf16[512,768]{1,0:T(8,128)(2,1)S(1)} %get-tuple-element.35.query_ref, bf16[512,384]{1,0:T(8,128)(2,1)S(1)} %get-tuple-element.39.key_ref, bf16[512,768]{1,0:T(8,128)(2,1)S(1)} %get-tuple-element.40.value_ref, ...), custom_call_target="tpu_custom_call", output_to_operand_aliasing={{0}: (3, {})} | custom-call | flops 1000 | bytes 1000 | tf_op jit(solution)/shard_map/pallas_call | solution.py:38
  55.1 0.6 collective-permute-start.12
  56.2 1.8 %shard_map.160 = (bf16[512,384]{1,0:T(8,128)(2,1)S(1)}, bf16[512,768]{1,0:T(8,128)(2,1)S(1)}) custom-call(bf16[512,384]{1,0:T(8,128)(2,1)S(1)} %collective-permute-done.3.refs_6_.refs_0_, bf16[512,384]{1,0:T(8,128)(2,1)S(1)} %shard_map.154.refs_2_.refs_1_, bf16[512,384]{1,0:T(8,128)(2,1)S(1)} %collective-permute-done.14.refs_2_, ...), custom_call_target="tpu_custom_call" | custom-call | flops 1000 | bytes 1000 | tf_op jit(solution)/shard_map/pallas_call | solution.py:38
  58.0 4.7 %shard_map.161 = (f32[512,1536]{1,0:T(8,128)S(1)}, f32[8,128]{1,0:T(8,128)}) custom-call(bf16[512,768]{1,0:T(8,128)(2,1)S(1)} %get-tuple-element.35.query_ref, bf16[512,384]{1,0:T(8,128)(2,1)S(1)} %get-tuple-element.46.key_ref, bf16[512,768]{1,0:T(8,128)(2,1)S(1)} %get-tuple-element.47.value_ref, ...), custom_call_target="tpu_custom_call", output_to_operand_aliasing={{0}: (3, {})} | custom-call | flops 1000 | bytes 1000 | tf_op jit(solution)/shard_map/pallas_call | solution.py:38
  62.7 1.8 %shard_map.159 = (bf16[512,384]{1,0:T(8,128)(2,1)S(1)}, bf16[512,768]{1,0:T(8,128)(2,1)S(1)}) custom-call(bf16[512,384]{1,0:T(8,128)(2,1)S(1)} %shard_map.152.refs_1_.refs_0_, bf16[512,384]{1,0:T(8,128)(2,1)S(1)} %shard_map.158.refs_1_, bf16[512,384]{1,0:T(8,128)(2,1)S(1)} %collective-permute-done.12.refs_2_, ...), custom_call_target="tpu_custom_call" | custom-call | flops 1000 | bytes 1000 | tf_op jit(solution)/shard_map/pallas_call | solution.py:38
  64.6 3.6 %shard_map.162.refs_1_.refs_0_ = bf16[256,384]{1,0:T(8,128)(2,1)S(1)} custom-call(bf16[512,768]{1,0:T(8,128)(2,1)S(1)} %get-tuple-element.35.query_ref, bf16[512,384]{1,0:T(8,128)(2,1)S(1)} %get-tuple-element.44.key_ref, bf16[512,768]{1,0:T(8,128)(2,1)S(1)} %get-tuple-element.45.value_ref, f32[512,1536]{1,0:T(8,128)S(1)} %get-tuple-element.49.refs_0_), custom_call_target="tpu_custom_call" | custom-call | flops 1000 | bytes 1000 | tf_op jit(solution)/shard_map/pallas_call | solution.py:38
  68.4 1.5 %collective-permute-start.16 = (bf16[256,384]{1,0:T(8,128)(2,1)S(1)}, bf16[256,384]{1,0:T(8,128)(2,1)S(1)}, u32[]{:S(2)}, u32[]{:S(2)}) collective-permute-start(bf16[256,384]{1,0:T(8,128)(2,1)S(1)} %shard_map.162.refs_1_.refs_0_), channel_id=1, source_target_pairs={{0,2},{1,3},{2,0},{3,1},{4,6},{5,7},{6,4},{7,5},{8,10},{9,11},{10,... | collective-permute-start | bytes 589832 | tf_op jit(solution)/shard_map/ppermute | solution.py:26
  69.9 2.1 %shard_map.163.refs_1_.refs_0_ = bf16[256,384]{1,0:T(8,128)(2,1)S(1)} custom-call(bf16[512,768]{1,0:T(8,128)(2,1)S(1)} %get-tuple-element.35.query_ref, bf16[512,384]{1,0:T(8,128)(2,1)S(1)} %get-tuple-element.44.key_ref, bf16[512,768]{1,0:T(8,128)(2,1)S(1)} %get-tuple-element.45.value_ref, f32[512,1536]{1,0:T(8,128)S(1)} %get-tuple-element.49.refs_0_), custom_call_target="tpu_custom_call" | custom-call | flops 1000 | bytes 1000 | tf_op jit(solution)/shard_map/pallas_call | solution.py:38
  72.2 3.4 %collective-permute-done.16.refs_0_ = bf16[256,384]{1,0:T(8,128)(2,1)S(1)} collective-permute-done((bf16[256,384]{1,0:T(8,128)(2,1)S(1)}, bf16[256,384]{1,0:T(8,128)(2,1)S(1)}, u32[]{:S(2)}, u32[]{:S(2)}) %collective-permute-start.16) | collective-permute-done | bytes 196640 | tf_op jit(solution)/shard_map/ppermute | solution.py:26
  75.7 1.5 %collective-permute-start.23 = (bf16[256,384]{1,0:T(8,128)(2,1)S(1)}, bf16[256,384]{1,0:T(8,128)(2,1)S(1)}, u32[]{:S(2)}, u32[]{:S(2)}) collective-permute-start(bf16[256,384]{1,0:T(8,128)(2,1)S(1)} %shard_map.163.refs_1_.refs_0_), channel_id=1, source_target_pairs={{0,2},{1,3},{2,0},{3,1},{4,6},{5,7},{6,4},{7,5},{8,10},{9,11},{10,... | collective-permute-start | bytes 589832 | tf_op jit(solution)/shard_map/ppermute | solution.py:26
  77.4 2.5 %shard_map.167 = (bf16[256,384]{1,0:T(8,128)(2,1)S(1)}, bf16[256,384]{1,0:T(8,128)(2,1)S(1)}, bf16[16,384]{1,0:T(8,128)(2,1)S(1)}, bf16[16,384]{1,0:T(8,128)(2,1)S(1)}) custom-call(s32[1]{0:T(128)} %bitcast.me_ref, s32[1]{0:T(128)} %bitcast.1.part_ref, bf16[256,384]{1,0:T(8,128)(2,1)S(1)} %shard_map.162.refs_1_.refs_0_, ...), custom_call_target="tpu_custom_call" | custom-call | flops 1000 | bytes 1000 | tf_op jit(solution)/shard_map/pallas_call | solution.py:38
  80.0 3.0 %collective-permute-done.23.refs_0_ = bf16[256,384]{1,0:T(8,128)(2,1)S(1)} collective-permute-done((bf16[256,384]{1,0:T(8,128)(2,1)S(1)}, bf16[256,384]{1,0:T(8,128)(2,1)S(1)}, u32[]{:S(2)}, u32[]{:S(2)}) %collective-permute-start.23) | collective-permute-done | bytes 196640 | tf_op jit(solution)/shard_map/ppermute | solution.py:26
  83.0 3.3 %collective-permute-start.26 = (bf16[16,384]{1,0:T(8,128)(2,1)S(1)}, bf16[16,384]{1,0:T(8,128)(2,1)S(1)}, u32[]{:S(2)}, u32[]{:S(2)}) collective-permute-start(bf16[16,384]{1,0:T(8,128)(2,1)S(1)} %get-tuple-element.54), channel_id=1, source_target_pairs={{0,4},{4,8},{8,12},{1,5},{5,9},{9,13},{2,6},{6,10},{10,14},{3,7},{... | collective-permute-start | bytes 36872 | tf_op jit(solution)/shard_map/ppermute | solution.py:542
  86.4 1.3 %collective-permute-start.27 = (bf16[16,384]{1,0:T(8,128)(2,1)S(1)}, bf16[16,384]{1,0:T(8,128)(2,1)S(1)}, u32[]{:S(2)}, u32[]{:S(2)}) collective-permute-start(bf16[16,384]{1,0:T(8,128)(2,1)S(1)} %get-tuple-element.55), channel_id=1, source_target_pairs={{4,0},{8,4},{12,8},{5,1},{9,5},{13,9},{6,2},{10,6},{14,10},{7,3},{... | collective-permute-start | bytes 36872 | tf_op jit(solution)/shard_map/ppermute | solution.py:543
  87.7 3.1 %shard_map.169 = (bf16[256,384]{1,0:T(8,128)(2,1)S(1)}, bf16[256,384]{1,0:T(8,128)(2,1)S(1)}, bf16[16,384]{1,0:T(8,128)(2,1)}, bf16[16,384]{1,0:T(8,128)(2,1)}) custom-call(s32[1]{0:T(128)} %bitcast.me_ref, s32[1]{0:T(128)} %bitcast.1.part_ref, bf16[256,384]{1,0:T(8,128)(2,1)S(1)} %shard_map.163.refs_1_.refs_0_, bf16[256,384]{1,0:T(8,128)(2,1)S(1)} %shard_map.168.refs_1_, ...), custom_call_target="tpu_custom_call" | custom-call | flops 1000 | bytes 1000 | tf_op jit(solution)/shard_map/pallas_call | solution.py:38
  90.9 1.1 %collective-permute-done.27.refs_1_ = bf16[16,384]{1,0:T(8,128)(2,1)S(1)} collective-permute-done((bf16[16,384]{1,0:T(8,128)(2,1)S(1)}, bf16[16,384]{1,0:T(8,128)(2,1)S(1)}, u32[]{:S(2)}, u32[]{:S(2)}) %collective-permute-start.27) | collective-permute-done | bytes 12320 | tf_op jit(solution)/shard_map/ppermute | solution.py:543
  92.0 1.7 %shard_map.170 = (bf16[256,768]{1,0:T(8,128)(2,1)S(1)}, bf16[256,768]{1,0:T(8,128)(2,1)S(1)}) custom-call(bf16[256,384]{1,0:T(8,128)(2,1)S(1)} %get-tuple-element.52.refs_1_.first_ref, bf16[256,384]{1,0:T(8,128)(2,1)S(1)} %get-tuple-element.53.second_ref, bf16[16,384]{1,0:T(8,128)(2,1)S(1)} %collective-permute-done.26.refs_0_, ...), custom_call_target="tpu_custom_call" | custom-call | flops 1000 | bytes 1000 | tf_op jit(solution)/shard_map/pallas_call | solution.py:38
  93.7 2.0 %shard_map.171 = (bf16[256,768]{1,0:T(8,128)(2,1)S(1)}, bf16[256,768]{1,0:T(8,128)(2,1)S(1)}) custom-call(bf16[256,384]{1,0:T(8,128)(2,1)S(1)} %get-tuple-element.52.refs_1_.first_ref, bf16[256,384]{1,0:T(8,128)(2,1)S(1)} %get-tuple-element.53.second_ref, f32[31,384]{1,0:T(8,128)S(1)} %copy-done.5, f32[2,384]{1,0:T(2,128)S(1)} %pad_maximum_fusion.1.refs_3_.refs_1_, ...), custom_call_target="tpu_custom_call" | custom-call | flops 1000 | bytes 1000 | tf_op jit(solution)/shard_map/pallas_call | solution.py:38
  95.7 0.6 collective-permute-start.30
  96.3 1.6 %collective-permute-start.29 = (bf16[256,384]{1,0:T(8,128)(2,1)S(1)}, bf16[256,384]{1,0:T(8,128)(2,1)S(1)}, u32[]{:S(2)}, u32[]{:S(2)}) collective-permute-start(bf16[256,384]{1,0:T(8,128)(2,1)S(1)} %add_convert_fusion.3), channel_id=1, source_target_pairs={{0,2},{1,3},{2,0},{3,1},{4,6},{5,7},{6,4},{7,5},{8,10},{9,11},{10,... | collective-permute-start | bytes 589832 | tf_op jit(solution)/shard_map/ppermute | solution.py:26
  98.0 1.3 %collective-permute-start.31 = (bf16[256,384]{1,0:T(8,128)(2,1)S(1)}, bf16[256,384]{1,0:T(8,128)(2,1)S(1)}, u32[]{:S(2)}, u32[]{:S(2)}) collective-permute-start(bf16[256,384]{1,0:T(8,128)(2,1)S(1)} %add_convert_fusion.1), channel_id=1, source_target_pairs={{0,2},{1,3},{2,0},{3,1},{4,6},{5,7},{6,4},{7,5},{8,10},{9,11},{10,... | collective-permute-start | bytes 589832 | tf_op jit(solution)/shard_map/ppermute | solution.py:26
  99.3 4.9 %collective-permute-done.29 = bf16[256,384]{1,0:T(8,128)(2,1)S(1)} collective-permute-done((bf16[256,384]{1,0:T(8,128)(2,1)S(1)}, bf16[256,384]{1,0:T(8,128)(2,1)S(1)}, u32[]{:S(2)}, u32[]{:S(2)}) %collective-permute-start.29) | collective-permute-done | bytes 196640 | tf_op jit(solution)/shard_map/ppermute | solution.py:26
  104.3 3.1 %collective-permute-done.31 = bf16[256,384]{1,0:T(8,128)(2,1)S(1)} collective-permute-done((bf16[256,384]{1,0:T(8,128)(2,1)S(1)}, bf16[256,384]{1,0:T(8,128)(2,1)S(1)}, u32[]{:S(2)}, u32[]{:S(2)}) %collective-permute-start.31) | collective-permute-done | bytes 196640 | tf_op jit(solution)/shard_map/ppermute | solution.py:26
  107.6 0.8 pad_maximum_fusion
  (69 shorter events, 1.7 us)
Async XLA Ops:
  0.0 14.2 %collective-permute-start = (bf16[512,384]{1,0:T(8,128)(2,1)}, bf16[512,384]{1,0:T(8,128)(2,1)S(1)}, u32[]{:S(2)}, u32[]{:S(2)}) collective-permute-start(bf16[512,384]{1,0:T(8,128)(2,1)} %refs_4_.3), channel_id=1, source_target_pairs={{0,2},{1,3},{2,0},{3,1},{4,6},{5,7},{6,4},{7,5},{8,10},{9,11},{10,... | collective-permute-start | bytes 1179656 | tf_op jit(solution)/shard_map/ppermute | solution.py:26
  2.9 12.9 %collective-permute-start.1 = (bf16[512,384]{1,0:T(8,128)(2,1)}, bf16[512,384]{1,0:T(8,128)(2,1)S(1)}, u32[]{:S(2)}, u32[]{:S(2)}) collective-permute-start(bf16[512,384]{1,0:T(8,128)(2,1)} %refs_4_.3), channel_id=1, source_target_pairs={{0,1},{1,0},{2,3},{3,2},{4,5},{5,4},{6,7},{7,6},{8,9},{9,8},{10,11... | collective-permute-start | bytes 1179656 | tf_op jit(solution)/shard_map/ppermute | solution.py:26
  2.9 21.2 %collective-permute-start.3 = (bf16[512,384]{1,0:T(8,128)(2,1)}, bf16[512,384]{1,0:T(8,128)(2,1)S(1)}, u32[]{:S(2)}, u32[]{:S(2)}) collective-permute-start(bf16[512,384]{1,0:T(8,128)(2,1)} %refs_4_.3), channel_id=1, source_target_pairs={{0,8},{4,12},{8,0},{12,4},{1,9},{5,13},{9,1},{13,5},{2,10},{6,14},... | collective-permute-start | bytes 1179656 | tf_op jit(solution)/shard_map/ppermute | solution.py:26
  5.5 19.3 %collective-permute-start.4 = (bf16[512,384]{1,0:T(8,128)(2,1)}, bf16[512,384]{1,0:T(8,128)(2,1)}, u32[]{:S(2)}, u32[]{:S(2)}) collective-permute-start(bf16[512,384]{1,0:T(8,128)(2,1)} %refs_4_.3), channel_id=1, source_target_pairs={{0,4},{4,0},{8,12},{12,8},{1,5},{5,1},{9,13},{13,9},{2,6},{6,2},{1... | collective-permute-start | bytes 1179656 | tf_op jit(solution)/shard_map/ppermute | solution.py:26
  14.2 0.6 copy-start.2
  14.8 18.2 %collective-permute-start.5 = (bf16[192,1536]{1,0:T(8,128)(2,1)S(1)}, bf16[192,1536]{1,0:T(8,128)(2,1)S(1)}, u32[]{:S(2)}, u32[]{:S(2)}) collective-permute-start(bf16[192,1536]{1,0:T(8,128)(2,1)S(1)} %shard_map.149), channel_id=1, source_target_pairs={{0,2},{1,3},{2,0},{3,1},{4,6},{5,7},{6,4},{7,5},{8,10},{9,11},{10,... | collective-permute-start | bytes 1769480 | tf_op jit(solution)/shard_map/ppermute | solution.py:26
  15.7 9.1 %collective-permute-start.2 = (bf16[512,384]{1,0:T(8,128)(2,1)S(1)}, bf16[512,384]{1,0:T(8,128)(2,1)S(1)}, u32[]{:S(2)}, u32[]{:S(2)}) collective-permute-start(bf16[512,384]{1,0:T(8,128)(2,1)S(1)} %shard_map.146.refs_1_.refs_5_), channel_id=1, source_target_pairs={{0,1},{1,0},{2,3},{3,2},{4,5},{5,4},{6,7},{7,6},{8,9},{9,8},{10,11... | collective-permute-start | bytes 1179656 | tf_op jit(solution)/shard_map/ppermute | solution.py:26
  15.8 17.2 %collective-permute-start.6 = (bf16[512,384]{1,0:T(8,128)(2,1)S(1)}, bf16[512,384]{1,0:T(8,128)(2,1)}, u32[]{:S(2)}, u32[]{:S(2)}) collective-permute-start(bf16[512,384]{1,0:T(8,128)(2,1)S(1)} %shard_map.146.refs_1_.refs_5_), channel_id=1, source_target_pairs={{0,4},{4,0},{8,12},{12,8},{1,5},{5,1},{9,13},{13,9},{2,6},{6,2},{1... | collective-permute-start | bytes 1179656 | tf_op jit(solution)/shard_map/ppermute | solution.py:26
  24.1 17.0 %collective-permute-start.7 = (bf16[512,384]{1,0:T(8,128)(2,1)S(1)}, bf16[512,384]{1,0:T(8,128)(2,1)S(1)}, u32[]{:S(2)}, u32[]{:S(2)}) collective-permute-start(bf16[512,384]{1,0:T(8,128)(2,1)S(1)} %collective-permute-done.3.refs_6_.refs_0_), channel_id=1, source_target_pairs={{0,4},{4,0},{8,12},{12,8},{1,5},{5,1},{9,13},{13,9},{2,6},{6,2},{1... | collective-permute-start | bytes 1179656 | tf_op jit(solution)/shard_map/ppermute | solution.py:26
  24.8 16.8 %collective-permute-start.9 = (bf16[512,384]{1,0:T(8,128)(2,1)}, bf16[512,384]{1,0:T(8,128)(2,1)}, u32[]{:S(2)}, u32[]{:S(2)}) collective-permute-start(bf16[512,384]{1,0:T(8,128)(2,1)} %collective-permute-done.4.refs_7_.refs_0_), channel_id=1, source_target_pairs={{0,1},{1,0},{2,3},{3,2},{4,5},{5,4},{6,7},{7,6},{8,9},{9,8},{10,11... | collective-permute-start | bytes 1179656 | tf_op jit(solution)/shard_map/ppermute | solution.py:26
  24.8 17.3 %collective-permute-start.11 = (bf16[512,384]{1,0:T(8,128)(2,1)S(1)}, bf16[512,384]{1,0:T(8,128)(2,1)S(1)}, u32[]{:S(2)}, u32[]{:S(2)}) collective-permute-start(bf16[512,384]{1,0:T(8,128)(2,1)S(1)} %collective-permute-done.3.refs_6_.refs_0_), channel_id=1, source_target_pairs={{0,2},{1,3},{2,0},{3,1},{4,6},{5,7},{6,4},{7,5},{8,10},{9,11},{10,... | collective-permute-start | bytes 1179656 | tf_op jit(solution)/shard_map/ppermute | solution.py:26
  25.4 0.8 copy-start.3
  26.2 6.7 %copy-start.1 = (bf16[512,384]{1,0:T(8,128)(2,1)S(1)}, bf16[512,384]{1,0:T(8,128)(2,1)}, u32[]{:S(2)}) copy-start(bf16[512,384]{1,0:T(8,128)(2,1)} %refs_4_.3) | copy-start | bytes 1179652
  33.0 14.5 %collective-permute-start.10 = (bf16[512,384]{1,0:T(8,128)(2,1)}, bf16[512,384]{1,0:T(8,128)(2,1)S(1)}, u32[]{:S(2)}, u32[]{:S(2)}) collective-permute-start(bf16[512,384]{1,0:T(8,128)(2,1)} %collective-permute-done.6.refs_9_.refs_1_), channel_id=1, source_target_pairs={{0,1},{1,0},{2,3},{3,2},{4,5},{5,4},{6,7},{7,6},{8,9},{9,8},{10,11... | collective-permute-start | bytes 1179656 | tf_op jit(solution)/shard_map/ppermute | solution.py:26
  36.0 5.7 %copy-start = (bf16[384,1536]{1,0:T(8,128)(2,1)S(1)}, bf16[384,1536]{1,0:T(8,128)(2,1)}, u32[]{:S(2)}) copy-start(bf16[384,1536]{1,0:T(8,128)(2,1)} %refs_8_.3) | copy-start | bytes 3538948
  41.2 13.9 %collective-permute-start.8 = (bf16[512,384]{1,0:T(8,128)(2,1)S(1)}, bf16[512,384]{1,0:T(8,128)(2,1)S(1)}, u32[]{:S(2)}, u32[]{:S(2)}) collective-permute-start(bf16[512,384]{1,0:T(8,128)(2,1)S(1)} %shard_map.152.refs_1_.refs_0_), channel_id=1, source_target_pairs={{0,2},{1,3},{2,0},{3,1},{4,6},{5,7},{6,4},{7,5},{8,10},{9,11},{10,... | collective-permute-start | bytes 1179656 | tf_op jit(solution)/shard_map/ppermute | solution.py:26
  41.6 14.0 %collective-permute-start.14 = (bf16[512,384]{1,0:T(8,128)(2,1)S(1)}, bf16[512,384]{1,0:T(8,128)(2,1)S(1)}, u32[]{:S(2)}, u32[]{:S(2)}) collective-permute-start(bf16[512,384]{1,0:T(8,128)(2,1)S(1)} %collective-permute-done.3.refs_6_.refs_0_), channel_id=1, source_target_pairs={{0,1},{1,0},{2,3},{3,2},{4,5},{5,4},{6,7},{7,6},{8,9},{9,8},{10,11... | collective-permute-start | bytes 1179656 | tf_op jit(solution)/shard_map/ppermute | solution.py:26
  41.6 34.0 %collective-permute-start.20 = (bf16[384,1536]{1,0:T(8,128)(2,1)S(1)}, bf16[384,1536]{1,0:T(8,128)(2,1)S(1)}, u32[]{:S(2)}, u32[]{:S(2)}) collective-permute-start(bf16[384,1536]{1,0:T(8,128)(2,1)S(1)} %copy-done), channel_id=1, source_target_pairs={{0,1},{1,0},{2,3},{3,2},{4,5},{5,4},{6,7},{7,6},{8,9},{9,8},{10,11... | collective-permute-start | bytes 3538952 | tf_op jit(solution)/shard_map/ppermute | solution.py:26
  42.2 2.9 %copy-start.4 = (f32[32,384]{1,0:T(8,128)S(1)}, f32[32,384]{1,0:T(8,128)}, u32[]{:S(2)}) copy-start(f32[32,384]{1,0:T(8,128)} %copy-done.2) | copy-start | bytes 147460
  42.2 26.1 %collective-permute-start.19 = (bf16[192,1536]{1,0:T(8,128)(2,1)S(1)}, bf16[192,1536]{1,0:T(8,128)(2,1)S(1)}, u32[]{:S(2)}, u32[]{:S(2)}) collective-permute-start(bf16[192,1536]{1,0:T(8,128)(2,1)S(1)} %shard_map.165.refs_9_), channel_id=1, source_target_pairs={{0,16},{16,0},{1,17},{17,1},{2,18},{18,2},{3,19},{19,3},{4,20},{20... | collective-permute-start | bytes 1769480 | tf_op jit(solution)/shard_map/ppermute | solution.py:26
  47.5 8.3 %collective-permute-start.15 = (bf16[512,384]{1,0:T(8,128)(2,1)S(1)}, bf16[512,384]{1,0:T(8,128)(2,1)S(1)}, u32[]{:S(2)}, u32[]{:S(2)}) collective-permute-start(bf16[512,384]{1,0:T(8,128)(2,1)S(1)} %shard_map.154.refs_2_.refs_1_), channel_id=1, source_target_pairs={{0,1},{1,0},{2,3},{3,2},{4,5},{5,4},{6,7},{7,6},{8,9},{9,8},{10,11... | collective-permute-start | bytes 1179656 | tf_op jit(solution)/shard_map/ppermute | solution.py:26
  55.1 7.6 %collective-permute-start.12 = (bf16[512,384]{1,0:T(8,128)(2,1)S(1)}, bf16[512,384]{1,0:T(8,128)(2,1)S(1)}, u32[]{:S(2)}, u32[]{:S(2)}) collective-permute-start(bf16[512,384]{1,0:T(8,128)(2,1)S(1)} %shard_map.152.refs_1_.refs_0_), channel_id=1, source_target_pairs={{0,1},{1,0},{2,3},{3,2},{4,5},{5,4},{6,7},{7,6},{8,9},{9,8},{10,11... | collective-permute-start | bytes 1179656 | tf_op jit(solution)/shard_map/ppermute | solution.py:26
  55.7 7.1 %collective-permute-start.13 = (bf16[512,384]{1,0:T(8,128)(2,1)S(1)}, bf16[512,384]{1,0:T(8,128)(2,1)S(1)}, u32[]{:S(2)}, u32[]{:S(2)}) collective-permute-start(bf16[512,384]{1,0:T(8,128)(2,1)S(1)} %shard_map.158.refs_1_), channel_id=1, source_target_pairs={{0,1},{1,0},{2,3},{3,2},{4,5},{5,4},{6,7},{7,6},{8,9},{9,8},{10,11... | collective-permute-start | bytes 1179656 | tf_op jit(solution)/shard_map/ppermute | solution.py:26
  55.8 21.4 %collective-permute-start.21 = (bf16[192,1536]{1,0:T(8,128)(2,1)S(1)}, bf16[192,1536]{1,0:T(8,128)(2,1)S(1)}, u32[]{:S(2)}, u32[]{:S(2)}) collective-permute-start(bf16[192,1536]{1,0:T(8,128)(2,1)S(1)} %shard_map.165.refs_9_), channel_id=1, source_target_pairs={{0,1},{1,0},{2,3},{3,2},{4,5},{5,4},{6,7},{7,6},{8,9},{9,8},{10,11... | collective-permute-start | bytes 1769480 | tf_op jit(solution)/shard_map/ppermute | solution.py:26
  68.3 9.1 %collective-permute-start.22 = (bf16[192,1536]{1,0:T(8,128)(2,1)S(1)}, bf16[192,1536]{1,0:T(8,128)(2,1)S(1)}, u32[]{:S(2)}, u32[]{:S(2)}) collective-permute-start(bf16[192,1536]{1,0:T(8,128)(2,1)S(1)} %shard_map.166.refs_10_), channel_id=1, source_target_pairs={{0,1},{1,0},{2,3},{3,2},{4,5},{5,4},{6,7},{7,6},{8,9},{9,8},{10,11... | collective-permute-start | bytes 1769480 | tf_op jit(solution)/shard_map/ppermute | solution.py:26
  68.4 7.2 %collective-permute-start.16 = (bf16[256,384]{1,0:T(8,128)(2,1)S(1)}, bf16[256,384]{1,0:T(8,128)(2,1)S(1)}, u32[]{:S(2)}, u32[]{:S(2)}) collective-permute-start(bf16[256,384]{1,0:T(8,128)(2,1)S(1)} %shard_map.162.refs_1_.refs_0_), channel_id=1, source_target_pairs={{0,2},{1,3},{2,0},{3,1},{4,6},{5,7},{6,4},{7,5},{8,10},{9,11},{10,... | collective-permute-start | bytes 589832 | tf_op jit(solution)/shard_map/ppermute | solution.py:26
  72.0 5.4 %collective-permute-start.17 = (bf16[256,384]{1,0:T(8,128)(2,1)S(1)}, bf16[256,384]{1,0:T(8,128)(2,1)S(1)}, u32[]{:S(2)}, u32[]{:S(2)}) collective-permute-start(bf16[256,384]{1,0:T(8,128)(2,1)S(1)} %shard_map.162.refs_1_.refs_0_), channel_id=1, source_target_pairs={{0,1},{1,0},{2,3},{3,2},{4,5},{5,4},{6,7},{7,6},{8,9},{9,8},{10,11... | collective-permute-start | bytes 589832 | tf_op jit(solution)/shard_map/ppermute | solution.py:26
  75.7 1.7 %collective-permute-start.18 = (bf16[256,384]{1,0:T(8,128)(2,1)S(1)}, bf16[256,384]{1,0:T(8,128)(2,1)S(1)}, u32[]{:S(2)}, u32[]{:S(2)}) collective-permute-start(bf16[256,384]{1,0:T(8,128)(2,1)S(1)} %shard_map.164.refs_1_), channel_id=1, source_target_pairs={{0,1},{1,0},{2,3},{3,2},{4,5},{5,4},{6,7},{7,6},{8,9},{9,8},{10,11... | collective-permute-start | bytes 589832 | tf_op jit(solution)/shard_map/ppermute | solution.py:26
  75.7 7.3 %collective-permute-start.23 = (bf16[256,384]{1,0:T(8,128)(2,1)S(1)}, bf16[256,384]{1,0:T(8,128)(2,1)S(1)}, u32[]{:S(2)}, u32[]{:S(2)}) collective-permute-start(bf16[256,384]{1,0:T(8,128)(2,1)S(1)} %shard_map.163.refs_1_.refs_0_), channel_id=1, source_target_pairs={{0,2},{1,3},{2,0},{3,1},{4,6},{5,7},{6,4},{7,5},{8,10},{9,11},{10,... | collective-permute-start | bytes 589832 | tf_op jit(solution)/shard_map/ppermute | solution.py:26
  77.2 10.5 %collective-permute-start.24 = (bf16[256,384]{1,0:T(8,128)(2,1)S(1)}, bf16[256,384]{1,0:T(8,128)(2,1)S(1)}, u32[]{:S(2)}, u32[]{:S(2)}) collective-permute-start(bf16[256,384]{1,0:T(8,128)(2,1)S(1)} %shard_map.163.refs_1_.refs_0_), channel_id=1, source_target_pairs={{0,1},{1,0},{2,3},{3,2},{4,5},{5,4},{6,7},{7,6},{8,9},{9,8},{10,11... | collective-permute-start | bytes 589832 | tf_op jit(solution)/shard_map/ppermute | solution.py:26
  77.4 5.6 %copy-start.6 = (f32[384]{0:T(512)S(1)}, f32[384]{0:T(512)}, u32[]{:S(2)}) copy-start(f32[384]{0:T(512)} %param.28) | copy-start | bytes 4612
  77.4 5.6 %copy-start.7 = (f32[384]{0:T(512)S(1)}, f32[384]{0:T(512)}, u32[]{:S(2)}) copy-start(f32[384]{0:T(512)} %param.27) | copy-start | bytes 4612
  83.0 4.7 %collective-permute-start.25 = (bf16[256,384]{1,0:T(8,128)(2,1)S(1)}, bf16[256,384]{1,0:T(8,128)(2,1)S(1)}, u32[]{:S(2)}, u32[]{:S(2)}) collective-permute-start(bf16[256,384]{1,0:T(8,128)(2,1)S(1)} %shard_map.168.refs_1_), channel_id=1, source_target_pairs={{0,1},{1,0},{2,3},{3,2},{4,5},{5,4},{6,7},{7,6},{8,9},{9,8},{10,11... | collective-permute-start | bytes 589832 | tf_op jit(solution)/shard_map/ppermute | solution.py:26
  83.0 7.8 %collective-permute-start.26 = (bf16[16,384]{1,0:T(8,128)(2,1)S(1)}, bf16[16,384]{1,0:T(8,128)(2,1)S(1)}, u32[]{:S(2)}, u32[]{:S(2)}) collective-permute-start(bf16[16,384]{1,0:T(8,128)(2,1)S(1)} %get-tuple-element.54), channel_id=1, source_target_pairs={{0,4},{4,8},{8,12},{1,5},{5,9},{9,13},{2,6},{6,10},{10,14},{3,7},{... | collective-permute-start | bytes 36872 | tf_op jit(solution)/shard_map/ppermute | solution.py:542
  86.4 5.6 %collective-permute-start.27 = (bf16[16,384]{1,0:T(8,128)(2,1)S(1)}, bf16[16,384]{1,0:T(8,128)(2,1)S(1)}, u32[]{:S(2)}, u32[]{:S(2)}) collective-permute-start(bf16[16,384]{1,0:T(8,128)(2,1)S(1)} %get-tuple-element.55), channel_id=1, source_target_pairs={{4,0},{8,4},{12,8},{5,1},{9,5},{13,9},{6,2},{10,6},{14,10},{7,3},{... | collective-permute-start | bytes 36872 | tf_op jit(solution)/shard_map/ppermute | solution.py:543
  87.7 4.3 %copy-start.5 = (f32[31,384]{1,0:T(8,128)S(1)}, f32[31,384]{1,0:T(8,128)}, u32[]{:S(2)}) copy-start(f32[31,384]{1,0:T(8,128)} %refs_0_.9) | copy-start | bytes 142852
  93.6 2.7 %collective-permute-start.28 = (bf16[256,768]{1,0:T(8,128)(2,1)S(1)}, bf16[256,768]{1,0:T(8,128)(2,1)S(1)}, u32[]{:S(2)}, u32[]{:S(2)}) collective-permute-start(bf16[256,768]{1,0:T(8,128)(2,1)S(1)} %get-tuple-element.57), channel_id=1, source_target_pairs={{0,1},{1,0},{2,3},{3,2},{4,5},{5,4},{6,7},{7,6},{8,9},{9,8},{10,11... | collective-permute-start | bytes 1179656 | tf_op jit(solution)/shard_map/ppermute | solution.py:26
  95.7 2.2 %collective-permute-start.30 = (bf16[256,768]{1,0:T(8,128)(2,1)S(1)}, bf16[256,768]{1,0:T(8,128)(2,1)S(1)}, u32[]{:S(2)}, u32[]{:S(2)}) collective-permute-start(bf16[256,768]{1,0:T(8,128)(2,1)S(1)} %get-tuple-element.60), channel_id=1, source_target_pairs={{0,1},{1,0},{2,3},{3,2},{4,5},{5,4},{6,7},{7,6},{8,9},{9,8},{10,11... | collective-permute-start | bytes 1179656 | tf_op jit(solution)/shard_map/ppermute | solution.py:26
  96.3 7.8 %collective-permute-start.29 = (bf16[256,384]{1,0:T(8,128)(2,1)S(1)}, bf16[256,384]{1,0:T(8,128)(2,1)S(1)}, u32[]{:S(2)}, u32[]{:S(2)}) collective-permute-start(bf16[256,384]{1,0:T(8,128)(2,1)S(1)} %add_convert_fusion.3), channel_id=1, source_target_pairs={{0,2},{1,3},{2,0},{3,1},{4,6},{5,7},{6,4},{7,5},{8,10},{9,11},{10,... | collective-permute-start | bytes 589832 | tf_op jit(solution)/shard_map/ppermute | solution.py:26
  98.0 9.5 %collective-permute-start.31 = (bf16[256,384]{1,0:T(8,128)(2,1)S(1)}, bf16[256,384]{1,0:T(8,128)(2,1)S(1)}, u32[]{:S(2)}, u32[]{:S(2)}) collective-permute-start(bf16[256,384]{1,0:T(8,128)(2,1)S(1)} %add_convert_fusion.1), channel_id=1, source_target_pairs={{0,2},{1,3},{2,0},{3,1},{4,6},{5,7},{6,4},{7,5},{8,10},{9,11},{10,... | collective-permute-start | bytes 589832 | tf_op jit(solution)/shard_map/ppermute | solution.py:26

commit v5 on v4

--- a/solution.py
+++ b/solution.py
@@ -200,43 +200,32 @@
             query_ref[:, base + PAIR : base + 2 * PAIR] = jnp.where(low, 0.0, queries).astype(BF16)
 
 
-def chunks_of(spans, rows):
-    pieces, local = [], 0
-    for start, size in spans:
-        step = math.gcd(size, rows)
-        for offset in range(0, size, step):
-            pieces.append((slice(start + offset, start + offset + step), slice(local, local + step)))
-            local += step
-    return pieces
-
-
-def attend_pair(pair, chunks, query_ref, keys, values, state_ref):
-    for source, rows in chunks:
-        for head in range(2):
-            index = 2 * pair + head
-            queries = query_ref[source, index * PAIR : (index + 1) * PAIR]
-            scores = lax.dot_general(
-                queries, keys, (((1,), (1,)), ((), ())), preferred_element_type=F32
-            )
-            peak = jnp.max(scores, axis=1, keepdims=True)
-            soft = jnp.exp2(scores - peak).astype(BF16)
-            sums = jnp.dot(soft, values[head], preferred_element_type=F32)
-            state_ref[rows, 2 * index * PAIR : (2 * index + 1) * PAIR] = sums
-            state_ref[rows, (2 * index + 1) * PAIR : (2 * index + 2) * PAIR] = jnp.broadcast_to(
-                peak, (peak.shape[0], PAIR)
-            )
-
-
-def merge_head(old_ref, part_ref, source, rows, index):
+def rows_of(ref, spans, cols):
+    return jnp.concatenate([ref[start : start + size, cols] for start, size in spans], axis=0)
+
+
+def attend_pair(pair, spans, query_ref, keys, values, state_ref):
+    for head in range(2):
+        index = 2 * pair + head
+        queries = rows_of(query_ref, spans, slice(index * PAIR, (index + 1) * PAIR))
+        scores = lax.dot_general(queries, keys, (((1,), (1,)), ((), ())), preferred_element_type=F32)
+        peak = jnp.max(scores, axis=1, keepdims=True)
+        soft = jnp.exp2(scores - peak).astype(BF16)
+        sums = jnp.dot(soft, values[head], preferred_element_type=F32)
+        state_ref[:, 2 * index * PAIR : (2 * index + 1) * PAIR] = sums
+        state_ref[:, (2 * index + 1) * PAIR : (2 * index + 2) * PAIR] = jnp.broadcast_to(peak, (peak.shape[0], PAIR))
+
+
+def merge_head(old_ref, part_ref, spans, index):
     sums = slice(2 * index * PAIR, (2 * index + 1) * PAIR)
     peaks = slice((2 * index + 1) * PAIR, (2 * index + 2) * PAIR)
-    old_peak, part_peak = old_ref[source, peaks], part_ref[rows, peaks]
+    old_peak, part_peak = rows_of(old_ref, spans, peaks), part_ref[:, peaks]
     peak = jnp.maximum(old_peak, part_peak)
-    total = old_ref[source, sums] * jnp.exp2(old_peak - peak) + part_ref[rows, sums] * jnp.exp2(part_peak - peak)
+    total = rows_of(old_ref, spans, sums) * jnp.exp2(old_peak - peak) + part_ref[:, sums] * jnp.exp2(part_peak - peak)
     return total, peak
 
 
-def attend_kernel(first, last, chunks, query_ref, key_ref, value_ref, *refs):
+def attend_kernel(first, last, spans, query_ref, key_ref, value_ref, *refs):
     if last:
         old_ref, attended, part = refs[0], refs[-2], refs[-1]
     elif first:
@@ -248,23 +237,22 @@
     pairs = query_ref.shape[1] // (2 * PAIR)
     for j in range(pairs):
         values = [value_ref[:, n * PAIR : (n + 1) * PAIR] for n in (2 * j, 2 * j + 1)]
-        attend_pair(j, chunks, query_ref, key_ref[:, j * PAIR : (j + 1) * PAIR], values, part)
+        attend_pair(j, spans, query_ref, key_ref[:, j * PAIR : (j + 1) * PAIR], values, part)
     if first:
         return
     low = lane_masks()
-    for source, rows in chunks:
-        for j in range(pairs):
-            heads = [merge_head(old_ref, part, source, rows, 2 * j + head) for head in range(2)]
-            if last:
-                (one, _), (two, _) = heads
-                both = jnp.where(low, one, two)
-                weight = pltpu.roll(jnp.where(low, two, one), HEAD_DIM, 1)
-                attended[rows, j * PAIR : (j + 1) * PAIR] = (both / weight).astype(BF16)
-            else:
-                for head, (sums, peak) in enumerate(heads):
-                    at = 2 * (2 * j + head) * PAIR
-                    state_ref[rows, at : at + PAIR] = sums
-                    state_ref[rows, at + PAIR : at + 2 * PAIR] = peak
+    for j in range(pairs):
+        heads = [merge_head(old_ref, part, spans, 2 * j + head) for head in range(2)]
+        if last:
+            (one, _), (two, _) = heads
+            both = jnp.where(low, one, two)
+            weight = pltpu.roll(jnp.where(low, two, one), HEAD_DIM, 1)
+            attended[:, j * PAIR : (j + 1) * PAIR] = (both / weight).astype(BF16)
+        else:
+            for head, (sums, peak) in enumerate(heads):
+                at = 2 * (2 * j + head) * PAIR
+                state_ref[:, at : at + PAIR] = sums
+                state_ref[:, at + PAIR : at + 2 * PAIR] = peak
 
 
 def middle_kernel(count, order, spans, me_ref, part_ref, *refs):
@@ -394,7 +382,7 @@
     place = me.astype(jnp.int32).reshape(1)
     order = list(range(0, grid, CORES)) + list(range(1, grid, CORES))
     padded = -(-width // PAIR) * PAIR
-    query_rows, every = 256, ((0, frames),)
+    every = ((0, frames),)
 
     def by_distance(cells):
         return jnp.concatenate(
@@ -438,7 +426,7 @@
     taps = pad_columns(depth_kernel, padded)
     bn = pad_columns(jnp.stack([bn_scale, bn_shift]), padded)
     qkv, qkv_sums = folded(place, order, 0, gains, (w_key, w_value, w_query))
-    chips[0] = [after(block, gains) for block in chips[0]]
+    chips[0] = [after(block, qkv_sums) for block in chips[0]]
     glu, glu_sums = folded(place, order, 2, gains, (w_glu_value, w_glu_gate))
 
     parts = lax.axis_size("parts")
@@ -461,7 +449,7 @@
     own = [frames_in] + chips[0]
     own_blocks = own + other_core(own)
     n = len(own_blocks)
-    early = [*[raw[s] for s in raw if s], *crossed, *chips[1]]
+    early = [*[raw[s] for s in raw if s], glu_sums, w_p]
     queries, keys, values = kernel_call(
         functools.partial(project_kernel, n, True),
         [wide, narrow, wide],
@@ -477,13 +465,14 @@
 
     prepare(2, None)
     state, token = kernel_call(
-        functools.partial(attend_kernel, True, False, chunks_of(every, query_rows)),
+        functools.partial(attend_kernel, True, False, every),
         [state_shape, token_shape],
-        [queries, keys, values],
+        [queries, keys, values, *crossed],
+        spaces={3 + i: pl.ANY for i in range(len(crossed))},
     )
     crossed = [after(block, token) for block in crossed]
     swapped = [exchange(block, "parts", 1) for block in crossed] if parts == 2 else []
-    moved = {1: chips[1]}
+    moved = {1: [after(block, token) for block in chips[1]]}
     for s in range(1, ctx):
         last = s == ctx - 1
         mine = [raw[s]] + moved[s]
@@ -497,9 +486,9 @@
         prepare(s + 2, token)
         moved[s + 1] = [after(block, token) for block in chips[s + 1]]
         behind = [raw[s + 2]] if s + 2 < ctx else []
-        behind += moved[s + 1] + ([glu_sums, w_p] if s == 1 else [])
+        behind += moved[s + 1]
         state, token = kernel_call(
-            functools.partial(attend_kernel, False, False, chunks_of(every, query_rows)),
+            functools.partial(attend_kernel, False, False, every),
             [state_shape, token_shape],
             [queries, keys, values, state, *behind],
             spaces={4 + i: pl.ANY for i in range(len(behind))},
@@ -511,7 +500,7 @@
     attended = []
     for h in range(2):
         (mine,) = kernel_call(
-            functools.partial(attend_kernel, False, True, chunks_of(spans[h], query_rows)),
+            functools.partial(attend_kernel, False, True, spans[h]),
             [((rows, padded), BF16)],
             [queries, keys, values, state],
             scratch=[pltpu.VMEM((rows, 4 * padded), F32)],

time: 109 us -> 103 us (0.945)
  Pallas kernels: 46.3 us -> 40.5 us
  waiting for transfers between devices: 27.5 us -> 32.5 us
  starting transfers between devices: 26.4 us -> 22.5 us
  local copies, waits for them, and re-layouts: 1.47 us -> 0.05 us
    pallas_call x18, Pallas kernels: 46.3 us -> 40.5 us  [kernel_call(): pl.pallas_call(body, in_specs=in_specs, out_specs=tuple((pl.BlockSpec(mem...]
    ppermute x30, waiting for transfers between devices: 26.4 us -> 31.5 us  [exchange(): return lax.ppermute(cells, axis, [(i, i ^ distance) for i in range(count)])]
    ppermute x30, starting transfers between devices: 21.8 us -> 18.1 us  [exchange(): return lax.ppermute(cells, axis, [(i, i ^ distance) for i in range(count)])]
    unnamed x16 -> x10, local copies, waits for them, and re-layouts: 1.45 us -> 0.03 us
  transfers between devices with their start and end apart: 32 -> 32, of which waited for: 8 -> 11; matrix products, arithmetic and copies ran while one was open for 0% -> 0% of each run, Pallas kernels for 41% -> 38%
where the time goes in v5:
time: 103 us; the launch traced here: 102 us
  Pallas kernels  40.5 us (39%)
  waiting for transfers between devices  32.5 us (32%)
  starting transfers between devices  22.5 us (22%)
  blocking collectives  5.23 us (5%)
  other arithmetic  1.12 us (1%)
    pallas_call x18, Pallas kernels, kernel_call(): pl.pallas_call(body, in_specs=in_specs, out_specs=tuple((pl.BlockSpec(mem...  40.5 us
    ppermute x30, waiting for transfers between devices, exchange(): return lax.ppermute(cells, axis, [(i, i ^ distance) for i in range(count)])  31.5 us
    ppermute x30, starting transfers between devices, exchange(): return lax.ppermute(cells, axis, [(i, i ^ distance) for i in range(count)])  18.1 us
    all_gather x1, blocking collectives, on_device(): gains = lax.all_gather(gains, 'grid', axis=0, tiled=True)  5.23 us
    ppermute x1, starting transfers between devices, on_device(): left = lax.ppermute(results[3], 'ctx', [(i, i + 1) for i in range(ctx - 1)])  3.09 us
  transfers between devices with their start and end apart: 32, of which 11 were waited for; matrix products, arithmetic and copies ran while one was open for 0% of the time, Pallas kernels for 38%

profile of v5, /device:TPU:0, one launch (start us, length us, event | category | flops | bytes accessed | tf_op | source)
XLA Modules:
  0.0 102.3 jit_solution(13858446971394008983)
XLA Ops:
  0.0 2.9 %collective-permute-start = (bf16[512,384]{1,0:T(8,128)(2,1)}, bf16[512,384]{1,0:T(8,128)(2,1)S(1)}, u32[]{:S(2)}, u32[]{:S(2)}) collective-permute-start(bf16[512,384]{1,0:T(8,128)(2,1)} %refs_4_.3), channel_id=1, source_target_pairs={{0,2},{1,3},{2,0},{3,1},{4,6},{5,7},{6,4},{7,5},{8,10},{9,11},{10,... | collective-permute-start | bytes 1179656 | tf_op jit(solution)/shard_map/ppermute | solution.py:26
  2.9 2.6 %collective-permute-start.3 = (bf16[512,384]{1,0:T(8,128)(2,1)}, bf16[512,384]{1,0:T(8,128)(2,1)S(1)}, u32[]{:S(2)}, u32[]{:S(2)}) collective-permute-start(bf16[512,384]{1,0:T(8,128)(2,1)} %refs_4_.3), channel_id=1, source_target_pairs={{0,8},{4,12},{8,0},{12,4},{1,9},{5,13},{9,1},{13,5},{2,10},{6,14},... | collective-permute-start | bytes 1179656 | tf_op jit(solution)/shard_map/ppermute | solution.py:26
  5.5 1.6 %collective-permute-start.4 = (bf16[512,384]{1,0:T(8,128)(2,1)}, bf16[512,384]{1,0:T(8,128)(2,1)S(1)}, u32[]{:S(2)}, u32[]{:S(2)}) collective-permute-start(bf16[512,384]{1,0:T(8,128)(2,1)} %refs_4_.3), channel_id=1, source_target_pairs={{0,4},{4,0},{8,12},{12,8},{1,5},{5,1},{9,13},{13,9},{2,6},{6,2},{1... | collective-permute-start | bytes 1179656 | tf_op jit(solution)/shard_map/ppermute | solution.py:26
  7.1 1.1 %shard_map.151.refs_0_ = bf16[192,1536]{1,0:T(8,128)(2,1)S(1)} custom-call(s32[1]{0:T(128)} %bitcast.1.part_ref, bf16[384,1536]{1,0:T(8,128)(2,1)} %refs_8_.3), custom_call_target="tpu_custom_call" | custom-call | flops 1000 | bytes 1000 | tf_op jit(solution)/shard_map/pallas_call | solution.py:38
  8.2 0.8 shard_map.145
  9.0 5.2 %all_gather.3.gains_ref = f32[32,384]{1,0:T(8,128)S(1)} all-gather(f32[8,384]{1,0:T(8,128)S(1)} %shard_map.145), channel_id=1, replica_groups=mesh['parts'=2,'ctx'=4,'grid'=4] {'grid'}, dimensions={0}, use_global_device_ids=true | all-gather | bytes 61440 | tf_op jit(solution)/shard_map/all_gather | solution.py:406
  14.2 3.0 %shard_map.146 = (bf16[1536,1152]{1,0:T(8,128)(2,1)S(1)}, f32[2,1152]{1,0:T(2,128)S(1)}) custom-call(s32[1]{0:T(128)} %bitcast.me_ref, f32[32,384]{1,0:T(8,128)S(1)} %all_gather.3.gains_ref, bf16[1536,384]{1,0:T(8,128)(2,1)} %refs_0_.6, bf16[1536,384]{1,0:T(8,128)(2,1)} %refs_1_.4, bf16[1536,384]{1,0:T(8,128)(2,1)} %refs_2_.4), custom_call_target="tpu_custom_call" | custom-call | flops 1000 | bytes 1000 | tf_op jit(solution)/shard_map/pallas_call | solution.py:38
  17.2 1.0 collective-permute-start.6
  18.2 1.6 %collective-permute-start.8 = (bf16[512,384]{1,0:T(8,128)(2,1)S(1)}, bf16[512,384]{1,0:T(8,128)(2,1)S(1)}, u32[]{:S(2)}, u32[]{:S(2)}) collective-permute-start(bf16[512,384]{1,0:T(8,128)(2,1)S(1)} %shard_map.147.refs_1_.refs_5_), channel_id=1, source_target_pairs={{0,4},{4,0},{8,12},{12,8},{1,5},{5,1},{9,13},{13,9},{2,6},{6,2},{1... | collective-permute-start | bytes 1179656 | tf_op jit(solution)/shard_map/ppermute | solution.py:26
  19.8 4.3 %collective-permute-done.3.refs_6_.refs_0_ = bf16[512,384]{1,0:T(8,128)(2,1)S(1)} collective-permute-done((bf16[512,384]{1,0:T(8,128)(2,1)}, bf16[512,384]{1,0:T(8,128)(2,1)S(1)}, u32[]{:S(2)}, u32[]{:S(2)}) %collective-permute-start.3) | collective-permute-done | bytes 393248 | tf_op jit(solution)/shard_map/ppermute | solution.py:26
  24.1 0.7 collective-permute-start.5
  24.8 0.6 collective-permute-start.11
  25.4 1.3 %shard_map.149.refs_9_.refs_4_.refs_2_ = bf16[384,1536]{1,0:T(8,128)(2,1)S(1)} custom-call(s32[1]{0:T(128)} %bitcast.me_ref, bf16[384,1536]{1,0:T(8,128)(2,1)} %source_ref.2), custom_call_target="tpu_custom_call" | custom-call | flops 1000 | bytes 1000 | tf_op jit(solution)/shard_map/pallas_call | solution.py:38
  26.7 2.5 %shard_map.148 = (bf16[1536,768]{1,0:T(8,128)(2,1)S(1)}, f32[2,768]{1,0:T(2,128)S(1)}) custom-call(s32[1]{0:T(128)} %bitcast.me_ref, f32[32,384]{1,0:T(8,128)S(1)} %all_gather.3.gains_ref, bf16[1536,384]{1,0:T(8,128)(2,1)} %refs_0_.7, bf16[1536,384]{1,0:T(8,128)(2,1)} %refs_1_.5), custom_call_target="tpu_custom_call" | custom-call | flops 1000 | bytes 1000 | tf_op jit(solution)/shard_map/pallas_call | solution.py:38
  29.2 3.0 %shard_map.150 = (bf16[512,768]{1,0:T(8,128)(2,1)S(1)}, bf16[512,384]{1,0:T(8,128)(2,1)S(1)}, bf16[512,768]{1,0:T(8,128)(2,1)S(1)}) custom-call(bf16[512,384]{1,0:T(8,128)(2,1)S(1)} %copy-done.1, bf16[512,384]{1,0:T(8,128)(2,1)S(1)} %shard_map.147.refs_1_.refs_5_, bf16[512,384]{1,0:T(8,128)(2,1)S(1)} %collective-permute-done.1.refs_2_.refs_6_, ...), custom_call_target="tpu_custom_call" | custom-call | flops 1000 | bytes 1000 | tf_op jit(solution)/shard_map/pallas_call | solution.py:38
  32.2 1.2 %collective-permute-done.6.refs_0_ = bf16[192,1536]{1,0:T(8,128)(2,1)S(1)} collective-permute-done((bf16[192,1536]{1,0:T(8,128)(2,1)S(1)}, bf16[192,1536]{1,0:T(8,128)(2,1)S(1)}, u32[]{:S(2)}, u32[]{:S(2)}) %collective-permute-start.6) | collective-permute-done | bytes 589856 | tf_op jit(solution)/shard_map/ppermute | solution.py:26
  33.4 2.2 %shard_map.153 = (f32[512,1536]{1,0:T(8,128)S(1)}, f32[8,128]{1,0:T(8,128)S(1)}) custom-call(bf16[512,768]{1,0:T(8,128)(2,1)S(1)} %get-tuple-element.36.query_ref, bf16[512,384]{1,0:T(8,128)(2,1)S(1)} %get-tuple-element.37.key_ref, bf16[512,768]{1,0:T(8,128)(2,1)S(1)} %get-tuple-element.38.value_ref, bf16[192,1536]{1,0:T(8,128)(2,1)S(1)} %collective-permute-done.6.refs_0_), custom_call_target="tpu_custom_call" | custom-call | flops 1000 | bytes 1000 | tf_op jit(solution)/shard_map/pallas_call | solution.py:38
  35.7 5.4 %collective-permute-done.5.refs_0_ = bf16[512,384]{1,0:T(8,128)(2,1)S(1)} collective-permute-done((bf16[512,384]{1,0:T(8,128)(2,1)S(1)}, bf16[512,384]{1,0:T(8,128)(2,1)S(1)}, u32[]{:S(2)}, u32[]{:S(2)}) %collective-permute-start.5) | collective-permute-done | bytes 393248 | tf_op jit(solution)/shard_map/ppermute | solution.py:26
  41.6 0.5 collective-permute-start.20
  42.2 1.6 %collective-permute-start.19 = (bf16[192,1536]{1,0:T(8,128)(2,1)S(1)}, bf16[192,1536]{1,0:T(8,128)(2,1)S(1)}, u32[]{:S(2)}, u32[]{:S(2)}) collective-permute-start(bf16[192,1536]{1,0:T(8,128)(2,1)S(1)} %shard_map.166.refs_9_), channel_id=1, source_target_pairs={{0,16},{16,0},{1,17},{17,1},{2,18},{18,2},{3,19},{19,3},{4,20},{20... | collective-permute-start | bytes 1769480 | tf_op jit(solution)/shard_map/ppermute | solution.py:26
  43.7 1.9 %shard_map.156 = (bf16[512,384]{1,0:T(8,128)(2,1)S(1)}, bf16[512,768]{1,0:T(8,128)(2,1)S(1)}) custom-call(bf16[512,384]{1,0:T(8,128)(2,1)S(1)} %collective-permute-done.4.refs_7_.refs_0_, bf16[512,384]{1,0:T(8,128)(2,1)S(1)} %shard_map.155.refs_1_, bf16[512,384]{1,0:T(8,128)(2,1)S(1)} %collective-permute-done.9.refs_2_, ...), custom_call_target="tpu_custom_call" | custom-call | flops 1000 | bytes 1000 | tf_op jit(solution)/shard_map/pallas_call | solution.py:38
  45.6 3.7 %shard_map.158 = (f32[512,1536]{1,0:T(8,128)S(1)}, f32[8,128]{1,0:T(8,128)S(1)}) custom-call(bf16[512,768]{1,0:T(8,128)(2,1)S(1)} %get-tuple-element.36.query_ref, bf16[512,384]{1,0:T(8,128)(2,1)S(1)} %get-tuple-element.40.key_ref, bf16[512,768]{1,0:T(8,128)(2,1)S(1)} %get-tuple-element.41.value_ref, ...), custom_call_target="tpu_custom_call", output_to_operand_aliasing={{0}: (3, {})} | custom-call | flops 1000 | bytes 1000 | tf_op jit(solution)/shard_map/pallas_call | solution.py:38
  49.3 2.8 %collective-permute-done.7.refs_0_ = bf16[512,384]{1,0:T(8,128)(2,1)S(1)} collective-permute-done((bf16[512,384]{1,0:T(8,128)(2,1)S(1)}, bf16[512,384]{1,0:T(8,128)(2,1)S(1)}, u32[]{:S(2)}, u32[]{:S(2)}) %collective-permute-start.7) | collective-permute-done | bytes 393248 | tf_op jit(solution)/shard_map/ppermute | solution.py:26
  52.2 0.5 collective-permute-start.13
  52.7 1.9 %shard_map.161 = (bf16[512,384]{1,0:T(8,128)(2,1)S(1)}, bf16[512,768]{1,0:T(8,128)(2,1)S(1)}) custom-call(bf16[512,384]{1,0:T(8,128)(2,1)S(1)} %collective-permute-done.3.refs_6_.refs_0_, bf16[512,384]{1,0:T(8,128)(2,1)S(1)} %shard_map.157.refs_2_.refs_1_, bf16[512,384]{1,0:T(8,128)(2,1)S(1)} %collective-permute-done.14.refs_2_, ...), custom_call_target="tpu_custom_call" | custom-call | flops 1000 | bytes 1000 | tf_op jit(solution)/shard_map/pallas_call | solution.py:38
  54.6 3.9 %shard_map.162 = (f32[512,1536]{1,0:T(8,128)S(1)}, f32[8,128]{1,0:T(8,128)}) custom-call(bf16[512,768]{1,0:T(8,128)(2,1)S(1)} %get-tuple-element.36.query_ref, bf16[512,384]{1,0:T(8,128)(2,1)S(1)} %get-tuple-element.46.key_ref, bf16[512,768]{1,0:T(8,128)(2,1)S(1)} %get-tuple-element.47.value_ref, ...), custom_call_target="tpu_custom_call", output_to_operand_aliasing={{0}: (3, {})} | custom-call | flops 1000 | bytes 1000 | tf_op jit(solution)/shard_map/pallas_call | solution.py:38
  58.5 1.9 %shard_map.160 = (bf16[512,384]{1,0:T(8,128)(2,1)S(1)}, bf16[512,768]{1,0:T(8,128)(2,1)S(1)}) custom-call(bf16[512,384]{1,0:T(8,128)(2,1)S(1)} %shard_map.154.refs_1_.refs_0_, bf16[512,384]{1,0:T(8,128)(2,1)S(1)} %shard_map.159.refs_1_, bf16[512,384]{1,0:T(8,128)(2,1)S(1)} %collective-permute-done.12.refs_2_, ...), custom_call_target="tpu_custom_call" | custom-call | flops 1000 | bytes 1000 | tf_op jit(solution)/shard_map/pallas_call | solution.py:38
  60.4 2.1 %shard_map.163.refs_1_.refs_0_ = bf16[256,384]{1,0:T(8,128)(2,1)S(1)} custom-call(bf16[512,768]{1,0:T(8,128)(2,1)S(1)} %get-tuple-element.36.query_ref, bf16[512,384]{1,0:T(8,128)(2,1)S(1)} %get-tuple-element.44.key_ref, bf16[512,768]{1,0:T(8,128)(2,1)S(1)} %get-tuple-element.45.value_ref, f32[512,1536]{1,0:T(8,128)S(1)} %get-tuple-element.49.refs_0_), custom_call_target="tpu_custom_call" | custom-call | flops 1000 | bytes 1000 | tf_op jit(solution)/shard_map/pallas_call | solution.py:38
  62.5 0.5 collective-permute-start.22
  63.5 2.1 %shard_map.164.refs_1_.refs_0_ = bf16[256,384]{1,0:T(8,128)(2,1)S(1)} custom-call(bf16[512,768]{1,0:T(8,128)(2,1)S(1)} %get-tuple-element.36.query_ref, bf16[512,384]{1,0:T(8,128)(2,1)S(1)} %get-tuple-element.44.key_ref, bf16[512,768]{1,0:T(8,128)(2,1)S(1)} %get-tuple-element.45.value_ref, f32[512,1536]{1,0:T(8,128)S(1)} %get-tuple-element.49.refs_0_), custom_call_target="tpu_custom_call" | custom-call | flops 1000 | bytes 1000 | tf_op jit(solution)/shard_map/pallas_call | solution.py:38
  65.7 4.2 %collective-permute-done.16.refs_0_ = bf16[256,384]{1,0:T(8,128)(2,1)S(1)} collective-permute-done((bf16[256,384]{1,0:T(8,128)(2,1)S(1)}, bf16[256,384]{1,0:T(8,128)(2,1)S(1)}, u32[]{:S(2)}, u32[]{:S(2)}) %collective-permute-start.16) | collective-permute-done | bytes 196640 | tf_op jit(solution)/shard_map/ppermute | solution.py:26
  69.9 0.5 collective-permute-start.23
  70.6 0.7 collective-permute-done.18.refs_3_
  71.3 2.5 %shard_map.168 = (bf16[256,384]{1,0:T(8,128)(2,1)S(1)}, bf16[256,384]{1,0:T(8,128)(2,1)S(1)}, bf16[16,384]{1,0:T(8,128)(2,1)S(1)}, bf16[16,384]{1,0:T(8,128)(2,1)S(1)}) custom-call(s32[1]{0:T(128)} %bitcast.me_ref, s32[1]{0:T(128)} %bitcast.1.part_ref, bf16[256,384]{1,0:T(8,128)(2,1)S(1)} %shard_map.163.refs_1_.refs_0_, ...), custom_call_target="tpu_custom_call" | custom-call | flops 1000 | bytes 1000 | tf_op jit(solution)/shard_map/pallas_call | solution.py:38
  73.9 3.3 %collective-permute-done.23.refs_0_ = bf16[256,384]{1,0:T(8,128)(2,1)S(1)} collective-permute-done((bf16[256,384]{1,0:T(8,128)(2,1)S(1)}, bf16[256,384]{1,0:T(8,128)(2,1)S(1)}, u32[]{:S(2)}, u32[]{:S(2)}) %collective-permute-start.23) | collective-permute-done | bytes 196640 | tf_op jit(solution)/shard_map/ppermute | solution.py:26
  77.2 3.1 %collective-permute-start.26 = (bf16[16,384]{1,0:T(8,128)(2,1)S(1)}, bf16[16,384]{1,0:T(8,128)(2,1)S(1)}, u32[]{:S(2)}, u32[]{:S(2)}) collective-permute-start(bf16[16,384]{1,0:T(8,128)(2,1)S(1)} %get-tuple-element.54), channel_id=1, source_target_pairs={{0,4},{4,8},{8,12},{1,5},{5,9},{9,13},{2,6},{6,10},{10,14},{3,7},{... | collective-permute-start | bytes 36872 | tf_op jit(solution)/shard_map/ppermute | solution.py:531
  80.3 1.3 %collective-permute-start.27 = (bf16[16,384]{1,0:T(8,128)(2,1)S(1)}, bf16[16,384]{1,0:T(8,128)(2,1)S(1)}, u32[]{:S(2)}, u32[]{:S(2)}) collective-permute-start(bf16[16,384]{1,0:T(8,128)(2,1)S(1)} %get-tuple-element.55), channel_id=1, source_target_pairs={{4,0},{8,4},{12,8},{5,1},{9,5},{13,9},{6,2},{10,6},{14,10},{7,3},{... | collective-permute-start | bytes 36872 | tf_op jit(solution)/shard_map/ppermute | solution.py:532
  81.7 3.2 %shard_map.170 = (bf16[256,384]{1,0:T(8,128)(2,1)S(1)}, bf16[256,384]{1,0:T(8,128)(2,1)S(1)}, bf16[16,384]{1,0:T(8,128)(2,1)}, bf16[16,384]{1,0:T(8,128)(2,1)}) custom-call(s32[1]{0:T(128)} %bitcast.me_ref, s32[1]{0:T(128)} %bitcast.1.part_ref, bf16[256,384]{1,0:T(8,128)(2,1)S(1)} %shard_map.164.refs_1_.refs_0_, bf16[256,384]{1,0:T(8,128)(2,1)S(1)} %shard_map.169.refs_1_, ...), custom_call_target="tpu_custom_call" | custom-call | flops 1000 | bytes 1000 | tf_op jit(solution)/shard_map/pallas_call | solution.py:38
  84.9 1.1 %collective-permute-done.27.refs_1_ = bf16[16,384]{1,0:T(8,128)(2,1)S(1)} collective-permute-done((bf16[16,384]{1,0:T(8,128)(2,1)S(1)}, bf16[16,384]{1,0:T(8,128)(2,1)S(1)}, u32[]{:S(2)}, u32[]{:S(2)}) %collective-permute-start.27) | collective-permute-done | bytes 12320 | tf_op jit(solution)/shard_map/ppermute | solution.py:532
  85.9 1.7 %shard_map.171 = (bf16[256,768]{1,0:T(8,128)(2,1)S(1)}, bf16[256,768]{1,0:T(8,128)(2,1)S(1)}) custom-call(bf16[256,384]{1,0:T(8,128)(2,1)S(1)} %get-tuple-element.52.refs_1_.first_ref, bf16[256,384]{1,0:T(8,128)(2,1)S(1)} %get-tuple-element.53.second_ref, bf16[16,384]{1,0:T(8,128)(2,1)S(1)} %collective-permute-done.26.refs_0_, ...), custom_call_target="tpu_custom_call" | custom-call | flops 1000 | bytes 1000 | tf_op jit(solution)/shard_map/pallas_call | solution.py:38
  87.7 2.0 %shard_map.172 = (bf16[256,768]{1,0:T(8,128)(2,1)S(1)}, bf16[256,768]{1,0:T(8,128)(2,1)S(1)}) custom-call(bf16[256,384]{1,0:T(8,128)(2,1)S(1)} %get-tuple-element.52.refs_1_.first_ref, bf16[256,384]{1,0:T(8,128)(2,1)S(1)} %get-tuple-element.53.second_ref, f32[31,384]{1,0:T(8,128)S(1)} %copy-done.2, f32[2,384]{1,0:T(2,128)S(1)} %pad_maximum_fusion.1.refs_3_.refs_1_, ...), custom_call_target="tpu_custom_call" | custom-call | flops 1000 | bytes 1000 | tf_op jit(solution)/shard_map/pallas_call | solution.py:38
  89.7 0.6 collective-permute-start.30
  90.3 0.6 collective-permute-start.29
  90.9 0.7 collective-permute-done.30
  91.7 0.9 collective-permute-start.31
  92.5 5.6 %collective-permute-done.29 = bf16[256,384]{1,0:T(8,128)(2,1)S(1)} collective-permute-done((bf16[256,384]{1,0:T(8,128)(2,1)S(1)}, bf16[256,384]{1,0:T(8,128)(2,1)S(1)}, u32[]{:S(2)}, u32[]{:S(2)}) %collective-permute-start.29) | collective-permute-done | bytes 196640 | tf_op jit(solution)/shard_map/ppermute | solution.py:26
  98.3 3.1 %collective-permute-done.31 = bf16[256,384]{1,0:T(8,128)(2,1)S(1)} collective-permute-done((bf16[256,384]{1,0:T(8,128)(2,1)S(1)}, bf16[256,384]{1,0:T(8,128)(2,1)S(1)}, u32[]{:S(2)}, u32[]{:S(2)}) %collective-permute-start.31) | collective-permute-done | bytes 196640 | tf_op jit(solution)/shard_map/ppermute | solution.py:26
  101.5 0.8 pad_maximum_fusion
  (64 shorter events, 1.9 us)
Async XLA Ops:
  0.0 17.2 %collective-permute-start = (bf16[512,384]{1,0:T(8,128)(2,1)}, bf16[512,384]{1,0:T(8,128)(2,1)S(1)}, u32[]{:S(2)}, u32[]{:S(2)}) collective-permute-start(bf16[512,384]{1,0:T(8,128)(2,1)} %refs_4_.3), channel_id=1, source_target_pairs={{0,2},{1,3},{2,0},{3,1},{4,6},{5,7},{6,4},{7,5},{8,10},{9,11},{10,... | collective-permute-start | bytes 1179656 | tf_op jit(solution)/shard_map/ppermute | solution.py:26
  2.9 15.3 %collective-permute-start.1 = (bf16[512,384]{1,0:T(8,128)(2,1)}, bf16[512,384]{1,0:T(8,128)(2,1)S(1)}, u32[]{:S(2)}, u32[]{:S(2)}) collective-permute-start(bf16[512,384]{1,0:T(8,128)(2,1)} %refs_4_.3), channel_id=1, source_target_pairs={{0,1},{1,0},{2,3},{3,2},{4,5},{5,4},{6,7},{7,6},{8,9},{9,8},{10,11... | collective-permute-start | bytes 1179656 | tf_op jit(solution)/shard_map/ppermute | solution.py:26
  2.9 21.2 %collective-permute-start.3 = (bf16[512,384]{1,0:T(8,128)(2,1)}, bf16[512,384]{1,0:T(8,128)(2,1)S(1)}, u32[]{:S(2)}, u32[]{:S(2)}) collective-permute-start(bf16[512,384]{1,0:T(8,128)(2,1)} %refs_4_.3), channel_id=1, source_target_pairs={{0,8},{4,12},{8,0},{12,4},{1,9},{5,13},{9,1},{13,5},{2,10},{6,14},... | collective-permute-start | bytes 1179656 | tf_op jit(solution)/shard_map/ppermute | solution.py:26
  5.5 19.3 %collective-permute-start.4 = (bf16[512,384]{1,0:T(8,128)(2,1)}, bf16[512,384]{1,0:T(8,128)(2,1)S(1)}, u32[]{:S(2)}, u32[]{:S(2)}) collective-permute-start(bf16[512,384]{1,0:T(8,128)(2,1)} %refs_4_.3), channel_id=1, source_target_pairs={{0,4},{4,0},{8,12},{12,8},{1,5},{5,1},{9,13},{13,9},{2,6},{6,2},{1... | collective-permute-start | bytes 1179656 | tf_op jit(solution)/shard_map/ppermute | solution.py:26
  17.2 16.2 %collective-permute-start.6 = (bf16[192,1536]{1,0:T(8,128)(2,1)S(1)}, bf16[192,1536]{1,0:T(8,128)(2,1)S(1)}, u32[]{:S(2)}, u32[]{:S(2)}) collective-permute-start(bf16[192,1536]{1,0:T(8,128)(2,1)S(1)} %shard_map.152), channel_id=1, source_target_pairs={{0,2},{1,3},{2,0},{3,1},{4,6},{5,7},{6,4},{7,5},{8,10},{9,11},{10,... | collective-permute-start | bytes 1769480 | tf_op jit(solution)/shard_map/ppermute | solution.py:26
  18.2 6.6 %collective-permute-start.2 = (bf16[512,384]{1,0:T(8,128)(2,1)S(1)}, bf16[512,384]{1,0:T(8,128)(2,1)S(1)}, u32[]{:S(2)}, u32[]{:S(2)}) collective-permute-start(bf16[512,384]{1,0:T(8,128)(2,1)S(1)} %shard_map.147.refs_1_.refs_5_), channel_id=1, source_target_pairs={{0,1},{1,0},{2,3},{3,2},{4,5},{5,4},{6,7},{7,6},{8,9},{9,8},{10,11... | collective-permute-start | bytes 1179656 | tf_op jit(solution)/shard_map/ppermute | solution.py:26
  18.2 17.4 %collective-permute-start.8 = (bf16[512,384]{1,0:T(8,128)(2,1)S(1)}, bf16[512,384]{1,0:T(8,128)(2,1)S(1)}, u32[]{:S(2)}, u32[]{:S(2)}) collective-permute-start(bf16[512,384]{1,0:T(8,128)(2,1)S(1)} %shard_map.147.refs_1_.refs_5_), channel_id=1, source_target_pairs={{0,4},{4,0},{8,12},{12,8},{1,5},{5,1},{9,13},{13,9},{2,6},{6,2},{1... | collective-permute-start | bytes 1179656 | tf_op jit(solution)/shard_map/ppermute | solution.py:26
  24.1 17.0 %collective-permute-start.5 = (bf16[512,384]{1,0:T(8,128)(2,1)S(1)}, bf16[512,384]{1,0:T(8,128)(2,1)S(1)}, u32[]{:S(2)}, u32[]{:S(2)}) collective-permute-start(bf16[512,384]{1,0:T(8,128)(2,1)S(1)} %collective-permute-done.3.refs_6_.refs_0_), channel_id=1, source_target_pairs={{0,4},{4,0},{8,12},{12,8},{1,5},{5,1},{9,13},{13,9},{2,6},{6,2},{1... | collective-permute-start | bytes 1179656 | tf_op jit(solution)/shard_map/ppermute | solution.py:26
  24.8 16.8 %collective-permute-start.9 = (bf16[512,384]{1,0:T(8,128)(2,1)S(1)}, bf16[512,384]{1,0:T(8,128)(2,1)S(1)}, u32[]{:S(2)}, u32[]{:S(2)}) collective-permute-start(bf16[512,384]{1,0:T(8,128)(2,1)S(1)} %collective-permute-done.4.refs_7_.refs_0_), channel_id=1, source_target_pairs={{0,1},{1,0},{2,3},{3,2},{4,5},{5,4},{6,7},{7,6},{8,9},{9,8},{10,11... | collective-permute-start | bytes 1179656 | tf_op jit(solution)/shard_map/ppermute | solution.py:26
  24.8 17.3 %collective-permute-start.11 = (bf16[512,384]{1,0:T(8,128)(2,1)S(1)}, bf16[512,384]{1,0:T(8,128)(2,1)S(1)}, u32[]{:S(2)}, u32[]{:S(2)}) collective-permute-start(bf16[512,384]{1,0:T(8,128)(2,1)S(1)} %collective-permute-done.3.refs_6_.refs_0_), channel_id=1, source_target_pairs={{0,2},{1,3},{2,0},{3,1},{4,6},{5,7},{6,4},{7,5},{8,10},{9,11},{10,... | collective-permute-start | bytes 1179656 | tf_op jit(solution)/shard_map/ppermute | solution.py:26
  26.7 2.5 %copy-start.1 = (bf16[512,384]{1,0:T(8,128)(2,1)S(1)}, bf16[512,384]{1,0:T(8,128)(2,1)}, u32[]{:S(2)}) copy-start(bf16[512,384]{1,0:T(8,128)(2,1)} %refs_4_.3) | copy-start | bytes 1179652
  35.6 6.0 %copy-start = (bf16[384,1536]{1,0:T(8,128)(2,1)S(1)}, bf16[384,1536]{1,0:T(8,128)(2,1)}, u32[]{:S(2)}) copy-start(bf16[384,1536]{1,0:T(8,128)(2,1)} %refs_8_.3) | copy-start | bytes 3538948
  35.6 8.1 %collective-permute-start.10 = (bf16[512,384]{1,0:T(8,128)(2,1)S(1)}, bf16[512,384]{1,0:T(8,128)(2,1)S(1)}, u32[]{:S(2)}, u32[]{:S(2)}) collective-permute-start(bf16[512,384]{1,0:T(8,128)(2,1)S(1)} %shard_map.155.refs_1_), channel_id=1, source_target_pairs={{0,1},{1,0},{2,3},{3,2},{4,5},{5,4},{6,7},{7,6},{8,9},{9,8},{10,11... | collective-permute-start | bytes 1179656 | tf_op jit(solution)/shard_map/ppermute | solution.py:26
  41.2 11.0 %collective-permute-start.7 = (bf16[512,384]{1,0:T(8,128)(2,1)S(1)}, bf16[512,384]{1,0:T(8,128)(2,1)S(1)}, u32[]{:S(2)}, u32[]{:S(2)}) collective-permute-start(bf16[512,384]{1,0:T(8,128)(2,1)S(1)} %shard_map.154.refs_1_.refs_0_), channel_id=1, source_target_pairs={{0,2},{1,3},{2,0},{3,1},{4,6},{5,7},{6,4},{7,5},{8,10},{9,11},{10,... | collective-permute-start | bytes 1179656 | tf_op jit(solution)/shard_map/ppermute | solution.py:26
  41.6 10.5 %collective-permute-start.14 = (bf16[512,384]{1,0:T(8,128)(2,1)S(1)}, bf16[512,384]{1,0:T(8,128)(2,1)S(1)}, u32[]{:S(2)}, u32[]{:S(2)}) collective-permute-start(bf16[512,384]{1,0:T(8,128)(2,1)S(1)} %collective-permute-done.3.refs_6_.refs_0_), channel_id=1, source_target_pairs={{0,1},{1,0},{2,3},{3,2},{4,5},{5,4},{6,7},{7,6},{8,9},{9,8},{10,11... | collective-permute-start | bytes 1179656 | tf_op jit(solution)/shard_map/ppermute | solution.py:26
  41.6 28.2 %collective-permute-start.20 = (bf16[384,1536]{1,0:T(8,128)(2,1)S(1)}, bf16[384,1536]{1,0:T(8,128)(2,1)S(1)}, u32[]{:S(2)}, u32[]{:S(2)}) collective-permute-start(bf16[384,1536]{1,0:T(8,128)(2,1)S(1)} %copy-done), channel_id=1, source_target_pairs={{0,1},{1,0},{2,3},{3,2},{4,5},{5,4},{6,7},{7,6},{8,9},{9,8},{10,11... | collective-permute-start | bytes 3538952 | tf_op jit(solution)/shard_map/ppermute | solution.py:26
  42.2 20.3 %collective-permute-start.19 = (bf16[192,1536]{1,0:T(8,128)(2,1)S(1)}, bf16[192,1536]{1,0:T(8,128)(2,1)S(1)}, u32[]{:S(2)}, u32[]{:S(2)}) collective-permute-start(bf16[192,1536]{1,0:T(8,128)(2,1)S(1)} %shard_map.166.refs_9_), channel_id=1, source_target_pairs={{0,16},{16,0},{1,17},{17,1},{2,18},{18,2},{3,19},{19,3},{4,20},{20... | collective-permute-start | bytes 1769480 | tf_op jit(solution)/shard_map/ppermute | solution.py:26
  43.7 8.9 %collective-permute-start.15 = (bf16[512,384]{1,0:T(8,128)(2,1)S(1)}, bf16[512,384]{1,0:T(8,128)(2,1)S(1)}, u32[]{:S(2)}, u32[]{:S(2)}) collective-permute-start(bf16[512,384]{1,0:T(8,128)(2,1)S(1)} %shard_map.157.refs_2_.refs_1_), channel_id=1, source_target_pairs={{0,1},{1,0},{2,3},{3,2},{4,5},{5,4},{6,7},{7,6},{8,9},{9,8},{10,11... | collective-permute-start | bytes 1179656 | tf_op jit(solution)/shard_map/ppermute | solution.py:26
  52.2 6.4 %collective-permute-start.12 = (bf16[512,384]{1,0:T(8,128)(2,1)S(1)}, bf16[512,384]{1,0:T(8,128)(2,1)S(1)}, u32[]{:S(2)}, u32[]{:S(2)}) collective-permute-start(bf16[512,384]{1,0:T(8,128)(2,1)S(1)} %shard_map.154.refs_1_.refs_0_), channel_id=1, source_target_pairs={{0,1},{1,0},{2,3},{3,2},{4,5},{5,4},{6,7},{7,6},{8,9},{9,8},{10,11... | collective-permute-start | bytes 1179656 | tf_op jit(solution)/shard_map/ppermute | solution.py:26
  52.2 6.3 %collective-permute-start.13 = (bf16[512,384]{1,0:T(8,128)(2,1)S(1)}, bf16[512,384]{1,0:T(8,128)(2,1)S(1)}, u32[]{:S(2)}, u32[]{:S(2)}) collective-permute-start(bf16[512,384]{1,0:T(8,128)(2,1)S(1)} %shard_map.159.refs_1_), channel_id=1, source_target_pairs={{0,1},{1,0},{2,3},{3,2},{4,5},{5,4},{6,7},{7,6},{8,9},{9,8},{10,11... | collective-permute-start | bytes 1179656 | tf_op jit(solution)/shard_map/ppermute | solution.py:26
  52.7 17.8 %collective-permute-start.21 = (bf16[192,1536]{1,0:T(8,128)(2,1)S(1)}, bf16[192,1536]{1,0:T(8,128)(2,1)S(1)}, u32[]{:S(2)}, u32[]{:S(2)}) collective-permute-start(bf16[192,1536]{1,0:T(8,128)(2,1)S(1)} %shard_map.166.refs_9_), channel_id=1, source_target_pairs={{0,1},{1,0},{2,3},{3,2},{4,5},{5,4},{6,7},{7,6},{8,9},{9,8},{10,11... | collective-permute-start | bytes 1769480 | tf_op jit(solution)/shard_map/ppermute | solution.py:26
  62.5 8.8 %collective-permute-start.22 = (bf16[192,1536]{1,0:T(8,128)(2,1)S(1)}, bf16[192,1536]{1,0:T(8,128)(2,1)S(1)}, u32[]{:S(2)}, u32[]{:S(2)}) collective-permute-start(bf16[192,1536]{1,0:T(8,128)(2,1)S(1)} %shard_map.167.refs_10_), channel_id=1, source_target_pairs={{0,1},{1,0},{2,3},{3,2},{4,5},{5,4},{6,7},{7,6},{8,9},{9,8},{10,11... | collective-permute-start | bytes 1769480 | tf_op jit(solution)/shard_map/ppermute | solution.py:26
  63.0 6.9 %collective-permute-start.16 = (bf16[256,384]{1,0:T(8,128)(2,1)S(1)}, bf16[256,384]{1,0:T(8,128)(2,1)S(1)}, u32[]{:S(2)}, u32[]{:S(2)}) collective-permute-start(bf16[256,384]{1,0:T(8,128)(2,1)S(1)} %shard_map.163.refs_1_.refs_0_), channel_id=1, source_target_pairs={{0,2},{1,3},{2,0},{3,1},{4,6},{5,7},{6,4},{7,5},{8,10},{9,11},{10,... | collective-permute-start | bytes 589832 | tf_op jit(solution)/shard_map/ppermute | solution.py:26
  65.6 5.0 %collective-permute-start.17 = (bf16[256,384]{1,0:T(8,128)(2,1)S(1)}, bf16[256,384]{1,0:T(8,128)(2,1)S(1)}, u32[]{:S(2)}, u32[]{:S(2)}) collective-permute-start(bf16[256,384]{1,0:T(8,128)(2,1)S(1)} %shard_map.163.refs_1_.refs_0_), channel_id=1, source_target_pairs={{0,1},{1,0},{2,3},{3,2},{4,5},{5,4},{6,7},{7,6},{8,9},{9,8},{10,11... | collective-permute-start | bytes 589832 | tf_op jit(solution)/shard_map/ppermute | solution.py:26
  69.9 1.4 %collective-permute-start.18 = (bf16[256,384]{1,0:T(8,128)(2,1)S(1)}, bf16[256,384]{1,0:T(8,128)(2,1)S(1)}, u32[]{:S(2)}, u32[]{:S(2)}) collective-permute-start(bf16[256,384]{1,0:T(8,128)(2,1)S(1)} %shard_map.165.refs_1_), channel_id=1, source_target_pairs={{0,1},{1,0},{2,3},{3,2},{4,5},{5,4},{6,7},{7,6},{8,9},{9,8},{10,11... | collective-permute-start | bytes 589832 | tf_op jit(solution)/shard_map/ppermute | solution.py:26
  69.9 7.3 %collective-permute-start.23 = (bf16[256,384]{1,0:T(8,128)(2,1)S(1)}, bf16[256,384]{1,0:T(8,128)(2,1)S(1)}, u32[]{:S(2)}, u32[]{:S(2)}) collective-permute-start(bf16[256,384]{1,0:T(8,128)(2,1)S(1)} %shard_map.164.refs_1_.refs_0_), channel_id=1, source_target_pairs={{0,2},{1,3},{2,0},{3,1},{4,6},{5,7},{6,4},{7,5},{8,10},{9,11},{10,... | collective-permute-start | bytes 589832 | tf_op jit(solution)/shard_map/ppermute | solution.py:26
  70.5 11.2 %collective-permute-start.24 = (bf16[256,384]{1,0:T(8,128)(2,1)S(1)}, bf16[256,384]{1,0:T(8,128)(2,1)S(1)}, u32[]{:S(2)}, u32[]{:S(2)}) collective-permute-start(bf16[256,384]{1,0:T(8,128)(2,1)S(1)} %shard_map.164.refs_1_.refs_0_), channel_id=1, source_target_pairs={{0,1},{1,0},{2,3},{3,2},{4,5},{5,4},{6,7},{7,6},{8,9},{9,8},{10,11... | collective-permute-start | bytes 589832 | tf_op jit(solution)/shard_map/ppermute | solution.py:26
  71.3 5.9 %copy-start.3 = (f32[384]{0:T(512)S(1)}, f32[384]{0:T(512)}, u32[]{:S(2)}) copy-start(f32[384]{0:T(512)} %param.28) | copy-start | bytes 4612
  71.3 5.9 %copy-start.4 = (f32[384]{0:T(512)S(1)}, f32[384]{0:T(512)}, u32[]{:S(2)}) copy-start(f32[384]{0:T(512)} %param.27) | copy-start | bytes 4612
  77.2 4.5 %collective-permute-start.25 = (bf16[256,384]{1,0:T(8,128)(2,1)S(1)}, bf16[256,384]{1,0:T(8,128)(2,1)S(1)}, u32[]{:S(2)}, u32[]{:S(2)}) collective-permute-start(bf16[256,384]{1,0:T(8,128)(2,1)S(1)} %shard_map.169.refs_1_), channel_id=1, source_target_pairs={{0,1},{1,0},{2,3},{3,2},{4,5},{5,4},{6,7},{7,6},{8,9},{9,8},{10,11... | collective-permute-start | bytes 589832 | tf_op jit(solution)/shard_map/ppermute | solution.py:26
  77.2 7.6 %collective-permute-start.26 = (bf16[16,384]{1,0:T(8,128)(2,1)S(1)}, bf16[16,384]{1,0:T(8,128)(2,1)S(1)}, u32[]{:S(2)}, u32[]{:S(2)}) collective-permute-start(bf16[16,384]{1,0:T(8,128)(2,1)S(1)} %get-tuple-element.54), channel_id=1, source_target_pairs={{0,4},{4,8},{8,12},{1,5},{5,9},{9,13},{2,6},{6,10},{10,14},{3,7},{... | collective-permute-start | bytes 36872 | tf_op jit(solution)/shard_map/ppermute | solution.py:531
  80.3 5.6 %collective-permute-start.27 = (bf16[16,384]{1,0:T(8,128)(2,1)S(1)}, bf16[16,384]{1,0:T(8,128)(2,1)S(1)}, u32[]{:S(2)}, u32[]{:S(2)}) collective-permute-start(bf16[16,384]{1,0:T(8,128)(2,1)S(1)} %get-tuple-element.55), channel_id=1, source_target_pairs={{4,0},{8,4},{12,8},{5,1},{9,5},{13,9},{6,2},{10,6},{14,10},{7,3},{... | collective-permute-start | bytes 36872 | tf_op jit(solution)/shard_map/ppermute | solution.py:532
  81.7 4.3 %copy-start.2 = (f32[31,384]{1,0:T(8,128)S(1)}, f32[31,384]{1,0:T(8,128)}, u32[]{:S(2)}) copy-start(f32[31,384]{1,0:T(8,128)} %refs_0_.9) | copy-start | bytes 142852
  87.6 2.7 %collective-permute-start.28 = (bf16[256,768]{1,0:T(8,128)(2,1)S(1)}, bf16[256,768]{1,0:T(8,128)(2,1)S(1)}, u32[]{:S(2)}, u32[]{:S(2)}) collective-permute-start(bf16[256,768]{1,0:T(8,128)(2,1)S(1)} %get-tuple-element.57), channel_id=1, source_target_pairs={{0,1},{1,0},{2,3},{3,2},{4,5},{5,4},{6,7},{7,6},{8,9},{9,8},{10,11... | collective-permute-start | bytes 1179656 | tf_op jit(solution)/shard_map/ppermute | solution.py:26
  89.7 1.9 %collective-permute-start.30 = (bf16[256,768]{1,0:T(8,128)(2,1)S(1)}, bf16[256,768]{1,0:T(8,128)(2,1)S(1)}, u32[]{:S(2)}, u32[]{:S(2)}) collective-permute-start(bf16[256,768]{1,0:T(8,128)(2,1)S(1)} %get-tuple-element.60), channel_id=1, source_target_pairs={{0,1},{1,0},{2,3},{3,2},{4,5},{5,4},{6,7},{7,6},{8,9},{9,8},{10,11... | collective-permute-start | bytes 1179656 | tf_op jit(solution)/shard_map/ppermute | solution.py:26
  90.3 7.8 %collective-permute-start.29 = (bf16[256,384]{1,0:T(8,128)(2,1)S(1)}, bf16[256,384]{1,0:T(8,128)(2,1)S(1)}, u32[]{:S(2)}, u32[]{:S(2)}) collective-permute-start(bf16[256,384]{1,0:T(8,128)(2,1)S(1)} %add_convert_fusion.3), channel_id=1, source_target_pairs={{0,2},{1,3},{2,0},{3,1},{4,6},{5,7},{6,4},{7,5},{8,10},{9,11},{10,... | collective-permute-start | bytes 589832 | tf_op jit(solution)/shard_map/ppermute | solution.py:26
  91.7 9.8 %collective-permute-start.31 = (bf16[256,384]{1,0:T(8,128)(2,1)S(1)}, bf16[256,384]{1,0:T(8,128)(2,1)S(1)}, u32[]{:S(2)}, u32[]{:S(2)}) collective-permute-start(bf16[256,384]{1,0:T(8,128)(2,1)S(1)} %add_convert_fusion.1), channel_id=1, source_target_pairs={{0,2},{1,3},{2,0},{3,1},{4,6},{5,7},{6,4},{7,5},{8,10},{9,11},{10,... | collective-permute-start | bytes 589832 | tf_op jit(solution)/shard_map/ppermute | solution.py:26
